TPU v7x, 128 devices: a whole 4x4x4 slice. The times are simulated.
128 devices in a mesh: band: 32 (over x, z, core), sub: 4 (over y).
Axes of the slice: x: 4, y: 4, z: 4, core: 2. Of those that a mesh axis runs over, the one named last changes fastest.
Arguments:
- grid_input: bfloat16 [262144, 227], P(('band', 'sub')), may hold values from -6 to 6
- grid_send: int32 [384, 4, 128], P(('band', 'sub')), may hold values from 0 to 2047, as said below
- grid_edge_src: int32 [1048576], P(('band', 'sub')), may hold values from 0 to 1535, as said below
- grid_edge_dst: int32 [1048576], P(('band', 'sub')), may hold values from 0 to 319
- edge_count: int32 [128], P(('band', 'sub')), may hold values from 1536 to 8192, as said below
- grid_edge_geo: bfloat16 [4, 1048576], P(None, ('band', 'sub')), may hold values from -6 to 6
- mesh_embed: bfloat16 [40960, 512], P(('band', 'sub')), may hold values from -6 to 6
- mesh_near_send: int32 [384, 4, 64], P(('band', 'sub')), may hold values from 0 to 319, as said below
- mesh_far_send: int32 [16384, 2], P(('band', 'sub')), may hold values from 0 to 319, as said below
- mesh_edge_src: int32 [327680], P(('band', 'sub')), may hold values from 0 to 1343, as said below
- mesh_edge_dst: int32 [327680], P(('band', 'sub')), may hold values from 0 to 319
- mesh_edge_lat: bfloat16 [327680, 512], P(('band', 'sub')), may hold values from -6 to 6
- enc_in: bfloat16 [227, 512], replicated, may hold values from -0.375 to 0.375
- enc_out: bfloat16 [512, 512], replicated, may hold values from -0.25 to 0.25
- send_proj: bfloat16 [512, 512], replicated, may hold values from -0.25 to 0.25
- recv_proj: bfloat16 [512, 512], replicated, may hold values from -0.25 to 0.25
- geo_proj: bfloat16 [4, 512], replicated, may hold values from -3 to 3
- msg_weight: bfloat16 [512, 512], replicated, may hold values from -0.25 to 0.25
- node_self: bfloat16 [512, 512], replicated, may hold values from -0.25 to 0.25
- node_agg: bfloat16 [512, 512], replicated, may hold values from -0.25 to 0.25
- node_out: bfloat16 [512, 512], replicated, may hold values from -0.25 to 0.25
- mesh_gain: float32 [512], replicated, may hold values from 0.1 to 1.9
- proc_send: bfloat16 [512, 512], replicated, may hold values from -0.25 to 0.25
- proc_recv: bfloat16 [512, 512], replicated, may hold values from -0.25 to 0.25
- edge_self: bfloat16 [512, 512], replicated, may hold values from -0.25 to 0.25
- edge_out: bfloat16 [512, 512], replicated, may hold values from -0.25 to 0.25
- upd_self: bfloat16 [512, 512], replicated, may hold values from -0.25 to 0.25
- upd_agg: bfloat16 [512, 512], replicated, may hold values from -0.25 to 0.25
- upd_out: bfloat16 [512, 512], replicated, may hold values from -0.25 to 0.25
- out_gain: float32 [512], replicated, may hold values from 0.1 to 1.9
Outputs:
- mesh_out: bfloat16 [40960, 512], P(('band', 'sub'))
Inputs may be any that keep to these rules, and one draw needn't show every extreme that they name: `grid_send`: local grid rows of the sending device. `grid_edge_src`: on each device the first edges use every received position whose source band exists exactly once, in order of position; later edges use such positions at random; positions from a band outside the grid are never used. `edge_count`: devices of the first and last band have 8192 live edges; every other device has at least 3 * 128 times the number of sub devices. `mesh_near_send`: local mesh rows of the sending device. `mesh_far_send`: local mesh rows of the sending device. `mesh_edge_src`: positions below 320 are the device's own rows; every received row from an existing band and every far row is used by exactly one edge of its device; rows from a band outside the grid are never used.
All inputs are finite; a program needn't handle non-finite values.
Results may differ from a plain program's by a relative error of at most 0.015.
Values may be sent and summed in bfloat16 or wider, within the bound.
No kernel may reach another device: no remote copies, remote signals or barrier semaphores. Data moves between devices by JAX's collectives and lax.ppermute only.
A program may use at most 64 MiB of HBM per device.

v0:
```python
import math

import jax
import jax.numpy as jnp
from jax import lax
from jax.sharding import PartitionSpec as P


def shifted_2(value, axis, steps):
    count = lax.axis_size(axis)
    first, last = (max(0, -steps), min(count, count - steps))
    return lax.ppermute(value, axis, [(source, source + steps) for source in range(first, last)])


def layer_norm(values):
    row_mean = jnp.mean(values, axis=-1, keepdims=True)
    centred = values - row_mean
    variance = jnp.mean(centred * centred, axis=-1, keepdims=True)
    return centred * lax.rsqrt(variance + 1e-05)


def project(inputs, weight):
    return jnp.dot(inputs, weight, preferred_element_type=jnp.float32).astype(jnp.bfloat16)


def encode_rows(inputs, enc_in, enc_out):
    hidden = jax.nn.silu(jnp.dot(inputs, enc_in, preferred_element_type=jnp.float32)).astype(
        jnp.bfloat16
    )
    return layer_norm(jnp.dot(hidden, enc_out, preferred_element_type=jnp.float32)).astype(
        jnp.bfloat16
    )


def scatter_rows(onehot, values):
    return lax.dot_general(
        onehot, values, (((0,), (0,)), ((), ())), preferred_element_type=jnp.float32
    )


def body(
    grid_input,
    grid_send,
    grid_edge_src,
    grid_edge_dst,
    edge_count,
    grid_edge_geo,
    mesh_embed,
    mesh_near_send,
    mesh_far_send,
    mesh_edge_src,
    mesh_edge_dst,
    mesh_edge_lat,
    enc_in,
    enc_out,
    send_proj,
    recv_proj,
    geo_proj,
    msg_weight,
    node_self,
    node_agg,
    node_out,
    mesh_gain,
    proc_send,
    proc_recv,
    edge_self,
    edge_out,
    upd_self,
    upd_agg,
    upd_out,
    out_gain,
):
    band_count = lax.axis_size("band")
    sub_count = lax.axis_size("sub")
    devices = band_count * sub_count
    slot_cap = grid_send.shape[2]
    near_cap = mesh_near_send.shape[2]
    far_cap = mesh_far_send.shape[1]
    mesh_rows = mesh_embed.shape[0]
    latent_width = mesh_embed.shape[1]
    flat_send = grid_send.reshape(-1)
    sender = project(encode_rows(grid_input, enc_in, enc_out), send_proj)
    payload = jnp.take(sender, flat_send, axis=0)
    row_width = payload.shape[1]
    stacked = payload.reshape(3, sub_count, slot_cap, row_width)
    in_sub = lax.all_to_all(stacked, "sub", split_axis=1, concat_axis=1, tiled=True)
    shifted = [shifted_2(in_sub[offset], "band", offset - 1) for offset in (0, 2)]
    arrived = jnp.stack([shifted[0], in_sub[1], shifted[1]])
    lookup = arrived.reshape(3 * sub_count * slot_cap, row_width)
    receiver = project(mesh_embed, recv_proj)
    live_total = edge_count[0]
    mesh_ids = jnp.arange(mesh_rows, dtype=jnp.int32)
    edge_total = grid_edge_src.shape[0]
    block_rows = math.gcd(edge_total, 2048)

    def grid_block(block, inflow):
        first_row = block * block_rows
        sources = lax.dynamic_slice_in_dim(grid_edge_src, first_row, block_rows)
        targets = lax.dynamic_slice_in_dim(grid_edge_dst, first_row, block_rows)
        geometry = lax.dynamic_slice_in_dim(grid_edge_geo, first_row, block_rows, 1)
        onehot = (targets[:, None] == mesh_ids[None, :]).astype(jnp.bfloat16)
        geo_term = lax.dot_general(
            geometry, geo_proj, (((0,), (0,)), ((), ())), preferred_element_type=jnp.float32
        )
        pre_act = (
            jnp.take(lookup, sources, axis=0).astype(jnp.float32)
            + jnp.dot(onehot, receiver, preferred_element_type=jnp.float32)
            + geo_term
        )
        edge_act = jax.nn.silu(pre_act).astype(jnp.bfloat16)
        live_mask = first_row + jnp.arange(block_rows, dtype=jnp.int32) < live_total
        message = jnp.where(
            live_mask[:, None],
            jnp.dot(edge_act, msg_weight, preferred_element_type=jnp.float32),
            0.0,
        ).astype(jnp.bfloat16)
        return inflow + scatter_rows(onehot, message)

    inflow = lax.fori_loop(
        0, edge_total // block_rows, grid_block, jnp.zeros((mesh_rows, latent_width), jnp.float32)
    ).astype(jnp.bfloat16)
    node_act = jax.nn.silu(
        jnp.dot(mesh_embed, node_self, preferred_element_type=jnp.float32)
        + jnp.dot(inflow, node_agg, preferred_element_type=jnp.float32)
    ).astype(jnp.bfloat16)
    mesh_latent = (
        mesh_embed.astype(jnp.float32)
        + layer_norm(jnp.dot(node_act, node_out, preferred_element_type=jnp.float32)) * mesh_gain
    ).astype(jnp.bfloat16)
    mesh_sender = project(mesh_latent, proc_send)
    target_rows = project(mesh_latent, proc_recv)
    near_out = jnp.take(mesh_sender, mesh_near_send.reshape(-1), axis=0).reshape(
        3, sub_count, near_cap, latent_width
    )
    near_sub = lax.all_to_all(near_out, "sub", split_axis=1, concat_axis=1, tiled=True)
    near_moved = [shifted_2(near_sub[offset], "band", offset - 1) for offset in (0, 2)]
    near_rows = jnp.stack([near_moved[0], near_sub[1], near_moved[1]]).reshape(
        3 * sub_count * near_cap, latent_width
    )
    outgoing = jnp.take(mesh_sender, mesh_far_send.reshape(-1), axis=0).reshape(
        devices, far_cap, latent_width
    )
    received = lax.all_to_all(outgoing, ("band", "sub"), split_axis=0, concat_axis=0, tiled=True)
    mesh_lookup = jnp.concatenate(
        [mesh_sender, near_rows, received.reshape(devices * far_cap, latent_width)], axis=0
    )
    mesh_edges = mesh_edge_src.shape[0]
    mesh_block = math.gcd(mesh_edges, 1280)

    def mesh_step(block, inflow_sum):
        first_row = block * mesh_block
        sources = lax.dynamic_slice_in_dim(mesh_edge_src, first_row, mesh_block)
        targets = lax.dynamic_slice_in_dim(mesh_edge_dst, first_row, mesh_block)
        lats = lax.dynamic_slice_in_dim(mesh_edge_lat, first_row, mesh_block)
        onehot = (targets[:, None] == mesh_ids[None, :]).astype(jnp.bfloat16)
        edge_pre = (
            jnp.dot(lats, edge_self, preferred_element_type=jnp.float32)
            + jnp.take(mesh_lookup, sources, axis=0).astype(jnp.float32)
            + jnp.dot(onehot, target_rows, preferred_element_type=jnp.float32)
        )
        edge_hidden = jax.nn.silu(edge_pre).astype(jnp.bfloat16)
        edge_new = (
            lats.astype(jnp.float32)
            + layer_norm(jnp.dot(edge_hidden, edge_out, preferred_element_type=jnp.float32))
        ).astype(jnp.bfloat16)
        return inflow_sum + scatter_rows(onehot, edge_new)

    edge_inflow = lax.fori_loop(
        0, mesh_edges // mesh_block, mesh_step, jnp.zeros((mesh_rows, latent_width), jnp.float32)
    ).astype(jnp.bfloat16)
    upd_act = jax.nn.silu(
        jnp.dot(mesh_latent, upd_self, preferred_element_type=jnp.float32)
        + jnp.dot(edge_inflow, upd_agg, preferred_element_type=jnp.float32)
    ).astype(jnp.bfloat16)
    return (
        mesh_latent.astype(jnp.float32)
        + layer_norm(jnp.dot(upd_act, upd_out, preferred_element_type=jnp.float32)) * out_gain
    ).astype(jnp.bfloat16)


def solution(mesh):
    return jax.shard_map(
        body,
        mesh=mesh,
        in_specs=(
            P(("band", "sub"), None),
            P(("band", "sub"), None, None),
            P(("band", "sub")),
            P(("band", "sub")),
            P(("band", "sub")),
            P(None, ("band", "sub")),
            P(("band", "sub"), None),
            P(("band", "sub"), None, None),
            P(("band", "sub"), None),
            P(("band", "sub")),
            P(("band", "sub")),
            P(("band", "sub"), None),
            P(),
            P(),
            P(),
            P(),
            P(),
            P(),
            P(),
            P(),
            P(),
            P(),
            P(),
            P(),
            P(),
            P(),
            P(),
            P(),
            P(),
            P(),
        ),
        out_specs=P(("band", "sub"), None),
        check_vma=False,
    )
```

profile of v0, /device:TPU:6, one launch (start us, length us, event | category | flops | bytes accessed | tf_op | source)
XLA Modules:
  0.0 258.9 jit_solution(15139254715538262564)
XLA Ops:
  1.2 5.4 %fusion.45 = (f32[2048]{0:T(1024)S(1)}, f32[2048,512]{0,1:T(8,128)}) fusion(bf16[512,512]{1,0:T(8,128)(2,1)} %param.47, bf16[2048,227]{0,1:T(8,128)(2,1)S(1)} %copy-done, bf16[227,512]{1,0:T(8,128)(2,1)} %param.46), kind=kOutput, calls=%fused_computation.105 | convolution fusion | flops 1556084736 | bytes 5889024 | tf_op jit(solution)/shard_map/dot_general | solution.py:30
  12.4 5.4 %gather_fusion.2 = bf16[1536,512]{1,0:T(8,128)(2,1)} fusion(bf16[2048,512]{1,0:T(8,128)(2,1)S(1)} %convolution_convert_fusion, s32[2048]{0:T(1024)S(1)} %pad_clamp_fusion.1), kind=kCustom, calls=%fused_computation.2 | custom fusion | bytes 3151872 | tf_op jit(solution)/shard_map/jit(_take)/gather | solution.py:83
  20.7 4.6 %all-to-all-start = ((bf16[3,4,128,512]{3,2,0,1:T(8,128)(2,1)}), bf16[3,4,128,512]{3,2,0,1:T(8,128)(2,1)S(1)}, u32[]{:S(2)}, u32[]{:S(2)}) async-start(bf16[3,4,128,512]{3,2,0,1:T(8,128)(2,1)} %copy_select_fusion), calls=%async_computation | async-start | bytes 3145728 | tf_op jit(solution)/shard_map/all_to_all | solution.py:86
  26.3 19.8 %all-to-all-done = bf16[3,4,128,512]{3,2,0,1:T(8,128)(2,1)S(1)} async-done(((bf16[3,4,128,512]{3,2,0,1:T(8,128)(2,1)}), bf16[3,4,128,512]{3,2,0,1:T(8,128)(2,1)S(1)}, u32[]{:S(2)}, u32[]{:S(2)}) %all-to-all-start) | async-done | bytes 1572896 | tf_op jit(solution)/shard_map/all_to_all | solution.py:86
  47.2 4.5 %collective-permute-start = (bf16[4,128,512]{2,1,0:T(8,128)(2,1)}, bf16[4,128,512]{2,1,0:T(8,128)(2,1)S(1)}, u32[]{:S(2)}, u32[]{:S(2)}) collective-permute-start(bf16[4,128,512]{2,1,0:T(8,128)(2,1)} %get-tuple-element.498), channel_id=1, source_target_pairs={{4,0},{8,4},{12,8},{16,12},{20,16},{24,20},{28,24},{32,28},{36,32}... | collective-permute-start | bytes 1572872 | tf_op jit(solution)/shard_map/ppermute | solution.py:12
  59.2 5.4 %collective-permute-done.1 = bf16[4,128,512]{2,1,0:T(8,128)(2,1)S(1)} collective-permute-done((bf16[4,128,512]{2,1,0:T(8,128)(2,1)}, bf16[4,128,512]{2,1,0:T(8,128)(2,1)S(1)}, u32[]{:S(2)}, u32[]{:S(2)}) %collective-permute-start.1) | collective-permute-done | bytes 524320 | tf_op jit(solution)/shard_map/ppermute | solution.py:12
  66.7 97.6 %while.28 = (s32[]{:T(128)}, f32[320,512]{1,0:T(8,128)}, s32[8192]{0:T(1024)}, s32[]{:T(128)}, s32[8192]{0:T(1024)S(1)}, /*index=5*/bf16[1536,512]{1,0:T(8,128)(...) while((s32[]{:T(128)}, f32[320,512]{1,0:T(8,128)}, ...), condition=%wide.region_3.4_spmd.clone, body=%wide.region_2.3_spmd.clone.sunk | while | flops 2437505024 | bytes 21131476 | solution.py:119
  71.5 9.1 %gather_fusion = bf16[2048,512]{1,0:T(8,128)(2,1)} fusion(bf16[1536,512]{1,0:T(8,128)(2,1)S(1)} %get-tuple-element.671, s32[2048]{0:T(1024)S(1)} %fusion.101), kind=kCustom, calls=%fused_computation.clone.clone.1 | custom fusion | bytes 4202496 | tf_op jit(solution)/shard_map/while/body/eval_jaxpr/jit(_take)/gather | solution.py:106
  80.7 6.5 %select_convert_fusion.2 = bf16[2048,512]{1,0:T(8,128)(2,1)} fusion(bf16[512,512]{1,0:T(8,128)(2,1)} %get-tuple-element.675, pred[2048]{0:T(1024)(128)(4,1)} %get-tuple-element.623, f32[2048,512]{1,0:T(8,128)} %fusion.100, bf16[4,512]{1,0:T(4,128)(2,1)} %get-tuple-element.674, bf16[2048,512]{1,0:T(8,128)(2,1)} %gather_fusion, ...), kind=kOutput, calls=%fused_computation.7.clone.1 | convolution fusion | flops 1093664768 | bytes 8937476 | tf_op jit(solution)/shard_map/while/body/eval_jaxpr/dot_general | solution.py:114
  95.8 9.1 %gather_fusion = bf16[2048,512]{1,0:T(8,128)(2,1)} fusion(bf16[1536,512]{1,0:T(8,128)(2,1)S(1)} %get-tuple-element.671, s32[2048]{0:T(1024)S(1)} %fusion.101), kind=kCustom, calls=%fused_computation.clone.clone.1 | custom fusion | bytes 4202496 | tf_op jit(solution)/shard_map/while/body/eval_jaxpr/jit(_take)/gather | solution.py:106
  105.0 6.5 %select_convert_fusion.2 = bf16[2048,512]{1,0:T(8,128)(2,1)} fusion(bf16[512,512]{1,0:T(8,128)(2,1)} %get-tuple-element.675, pred[2048]{0:T(1024)(128)(4,1)} %get-tuple-element.623, f32[2048,512]{1,0:T(8,128)} %fusion.100, bf16[4,512]{1,0:T(4,128)(2,1)} %get-tuple-element.674, bf16[2048,512]{1,0:T(8,128)(2,1)} %gather_fusion, ...), kind=kOutput, calls=%fused_computation.7.clone.1 | convolution fusion | flops 1093664768 | bytes 8937476 | tf_op jit(solution)/shard_map/while/body/eval_jaxpr/dot_general | solution.py:114
  120.2 9.1 %gather_fusion = bf16[2048,512]{1,0:T(8,128)(2,1)} fusion(bf16[1536,512]{1,0:T(8,128)(2,1)S(1)} %get-tuple-element.671, s32[2048]{0:T(1024)S(1)} %fusion.101), kind=kCustom, calls=%fused_computation.clone.clone.1 | custom fusion | bytes 4202496 | tf_op jit(solution)/shard_map/while/body/eval_jaxpr/jit(_take)/gather | solution.py:106
  129.4 6.5 %select_convert_fusion.2 = bf16[2048,512]{1,0:T(8,128)(2,1)} fusion(bf16[512,512]{1,0:T(8,128)(2,1)} %get-tuple-element.675, pred[2048]{0:T(1024)(128)(4,1)} %get-tuple-element.623, f32[2048,512]{1,0:T(8,128)} %fusion.100, bf16[4,512]{1,0:T(4,128)(2,1)} %get-tuple-element.674, bf16[2048,512]{1,0:T(8,128)(2,1)} %gather_fusion, ...), kind=kOutput, calls=%fused_computation.7.clone.1 | convolution fusion | flops 1093664768 | bytes 8937476 | tf_op jit(solution)/shard_map/while/body/eval_jaxpr/dot_general | solution.py:114
  144.6 9.1 %gather_fusion = bf16[2048,512]{1,0:T(8,128)(2,1)} fusion(bf16[1536,512]{1,0:T(8,128)(2,1)S(1)} %get-tuple-element.671, s32[2048]{0:T(1024)S(1)} %fusion.101), kind=kCustom, calls=%fused_computation.clone.clone.1 | custom fusion | bytes 4202496 | tf_op jit(solution)/shard_map/while/body/eval_jaxpr/jit(_take)/gather | solution.py:106
  153.8 6.5 %select_convert_fusion.2 = bf16[2048,512]{1,0:T(8,128)(2,1)} fusion(bf16[512,512]{1,0:T(8,128)(2,1)} %get-tuple-element.675, pred[2048]{0:T(1024)(128)(4,1)} %get-tuple-element.623, f32[2048,512]{1,0:T(8,128)} %fusion.100, bf16[4,512]{1,0:T(4,128)(2,1)} %get-tuple-element.674, bf16[2048,512]{1,0:T(8,128)(2,1)} %gather_fusion, ...), kind=kOutput, calls=%fused_computation.7.clone.1 | convolution fusion | flops 1093664768 | bytes 8937476 | tf_op jit(solution)/shard_map/while/body/eval_jaxpr/dot_general | solution.py:114
  179.4 6.1 %all-to-all-done.1 = bf16[3,4,64,512]{3,2,0,1:T(8,128)(2,1)S(1)} async-done(((bf16[3,4,64,512]{3,2,0,1:T(8,128)(2,1)}), bf16[3,4,64,512]{3,2,0,1:T(8,128)(2,1)S(1)}, u32[]{:S(2)}, u32[]{:S(2)}) %all-to-all-start.1) | async-done | bytes 786464 | tf_op jit(solution)/shard_map/all_to_all | solution.py:135
  185.5 7.1 %all-to-all-start.2 = ((bf16[128,2,512]{2,1,0:T(2,128)(2,1)}), bf16[128,2,512]{2,1,0:T(2,128)(2,1)S(1)}, u32[]{:S(2)}, u32[]{:S(2)}) async-start(bf16[128,2,512]{2,1,0:T(2,128)(2,1)} %broadcast_select_fusion), calls=%async_computation.2 | async-start | bytes 524288 | tf_op jit(solution)/shard_map/all_to_all | solution.py:143
  193.5 5.3 %collective-permute-start.2 = (bf16[4,64,512]{2,1,0:T(8,128)(2,1)}, bf16[4,64,512]{2,1,0:T(8,128)(2,1)S(1)}, u32[]{:S(2)}, u32[]{:S(2)}) collective-permute-start(bf16[4,64,512]{2,1,0:T(8,128)(2,1)} %get-tuple-element.501), channel_id=1, source_target_pairs={{4,0},{8,4},{12,8},{16,12},{20,16},{24,20},{28,24},{32,28},{36,32}... | collective-permute-start | bytes 786440 | tf_op jit(solution)/shard_map/ppermute | solution.py:12
  203.8 5.1 %collective-permute-done.3 = bf16[4,64,512]{2,1,0:T(8,128)(2,1)S(1)} collective-permute-done((bf16[4,64,512]{2,1,0:T(8,128)(2,1)}, bf16[4,64,512]{2,1,0:T(8,128)(2,1)S(1)}, u32[]{:S(2)}, u32[]{:S(2)}) %collective-permute-start.3) | collective-permute-done | bytes 262176 | tf_op jit(solution)/shard_map/ppermute | solution.py:12
  210.0 45.4 %while.29 = (s32[]{:T(128)}, f32[320,512]{1,0:T(8,128)}, s32[2560]{0:T(1024)S(1)}, bf16[2560,512]{1,0:T(8,128)(2,1)}, bf16[512,512]{1,0:T(8,128)(2,1)S(1)}, /*in...) while((s32[]{:T(128)}, f32[320,512]{1,0:T(8,128)}, ...), condition=%wide.region_9.10_spmd.clone, body=%wide.region_6.9_spmd.clone.sunk | while | flops 2194402048 | bytes 39485200 | solution.py:168
  210.1 4.7 %gather_fusion.1 = bf16[1280,512]{1,0:T(8,128)(2,1)} fusion(bf16[1344,512]{1,0:T(8,128)(2,1)S(1)} %get-tuple-element.712, s32[2048]{0:T(1024)S(1)} %pad_clamp_fusion.5), kind=kCustom, calls=%fused_computation.1.clone.clone.1 | custom fusion | bytes 2626560 | tf_op jit(solution)/shard_map/while/body/eval_jaxpr/jit(_take)/gather | solution.py:158
  219.0 5.1 %fusion.108 = (f32[1280]{0:T(1024)S(1)}, f32[1280,512]{0,1:T(8,128)}) fusion(bf16[512,512]{1,0:T(8,128)(2,1)} %get-tuple-element.714, f32[1280,512]{1,0:T(8,128)} %convolution_add_fusion.5, bf16[320,512]{1,0:T(8,128)(2,1)S(1)} %copy-done.12, s32[1280]{0:T(1024)S(1)} %dynamic_slice.68), kind=kOutput, calls=%fused_computation.104.clone.1 | convolution fusion | flops 1095514880 | bytes 6105088 | tf_op jit(solution)/shard_map/while/body/eval_jaxpr/dot_general | solution.py:164
  232.7 4.7 %gather_fusion.1 = bf16[1280,512]{1,0:T(8,128)(2,1)} fusion(bf16[1344,512]{1,0:T(8,128)(2,1)S(1)} %get-tuple-element.712, s32[2048]{0:T(1024)S(1)} %pad_clamp_fusion.5), kind=kCustom, calls=%fused_computation.1.clone.clone.1 | custom fusion | bytes 2626560 | tf_op jit(solution)/shard_map/while/body/eval_jaxpr/jit(_take)/gather | solution.py:158
  241.6 5.1 %fusion.108 = (f32[1280]{0:T(1024)S(1)}, f32[1280,512]{0,1:T(8,128)}) fusion(bf16[512,512]{1,0:T(8,128)(2,1)} %get-tuple-element.714, f32[1280,512]{1,0:T(8,128)} %convolution_add_fusion.5, bf16[320,512]{1,0:T(8,128)(2,1)S(1)} %copy-done.12, s32[1280]{0:T(1024)S(1)} %dynamic_slice.68), kind=kOutput, calls=%fused_computation.104.clone.1 | convolution fusion | flops 1095514880 | bytes 6105088 | tf_op jit(solution)/shard_map/while/body/eval_jaxpr/dot_general | solution.py:164
  (150 shorter events, 107.6 us)
Async XLA Ops:
  6.6 2.8 %copy-start.17 = (s32[3,4,128]{2,1,0:T(4,128)S(1)}, s32[3,4,128]{2,1,0:T(4,128)}, u32[]{:S(2)}) copy-start(s32[3,4,128]{2,1,0:T(4,128)} %param.35) | copy-start | bytes 18436
  6.6 3.5 %copy-start.4 = (f32[2048,512]{0,1:T(8,128)S(1)}, f32[2048,512]{0,1:T(8,128)}, u32[]{:S(2)}) copy-start(f32[2048,512]{0,1:T(8,128)} %get-tuple-element.505) | copy-start | bytes 12582916
  17.9 7.5 %copy-start.18 = (s32[3,4,64]{2,1,0:T(4,128)S(1)}, s32[3,4,64]{2,1,0:T(4,128)}, u32[]{:S(2)}) copy-start(s32[3,4,64]{2,1,0:T(4,128)} %param.41) | copy-start | bytes 9220
  17.9 7.6 %copy-start.24 = (s32[128,2]{0,1:T(2,128)S(1)}, s32[128,2]{0,1:T(2,128)}, u32[]{:S(2)}) copy-start(s32[128,2]{0,1:T(2,128)} %param.42) | copy-start | bytes 3076
  20.7 34.7 %copy-start.5 = (bf16[320,512]{1,0:T(8,128)(2,1)S(1)}, bf16[320,512]{1,0:T(8,128)(2,1)}, u32[]{:S(2)}) copy-start(bf16[320,512]{1,0:T(8,128)(2,1)} %param.40) | copy-start | bytes 983044
  20.7 25.3 %all-to-all-start = ((bf16[3,4,128,512]{3,2,0,1:T(8,128)(2,1)}), bf16[3,4,128,512]{3,2,0,1:T(8,128)(2,1)S(1)}, u32[]{:S(2)}, u32[]{:S(2)}) async-start(bf16[3,4,128,512]{3,2,0,1:T(8,128)(2,1)} %copy_select_fusion), calls=%async_computation | async-start | bytes 3145728 | tf_op jit(solution)/shard_map/all_to_all | solution.py:86
  47.2 11.9 %collective-permute-start = (bf16[4,128,512]{2,1,0:T(8,128)(2,1)}, bf16[4,128,512]{2,1,0:T(8,128)(2,1)S(1)}, u32[]{:S(2)}, u32[]{:S(2)}) collective-permute-start(bf16[4,128,512]{2,1,0:T(8,128)(2,1)} %get-tuple-element.498), channel_id=1, source_target_pairs={{4,0},{8,4},{12,8},{16,12},{20,16},{24,20},{28,24},{32,28},{36,32}... | collective-permute-start | bytes 1572872 | tf_op jit(solution)/shard_map/ppermute | solution.py:12
  51.7 12.8 %collective-permute-start.1 = (bf16[4,128,512]{2,1,0:T(8,128)(2,1)}, bf16[4,128,512]{2,1,0:T(8,128)(2,1)S(1)}, u32[]{:S(2)}, u32[]{:S(2)}) collective-permute-start(bf16[4,128,512]{2,1,0:T(8,128)(2,1)} %get-tuple-element.499), channel_id=1, source_target_pairs={{0,4},{4,8},{8,12},{12,16},{16,20},{20,24},{24,28},{28,32},{32,36}... | collective-permute-start | bytes 1572872 | tf_op jit(solution)/shard_map/ppermute | solution.py:12
  55.5 9.8 %copy-start.7 = (bf16[1,4,128,512]{3,2,1,0:T(8,128)(2,1)S(1)}, bf16[1,4,128,512]{3,2,1,0:T(8,128)(2,1)}, u32[]{:S(2)}) copy-start(bf16[1,4,128,512]{3,2,1,0:T(8,128)(2,1)} %get-tuple-element.500) | copy-start | bytes 1572868
  56.9 9.8 %copy-start.13 = (s32[8192]{0:T(1024)S(1)}, s32[8192]{0:T(1024)}, u32[]{:S(2)}) copy-start(s32[8192]{0:T(1024)} %param.36) | copy-start | bytes 98308
  59.2 5.4 %copy-start.10 = (bf16[4,128,512]{2,1,0:T(8,128)(2,1)}, bf16[4,128,512]{2,1,0:T(8,128)(2,1)S(1)}, u32[]{:S(2)}) copy-start(bf16[4,128,512]{2,1,0:T(8,128)(2,1)S(1)} %collective-permute-done) | copy-start | bytes 1572868
  66.7 97.6 %copy-start.8 = (f32[320,512]{1,0:T(8,128)S(1)}, f32[320,512]{1,0:T(8,128)}, u32[]{:S(2)}) copy-start(f32[320,512]{1,0:T(8,128)} %fusion.52) | copy-start | bytes 1966084
  168.4 2.7 %copy-start.20 = (pred[3,4,64]{2,0,1:T(4,128)(4,1)S(1)}, pred[3,4,64]{2,0,1:T(4,128)(4,1)}, u32[]{:S(2)}) copy-start(pred[3,4,64]{2,0,1:T(4,128)(4,1)} %copy.40) | copy-start | bytes 2308
  171.1 4.9 %copy-start.21 = (s32[256,1]{0,1:T(1,128)S(1)}, s32[256,1]{0,1:T(1,128)}, u32[]{:S(2)}) copy-start(s32[256,1]{0,1:T(1,128)} %compare_select_fusion.6) | copy-start | bytes 3076
  172.2 5.1 %copy-start.16 = (pred[128,2]{1,0:T(8,128)(4,1)S(1)}, pred[128,2]{1,0:T(8,128)(4,1)}, u32[]{:S(2)}) copy-start(pred[128,2]{1,0:T(8,128)(4,1)} %copy.44) | copy-start | bytes 772
  172.2 6.1 %copy-start.9 = (bf16[512,512]{1,0:T(8,128)(2,1)S(1)}, bf16[512,512]{1,0:T(8,128)(2,1)}, u32[]{:S(2)}) copy-start(bf16[512,512]{1,0:T(8,128)(2,1)} %param.57) | copy-start | bytes 1572868
  172.2 13.3 %all-to-all-start.1 = ((bf16[3,4,64,512]{3,2,0,1:T(8,128)(2,1)}), bf16[3,4,64,512]{3,2,0,1:T(8,128)(2,1)S(1)}, u32[]{:S(2)}, u32[]{:S(2)}) async-start(bf16[3,4,64,512]{3,2,0,1:T(8,128)(2,1)} %copy_select_fusion.1), calls=%async_computation.1 | async-start | bytes 1572864 | tf_op jit(solution)/shard_map/all_to_all | solution.py:135
  185.5 17.5 %all-to-all-start.2 = ((bf16[128,2,512]{2,1,0:T(2,128)(2,1)}), bf16[128,2,512]{2,1,0:T(2,128)(2,1)S(1)}, u32[]{:S(2)}, u32[]{:S(2)}) async-start(bf16[128,2,512]{2,1,0:T(2,128)(2,1)} %broadcast_select_fusion), calls=%async_computation.2 | async-start | bytes 524288 | tf_op jit(solution)/shard_map/all_to_all | solution.py:143
  193.5 10.3 %collective-permute-start.2 = (bf16[4,64,512]{2,1,0:T(8,128)(2,1)}, bf16[4,64,512]{2,1,0:T(8,128)(2,1)S(1)}, u32[]{:S(2)}, u32[]{:S(2)}) collective-permute-start(bf16[4,64,512]{2,1,0:T(8,128)(2,1)} %get-tuple-element.501), channel_id=1, source_target_pairs={{4,0},{8,4},{12,8},{16,12},{20,16},{24,20},{28,24},{32,28},{36,32}... | collective-permute-start | bytes 786440 | tf_op jit(solution)/shard_map/ppermute | solution.py:12
  198.8 10.0 %collective-permute-start.3 = (bf16[4,64,512]{2,1,0:T(8,128)(2,1)}, bf16[4,64,512]{2,1,0:T(8,128)(2,1)S(1)}, u32[]{:S(2)}, u32[]{:S(2)}) collective-permute-start(bf16[4,64,512]{2,1,0:T(8,128)(2,1)} %get-tuple-element.502), channel_id=1, source_target_pairs={{0,4},{4,8},{8,12},{12,16},{16,20},{20,24},{24,28},{28,32},{32,36}... | collective-permute-start | bytes 786440 | tf_op jit(solution)/shard_map/ppermute | solution.py:12
  202.9 7.0 %copy-start.3 = (bf16[512,512]{1,0:T(8,128)(2,1)S(1)}, bf16[512,512]{1,0:T(8,128)(2,1)}, u32[]{:S(2)}) copy-start(bf16[512,512]{1,0:T(8,128)(2,1)} %param.58) | copy-start | bytes 1572868
  202.9 7.0 %copy-start.14 = (s32[2560]{0:T(1024)S(1)}, s32[2560]{0:T(1024)}, u32[]{:S(2)}) copy-start(s32[2560]{0:T(1024)} %param.43) | copy-start | bytes 30724
  203.0 7.0 %copy-start.15 = (s32[2560]{0:T(1024)S(1)}, s32[2560]{0:T(1024)}, u32[]{:S(2)}) copy-start(s32[2560]{0:T(1024)} %param.44) | copy-start | bytes 30724
  255.4 2.6 %copy-start.23 = (f32[512]{0:T(512)S(1)}, f32[512]{0:T(512)}, u32[]{:S(2)}) copy-start(f32[512]{0:T(512)} %param.63) | copy-start | bytes 6148
  (11 other events, 22.4 us)
where the time goes:
time: 260 us; the launch traced here: 259 us
  matrix products  97.1 us (37%)
  local copies, waits for them, and re-layouts  73.7 us (28%)
  waiting for transfers between devices  36.3 us (14%)
  starting transfers between devices  29.1 us (11%)
  other arithmetic  22.3 us (9%)
    gather x4, local copies, waits for them, and re-layouts, grid_block(): jnp.take(lookup, sources, axis=0).astype(jnp.float32)  36.5 us
    dot_general x4, matrix products, grid_block(): jnp.dot(edge_act, msg_weight, preferred_element_type=jnp.float32)  26.1 us
    dot_general x6, matrix products, scatter_rows(): lax.dot_general(onehot, values, (((0,), (0,)), ((), ())), preferred_eleme...  24.1 us
    all_to_all x1, waiting for transfers between devices, body(): lax.all_to_all(stacked, 'sub', split_axis=1, concat_axis=1, tiled=True)  19.8 us
    ppermute x4, starting transfers between devices, shifted_2(): lax.ppermute(value, axis, [(source, source + steps) for source in range(f...  13.6 us
    dot_general x4, matrix products, grid_block(): jnp.dot(onehot, receiver, preferred_element_type=jnp.float32)  11.4 us
    ppermute x4, waiting for transfers between devices, shifted_2(): lax.ppermute(value, axis, [(source, source + steps) for source in range(f...  10.4 us
    dot_general x2, matrix products, mesh_step(): jnp.dot(edge_hidden, edge_out, preferred_element_type=jnp.float32)  10.2 us
  transfers between devices with their start and end apart: 7, of which 4 were waited for; matrix products, arithmetic and copies ran while one was open for 5% of the time, Pallas kernels for 0%

commit v1 on v0

v1 whole, which is shorter than its diff:
```python
import functools

import jax
import jax.numpy as jnp
from jax import lax
from jax.experimental import pallas as pl
from jax.experimental.pallas import tpu as pltpu
from jax.sharding import PartitionSpec as P

LANES = 128
EDGE_BLOCK = 512
VMEM_BYTES = 48 * 1024 * 1024


def shifted(value, steps):
    count = lax.axis_size("band")
    first, last = (max(0, -steps), min(count, count - steps))
    return lax.ppermute(value, "band", [(source, source + steps) for source in range(first, last)])


def layer_norm(values):
    row_mean = jnp.mean(values, axis=-1, keepdims=True)
    centred = values - row_mean
    variance = jnp.mean(centred * centred, axis=-1, keepdims=True)
    return centred * lax.rsqrt(variance + 1e-05)


def silu(values):
    half = 0.5 * values
    return half + half * jnp.tanh(half)


def dot(left, right):
    return jnp.dot(left, right, preferred_element_type=jnp.float32)


def half(values):
    return values.astype(jnp.bfloat16)


def column(row):
    return jnp.broadcast_to(row, (LANES, LANES)).T


def columns(ref, first, count):
    return jnp.concatenate([column(ref[pl.ds(first + k, 1), :]) for k in range(count)], axis=0)


def row_of(ref, first, count):
    return jnp.concatenate([ref[pl.ds(first + k, 1), :] for k in range(count)], axis=1)


def picks(indices, width, offset=0):
    lane = lax.broadcasted_iota(jnp.int32, indices.shape, 1)
    parts = [
        half(jnp.where(indices == lane + (offset + first), 1.0, 0.0))
        for first in range(0, width, LANES)
    ]
    return jnp.concatenate(parts, axis=1)


def scatter_picks(row, height):
    shape = (height, row.shape[1])
    sub = lax.broadcasted_iota(jnp.int32, shape, 0)
    return half(jnp.where(sub == jnp.broadcast_to(row, shape), 1.0, 0.0))


def whole(*shape):
    return pl.BlockSpec(memory_space=pltpu.VMEM)


def in_smem():
    return pl.BlockSpec(memory_space=pltpu.SMEM)


def local_call(kernel, out_shape, in_specs, scratch=(), flops=0, nbytes=0):
    return pl.pallas_call(
        kernel,
        out_shape=out_shape,
        in_specs=in_specs,
        out_specs=jax.tree.map(lambda _: pl.BlockSpec(memory_space=pltpu.VMEM), out_shape),
        scratch_shapes=list(scratch),
        compiler_params=pltpu.CompilerParams(vmem_limit_bytes=VMEM_BYTES),
        cost_estimate=pl.CostEstimate(flops=flops, bytes_accessed=nbytes, transcendentals=0),
    )


def pick_grid_kernel(send_ref, grid_ref, out_ref):
    rows, width = grid_ref.shape
    slots = send_ref.shape[0]
    out_ref[...] = jnp.zeros_like(out_ref)

    def step(k, carry):
        onehot = picks(columns(send_ref, 2 * k, 2), rows)
        out_ref[pl.ds(pl.multiple_of(2 * k * LANES, 2 * LANES), 2 * LANES), 0:width] = half(
            dot(onehot, grid_ref[...])
        )
        return carry

    lax.fori_loop(0, slots // 2, step, 0)


def encoder_kernel(
    place_ref,
    live_ref,
    first_ref,
    second_ref,
    third_ref,
    src_ref,
    dst_ref,
    geo_ref,
    embed_ref,
    near_ref,
    far_ref,
    enc_in_ref,
    enc_out_ref,
    send_proj_ref,
    recv_proj_ref,
    geo_proj_ref,
    msg_ref,
    node_self_ref,
    node_agg_ref,
    node_out_ref,
    gain_ref,
    proc_send_ref,
    proc_recv_ref,
    latent_ref,
    pair_ref,
    out_ref,
    table_ref,
    enc_ref,
    sum_ref,
):
    mesh_rows, latent = embed_ref.shape
    chunk = first_ref.shape[0]
    base = table_ref.shape[0] - 3 * chunk
    geo_rows = geo_ref.shape[0]
    is_first = place_ref[0] == 0
    is_last = place_ref[0] == place_ref[1] - 1
    polar = is_first | is_last
    live = live_ref[0]

    enc_ref[...] = jnp.zeros_like(enc_ref)
    enc_ref[0 : enc_in_ref.shape[0], :] = enc_in_ref[...]
    table_ref[0:mesh_rows, :] = half(dot(embed_ref[...], recv_proj_ref[...]))
    table_ref[mesh_rows:base, :] = jnp.concatenate(
        [
            geo_proj_ref[...].astype(jnp.float32),
            jnp.zeros((base - mesh_rows - geo_rows, latent), jnp.float32),
        ],
        axis=0,
    ).astype(jnp.bfloat16)

    def encode(rows_ref, place):
        hidden = half(silu(dot(rows_ref[...], enc_ref[...])))
        lat = half(layer_norm(dot(hidden, enc_out_ref[...])))
        table_ref[pl.ds(place, chunk), :] = half(dot(lat, send_proj_ref[...]))

    start = jnp.where(is_last, base - chunk, base)

    @pl.when(jnp.logical_not(is_last))
    def _():
        encode(first_ref, base)

    encode(second_ref, pl.multiple_of(start + chunk, chunk))

    @pl.when(jnp.logical_not(is_first))
    def _():
        encode(third_ref, pl.multiple_of(start + 2 * chunk, chunk))

    sum_ref[...] = jnp.zeros_like(sum_ref)
    per = EDGE_BLOCK // LANES
    src_shift = jnp.where(is_last, chunk, 0)

    def geometry(block):
        pieces = []
        for k in range(per):
            lane0 = pl.multiple_of(block * EDGE_BLOCK + k * LANES, LANES)
            geo = geo_ref[:, pl.ds(lane0, LANES)].astype(jnp.float32)
            low = mesh_rows % LANES
            square = jnp.concatenate(
                [
                    jnp.zeros((low, LANES), jnp.float32),
                    geo,
                    jnp.zeros((LANES - low - geo_rows, LANES), jnp.float32),
                ],
                axis=0,
            )
            pieces.append(square.T)
        return jnp.concatenate(pieces, axis=0)

    def own_picks(block):
        target = columns(dst_ref, block * per, per)
        lane = lax.broadcasted_iota(jnp.int32, target.shape, 1)
        geo_block = mesh_rows // LANES
        parts = []
        for k in range(base // LANES):
            if k > geo_block:
                parts.append(jnp.zeros(target.shape, jnp.bfloat16))
                continue
            part = jnp.where(target == lane + k * LANES, 1.0, 0.0)
            if k == geo_block:
                part = part + geometry(block)
            parts.append(half(part))
        return jnp.concatenate(parts, axis=1)

    def finish(block, pre):
        act = half(silu(pre))
        lane = lax.broadcasted_iota(jnp.int32, (1, EDGE_BLOCK), 1)
        target = row_of(dst_ref, block * per, per)
        target = jnp.where(block * EDGE_BLOCK + lane < live, target, -1)
        sum_ref[...] += dot(scatter_picks(target, mesh_rows), act)

    def in_order(block, carry):
        pre = dot(own_picks(block), table_ref[0:base, :])
        place = pl.multiple_of(base + block * EDGE_BLOCK, EDGE_BLOCK)
        finish(block, pre + table_ref[pl.ds(place, EDGE_BLOCK), :].astype(jnp.float32))
        return carry

    def at_random(lookup_rows, block, carry):
        source = columns(src_ref, block * per, per) - src_shift
        onehot = jnp.concatenate([own_picks(block), picks(source, lookup_rows)], axis=1)
        finish(block, dot(onehot, table_ref[0 : base + lookup_rows, :]))
        return carry

    blocks = pl.cdiv(live, EDGE_BLOCK)
    ordered = jnp.where(polar, 2, 3) * (chunk // EDGE_BLOCK)
    lax.fori_loop(0, ordered, in_order, 0)

    @pl.when(polar)
    def _():
        lax.fori_loop(ordered, blocks, functools.partial(at_random, 2 * chunk), 0)

    @pl.when(jnp.logical_not(polar))
    def _():
        lax.fori_loop(ordered, blocks, functools.partial(at_random, 3 * chunk), 0)

    total = sum_ref[...]
    high = half(total)
    low = half(total - high.astype(jnp.float32))
    inflow = half(dot(high, msg_ref[...]) + dot(low, msg_ref[...]))
    embed = embed_ref[...]
    node_act = half(silu(dot(embed, node_self_ref[...]) + dot(inflow, node_agg_ref[...])))
    mesh_latent = half(
        embed.astype(jnp.float32) + layer_norm(dot(node_act, node_out_ref[...])) * gain_ref[...]
    )
    latent_ref[...] = mesh_latent
    sender = half(dot(mesh_latent, proc_send_ref[...]))
    pair_ref[0:mesh_rows, :] = sender
    pair_ref[mesh_rows : 2 * mesh_rows, :] = half(dot(mesh_latent, proc_recv_ref[...]))
    padded = -(-mesh_rows // LANES) * LANES
    sender_pad = jnp.concatenate(
        [sender, jnp.zeros((padded - mesh_rows, latent), jnp.bfloat16)], axis=0
    )
    near_slots = near_ref.shape[0]
    for k in range(near_slots):
        out_ref[k * LANES : (k + 1) * LANES, :] = half(
            dot(picks(column(near_ref[k : k + 1, :]), padded), sender_pad)
        )
    for k in range(far_ref.shape[0]):
        out_ref[(near_slots + k) * LANES : (near_slots + k + 1) * LANES, :] = half(
            dot(picks(column(far_ref[k : k + 1, :]), padded), sender_pad)
        )


def edge_start_kernel(src_ref, dst_ref, lat_ref, self_ref, pair_ref, out_ref):
    mesh_rows = pair_ref.shape[0] // 2
    block_rows = 512
    per = block_rows // LANES
    pairs = pair_ref[...]

    def step(block, carry):
        row0 = pl.multiple_of(block * block_rows, block_rows)
        source = columns(src_ref, block * per, per)
        target = columns(dst_ref, block * per, per) + mesh_rows
        lane = lax.broadcasted_iota(jnp.int32, source.shape, 1)
        parts = []
        for first in range(0, 2 * mesh_rows, LANES):
            hit = None
            if first < mesh_rows:
                own = jnp.where(source < mesh_rows, source, -1)
                hit = own == lane + first
            if first + LANES > mesh_rows:
                other = target == lane + first
                hit = other if hit is None else hit | other
            parts.append(half(jnp.where(hit, 1.0, 0.0)))
        onehot = jnp.concatenate(parts, axis=1)
        out_ref[pl.ds(row0, block_rows), :] = dot(
            lat_ref[pl.ds(row0, block_rows), :], self_ref[...]
        ) + dot(onehot, pairs)
        return carry

    lax.fori_loop(0, lat_ref.shape[0] // block_rows, step, 0)


def edge_finish_kernel(
    src_ref,
    dst_ref,
    lat_ref,
    pre_ref,
    near0_ref,
    near1_ref,
    near2_ref,
    far_ref,
    latent_ref,
    edge_out_ref,
    upd_self_ref,
    upd_agg_ref,
    upd_out_ref,
    gain_ref,
    out_ref,
    table_ref,
    sum_ref,
):
    mesh_rows = latent_ref.shape[0]
    block_rows = 512
    per = block_rows // LANES
    near = near0_ref.shape[0]
    table_ref[0:near, :] = near0_ref[...]
    table_ref[near : 2 * near, :] = near1_ref[...]
    table_ref[2 * near : 3 * near, :] = near2_ref[...]
    table_ref[3 * near :, :] = far_ref[...]
    sum_ref[...] = jnp.zeros_like(sum_ref)

    def step(block, carry):
        row0 = pl.multiple_of(block * block_rows, block_rows)
        source = columns(src_ref, block * per, per) - mesh_rows
        pre = pre_ref[pl.ds(row0, block_rows), :] + dot(
            picks(source, table_ref.shape[0]), table_ref[...]
        )
        hidden = half(silu(pre))
        new = half(
            lat_ref[pl.ds(row0, block_rows), :].astype(jnp.float32)
            + layer_norm(dot(hidden, edge_out_ref[...]))
        )
        sum_ref[...] += dot(scatter_picks(row_of(dst_ref, block * per, per), mesh_rows), new)
        return carry

    lax.fori_loop(0, lat_ref.shape[0] // block_rows, step, 0)
    inflow = half(sum_ref[...])
    latent = latent_ref[...]
    act = half(silu(dot(latent, upd_self_ref[...]) + dot(inflow, upd_agg_ref[...])))
    out_ref[...] = half(
        latent.astype(jnp.float32) + layer_norm(dot(act, upd_out_ref[...])) * gain_ref[...]
    )


def body(
    grid_input,
    grid_send,
    grid_edge_src,
    grid_edge_dst,
    edge_count,
    grid_edge_geo,
    mesh_embed,
    mesh_near_send,
    mesh_far_send,
    mesh_edge_src,
    mesh_edge_dst,
    mesh_edge_lat,
    enc_in,
    enc_out,
    send_proj,
    recv_proj,
    geo_proj,
    msg_weight,
    node_self,
    node_agg,
    node_out,
    mesh_gain,
    proc_send,
    proc_recv,
    edge_self,
    edge_out,
    upd_self,
    upd_agg,
    upd_out,
    out_gain,
):
    band_count = lax.axis_size("band")
    sub_count = lax.axis_size("sub")
    slot_cap = grid_send.shape[2]
    near_cap = mesh_near_send.shape[2]
    far_cap = mesh_far_send.shape[1]
    mesh_rows, latent = mesh_embed.shape
    edges = grid_edge_src.shape[0]
    mesh_edges = mesh_edge_src.shape[0]
    wide = 256
    bf16, f32 = jnp.bfloat16, jnp.float32

    sent = 3 * sub_count * slot_cap
    payload = local_call(
        pick_grid_kernel,
        jax.ShapeDtypeStruct((sent, wide), bf16),
        [whole()] * 2,
        flops=2 * sent * grid_input.shape[0] * wide,
        nbytes=2 * wide * (sent + grid_input.shape[0]),
    )(grid_send.reshape(sent // LANES, LANES), grid_input)
    in_sub = lax.all_to_all(
        payload.reshape(3, sub_count, slot_cap, wide), "sub", split_axis=1, concat_axis=1, tiled=True
    )
    arrived = [
        part.reshape(sub_count * slot_cap, wide)
        for part in (shifted(in_sub[0], -1), in_sub[1], shifted(in_sub[2], 1))
    ]

    near_index = mesh_near_send.transpose(1, 0, 2).reshape(-1, LANES)
    far_index = (
        mesh_far_send.reshape(band_count, sub_count, far_cap).transpose(1, 0, 2).reshape(-1, LANES)
    )
    place = jnp.stack([lax.axis_index("band"), jnp.int32(band_count)]).astype(jnp.int32)
    near_total = 3 * sub_count * near_cap
    far_total = band_count * sub_count * far_cap
    mesh_latent, pairs, outgoing = local_call(
        encoder_kernel,
        (
            jax.ShapeDtypeStruct((mesh_rows, latent), bf16),
            jax.ShapeDtypeStruct((2 * mesh_rows, latent), bf16),
            jax.ShapeDtypeStruct((near_total + far_total, latent), bf16),
        ),
        [in_smem()] * 2 + [whole()] * 21,
        scratch=[
            pltpu.VMEM((512 + sent, latent), bf16),
            pltpu.VMEM((wide, latent), bf16),
            pltpu.VMEM((mesh_rows, latent), f32),
        ],
        flops=2 * edges * 2048 * latent,
        nbytes=16 << 20,
    )(
        place,
        edge_count,
        *arrived,
        grid_edge_src.reshape(-1, LANES),
        grid_edge_dst.reshape(-1, LANES),
        grid_edge_geo,
        mesh_embed,
        near_index,
        far_index,
        enc_in,
        enc_out,
        send_proj,
        recv_proj,
        geo_proj,
        msg_weight,
        node_self,
        node_agg,
        node_out,
        mesh_gain.reshape(1, latent),
        proc_send,
        proc_recv,
    )

    mesh_src = mesh_edge_src.reshape(-1, LANES)
    mesh_dst = mesh_edge_dst.reshape(-1, LANES)
    near_out = outgoing[:near_total].reshape(sub_count, 3 * near_cap, latent)
    far_out = outgoing[near_total:].reshape(sub_count, band_count * far_cap, latent)
    near_sub = lax.all_to_all(near_out, "sub", split_axis=0, concat_axis=0, tiled=True).reshape(
        sub_count, 3, near_cap, latent
    )
    near_parts = [
        part.reshape(sub_count * near_cap, latent)
        for part in (shifted(near_sub[:, 0], -1), near_sub[:, 1], shifted(near_sub[:, 2], 1))
    ]
    far_sub = lax.all_to_all(far_out, "sub", split_axis=0, concat_axis=0, tiled=True)
    far_band = lax.all_to_all(
        far_sub.reshape(sub_count, band_count, far_cap, latent).transpose(1, 0, 2, 3),
        "band",
        split_axis=0,
        concat_axis=0,
        tiled=True,
    )
    far_rows = far_band.reshape(far_total, latent)

    pre = local_call(
        edge_start_kernel,
        jax.ShapeDtypeStruct((mesh_edges, latent), f32),
        [whole()] * 5,
        flops=2 * mesh_edges * 1280 * latent,
        nbytes=8 << 20,
    )(mesh_src, mesh_dst, mesh_edge_lat, edge_self, pairs)
    return local_call(
        edge_finish_kernel,
        jax.ShapeDtypeStruct((mesh_rows, latent), bf16),
        [whole()] * 14,
        scratch=[
            pltpu.VMEM((near_total + far_total, latent), bf16),
            pltpu.VMEM((mesh_rows, latent), f32),
        ],
        flops=2 * mesh_edges * 2048 * latent,
        nbytes=12 << 20,
    )(
        mesh_src,
        mesh_dst,
        mesh_edge_lat,
        pre,
        *near_parts,
        far_rows,
        mesh_latent,
        edge_out,
        upd_self,
        upd_agg,
        upd_out,
        out_gain.reshape(1, latent),
    )


def solution(mesh):
    rows = P(("band", "sub"), None)
    blocks = P(("band", "sub"), None, None)
    flat = P(("band", "sub"))
    return jax.shard_map(
        body,
        mesh=mesh,
        in_specs=(
            rows,
            blocks,
            flat,
            flat,
            flat,
            P(None, ("band", "sub")),
            rows,
            blocks,
            rows,
            flat,
            flat,
            rows,
        )
        + (P(),) * 18,
        out_specs=rows,
        check_vma=False,
    )
```

time: 260 us -> 141 us (0.54)
  matrix products: 97.1 us -> 0 us
  local copies, waits for them, and re-layouts: 73.7 us -> 30.1 us
  Pallas kernels: 0 us -> 38.5 us
  other arithmetic: 22.3 us -> 0.08 us
  waiting for transfers between devices: 36.3 us -> 19.1 us
  blocking collectives: 0 us -> 16.6 us
  starting transfers between devices: 29.1 us -> 34.9 us
    dot_general x27 -> x0, matrix products: 97.1 us -> none  [the longest x4 26.1 us: grid_block(): jnp.dot(edge_act, msg_weight, preferred_element_type=jnp.float32)]
    gather x10 -> x0, local copies, waits for them, and re-layouts: 55.4 us -> none  [the longest x4 36.5 us: grid_block(): jnp.take(lookup, sources, axis=0).astype(jnp.float32)]
    pallas_call x0 -> x4, Pallas kernels: none -> 38.5 us  [the longest x1 15.9 us: body(): local_call(encoder_kernel, (jax.ShapeDtypeStruct((mesh_rows, latent), bf1...]
    all_to_all x0 -> x1, blocking collectives: none -> 16.6 us  [body(): lax.all_to_all(payload.reshape(3, sub_count, slot_cap, wide), 'sub', spli...]
    unnamed x45 -> x59, local copies, waits for them, and re-layouts: 2.74 us -> 17.8 us
    dynamic_slice x10 -> x0, local copies, waits for them, and re-layouts: 10.8 us -> none  [the longest x4 7.89 us: mesh_step(): lats = lax.dynamic_slice_in_dim(mesh_edge_lat, first_row, mesh_block)]
    ppermute x4, waiting for transfers between devices: 10.4 us -> 1.41 us  [shifted(): lax.ppermute(value, 'band', [(source, source + steps) for source in range...]
    all_to_all x3, waiting for transfers between devices: 25.8 us -> 17.7 us  [the longest x1 12 us: body(): lax.all_to_all(near_out, 'sub', split_axis=0, concat_axis=0, tiled=True)]
  transfers between devices with their start and end apart: 7 -> 7, of which waited for: 4 -> 3; matrix products, arithmetic and copies ran while one was open for 5% -> 6% of each run, Pallas kernels for 0% -> 5%
where the time goes in v1:
time: 141 us; the launch traced here: 140 us
  Pallas kernels  38.5 us (27%)
  starting transfers between devices  34.9 us (25%)
  local copies, waits for them, and re-layouts  30.1 us (21%)
  waiting for transfers between devices  19.1 us (14%)
  blocking collectives  16.6 us (12%)
    unnamed x59, local copies, waits for them, and re-layouts  17.8 us
    all_to_all x1, blocking collectives, body(): lax.all_to_all(payload.reshape(3, sub_count, slot_cap, wide), 'sub', spli...  16.6 us
    pallas_call x1, Pallas kernels, body(): local_call(encoder_kernel, (jax.ShapeDtypeStruct((mesh_rows, latent), bf1...  15.9 us
    ppermute x4, starting transfers between devices, shifted(): lax.ppermute(value, 'band', [(source, source + steps) for source in range...  15.5 us
    pallas_call x1, Pallas kernels, body(): local_call(edge_finish_kernel, jax.ShapeDtypeStruct((mesh_rows, latent),...  12.8 us
    all_to_all x1, waiting for transfers between devices, body(): lax.all_to_all(near_out, 'sub', split_axis=0, concat_axis=0, tiled=True)  12 us
    all_to_all x1, starting transfers between devices, body(): lax.all_to_all(far_sub.reshape(sub_count, band_count, far_cap, latent).tr...  11.5 us
    pallas_call x1, Pallas kernels, body(): local_call(edge_start_kernel, jax.ShapeDtypeStruct((mesh_edges, latent),...  6.94 us
  transfers between devices with their start and end apart: 7, of which 3 were waited for; matrix products, arithmetic and copies ran while one was open for 6% of the time, Pallas kernels for 5%

profile of v1, /device:TPU:6, one launch (start us, length us, event | category | flops | bytes accessed | tf_op | source)
XLA Modules:
  0.0 140.3 jit_solution(6334493373606692275)
XLA Ops:
  0.7 1.5 %copy.39.grid_ref = bf16[2048,227]{1,0:T(8,128)(2,1)S(1)} copy(bf16[2048,227]{0,1:T(8,128)(2,1)} %param.30) | data formatting | bytes 1859584 | tf_op args[0]
  2.3 2.9 %shard_map.280 = bf16[1536,256]{1,0:T(8,128)(2,1)S(1)} custom-call(s32[12,128]{1,0:T(8,128)S(1)} %reshape.62.send_ref, bf16[2048,227]{1,0:T(8,128)(2,1)S(1)} %copy.39.grid_ref), custom_call_target="tpu_custom_call" | custom-call | flops 1610612736 | bytes 1835008 | tf_op jit(solution)/shard_map/pallas_call | solution.py:392
  5.3 16.6 %all_to_all.20 = bf16[3,4,128,256]{3,2,0,1:T(8,128)(2,1)S(1)} all-to-all(bf16[3,4,128,256]{3,2,0,1:T(8,128)(2,1)S(1)} %copy.40), channel_id=1, replica_groups=mesh['band'=32,'sub'=4] {'sub'}, dimensions={1} | all-to-all | bytes 1572864 | tf_op jit(solution)/shard_map/all_to_all | solution.py:399
  22.7 1.9 %collective-permute-start.1 = (bf16[4,128,256]{2,1,0:T(8,128)(2,1)}, bf16[4,128,256]{2,1,0:T(8,128)(2,1)S(1)}, u32[]{:S(2)}, u32[]{:S(2)}) collective-permute-start(bf16[4,128,256]{2,1,0:T(8,128)(2,1)} %get-tuple-element.14), channel_id=1, source_target_pairs={{0,4},{4,8},{8,12},{12,16},{16,20},{20,24},{24,28},{28,32},{32,36}... | collective-permute-start | bytes 786440 | tf_op jit(solution)/shard_map/ppermute | solution.py:18
  24.6 5.8 %collective-permute-start = (bf16[4,128,256]{2,1,0:T(8,128)(2,1)}, bf16[4,128,256]{2,1,0:T(8,128)(2,1)S(1)}, u32[]{:S(2)}, u32[]{:S(2)}) collective-permute-start(bf16[4,128,256]{2,1,0:T(8,128)(2,1)} %get-tuple-element.16), channel_id=1, source_target_pairs={{4,0},{8,4},{12,8},{16,12},{20,16},{24,20},{28,24},{32,28},{36,32}... | collective-permute-start | bytes 786440 | tf_op jit(solution)/shard_map/ppermute | solution.py:18
  33.1 1.4 %collective-permute-done = bf16[4,128,256]{2,1,0:T(8,128)(2,1)S(1)} collective-permute-done((bf16[4,128,256]{2,1,0:T(8,128)(2,1)}, bf16[4,128,256]{2,1,0:T(8,128)(2,1)S(1)}, u32[]{:S(2)}, u32[]{:S(2)}) %collective-permute-start) | collective-permute-done | bytes 262176 | tf_op jit(solution)/shard_map/ppermute | solution.py:18
  36.3 1.0 copy-done.6
  38.4 1.0 copy-done.8
  42.9 15.9 %shard_map.281 = (bf16[320,512]{1,0:T(8,128)(2,1)S(1)}, bf16[640,512]{1,0:T(8,128)(2,1)}, bf16[1024,512]{1,0:T(8,128)(2,1)}) custom-call(s32[2]{0:T(128)S(1)} %pad_add_fusion.place_ref, s32[1]{0:T(128)S(6)} %copy.45.live_ref, bf16[512,256]{1,0:T(8,128)(2,1)S(1)} %bitcast.36, bf16[512,256]{1,0:T(8,128)(2,1)S(1)} %bitcast.33, bf16[512,256]{1,0:T(8,128)(2,1)S(1)} %bitcast.35, ...), custom_call_target="tpu_custom_call" | custom-call | flops 17179869184 | bytes 16777216 | tf_op jit(solution)/shard_map/pallas_call | solution.py:414
  59.5 1.8 %slice.31 = bf16[256,512]{1,0:T(8,128)(2,1)} slice(bf16[1024,512]{1,0:T(8,128)(2,1)} %get-tuple-element.9), slice={[768:1024], [0:512]} | slice | bytes 524288 | tf_op jit(solution)/shard_map/slice | solution.py:456
  61.3 3.7 %all-to-all-start.2 = ((bf16[4,64,512]{2,1,0:T(8,128)(2,1)}), bf16[4,64,512]{2,1,0:T(8,128)(2,1)S(1)}, u32[]{:S(2)}, u32[]{:S(2)}) async-start(bf16[4,64,512]{2,1,0:T(8,128)(2,1)} %bitcast.21), calls=%async_computation.2 | async-start | bytes 524288 | tf_op jit(solution)/shard_map/all_to_all | solution.py:464
  65.0 2.1 %slice.27 = bf16[768,512]{1,0:T(8,128)(2,1)} slice(bf16[1024,512]{1,0:T(8,128)(2,1)} %get-tuple-element.9), slice={[0:768], [0:512]} | slice | bytes 1572864 | tf_op jit(solution)/shard_map/slice | solution.py:455
  67.1 5.7 %all-to-all-done.2 = bf16[4,64,512]{2,1,0:T(8,128)(2,1)S(1)} async-done(((bf16[4,64,512]{2,1,0:T(8,128)(2,1)}), bf16[4,64,512]{2,1,0:T(8,128)(2,1)S(1)}, u32[]{:S(2)}, u32[]{:S(2)}) %all-to-all-start.2) | async-done | bytes 262176 | tf_op jit(solution)/shard_map/all_to_all | solution.py:464
  72.8 4.2 %all-to-all-start.1 = ((bf16[4,192,512]{2,1,0:T(8,128)(2,1)}), bf16[4,192,512]{2,1,0:T(8,128)(2,1)}, u32[]{:S(2)}, u32[]{:S(2)}) async-start(bf16[4,192,512]{2,1,0:T(8,128)(2,1)} %bitcast.14), calls=%async_computation.1 | async-start | bytes 1572864 | tf_op jit(solution)/shard_map/all_to_all | solution.py:457
  77.9 12.0 %all-to-all-done.1 = bf16[4,192,512]{2,1,0:T(8,128)(2,1)} async-done(((bf16[4,192,512]{2,1,0:T(8,128)(2,1)}), bf16[4,192,512]{2,1,0:T(8,128)(2,1)}, u32[]{:S(2)}, u32[]{:S(2)}) %all-to-all-start.1) | async-done | bytes 786464 | tf_op jit(solution)/shard_map/all_to_all | solution.py:457
  89.9 11.5 %all-to-all-start.3 = ((bf16[32,4,2,512]{3,1,2,0:T(4,128)(2,1)}), bf16[32,4,2,512]{3,1,2,0:T(4,128)(2,1)S(1)}, u32[]{:S(2)}, u32[]{:S(2)}) async-start(bf16[32,4,2,512]{3,1,2,0:T(4,128)(2,1)} %bitcast.23), calls=%async_computation.3 | async-start | bytes 524288 | tf_op jit(solution)/shard_map/all_to_all | solution.py:465
  101.4 2.0 %slice_bitcast_fusion = (bf16[4,64,512]{2,1,0:T(8,128)(2,1)}, bf16[4,1,64,512]{3,2,1,0:T(8,128)(2,1)S(1)}, bf16[4,64,512]{2,1,0:T(8,128)(2,1)}) fusion(bf16[4,3,64,512]{3,2,1,0:T(8,128)(2,1)} %bitcast.15), kind=kLoop, calls=%fused_computation | loop fusion | bytes 1572864 | tf_op jit(solution)/shard_map/squeeze | solution.py:462
  103.4 2.0 %collective-permute-start.3 = (bf16[4,64,512]{2,1,0:T(8,128)(2,1)}, bf16[4,64,512]{2,1,0:T(8,128)(2,1)S(1)}, u32[]{:S(2)}, u32[]{:S(2)}) collective-permute-start(bf16[4,64,512]{2,1,0:T(8,128)(2,1)} %get-tuple-element.11), channel_id=1, source_target_pairs={{0,4},{4,8},{8,12},{12,16},{16,20},{20,24},{24,28},{28,32},{32,36}... | collective-permute-start | bytes 786440 | tf_op jit(solution)/shard_map/ppermute | solution.py:18
  105.4 5.8 %collective-permute-start.2 = (bf16[4,64,512]{2,1,0:T(8,128)(2,1)}, bf16[4,64,512]{2,1,0:T(8,128)(2,1)}, u32[]{:S(2)}, u32[]{:S(2)}) collective-permute-start(bf16[4,64,512]{2,1,0:T(8,128)(2,1)} %get-tuple-element.13), channel_id=1, source_target_pairs={{4,0},{8,4},{12,8},{16,12},{20,16},{24,20},{28,24},{32,28},{36,32}... | collective-permute-start | bytes 786440 | tf_op jit(solution)/shard_map/ppermute | solution.py:18
  112.3 1.1 copy-done.26
  113.4 6.9 %shard_map.282.pre_ref = f32[2560,512]{1,0:T(8,128)} custom-call(s32[20,128]{1,0:T(8,128)S(1)} %bitcast.40, s32[20,128]{1,0:T(8,128)S(1)} %bitcast.42, bf16[2560,512]{1,0:T(8,128)(2,1)S(1)} %copy-done, bf16[512,512]{1,0:T(8,128)(2,1)S(1)} %copy-done.9, bf16[640,512]{1,0:T(8,128)(2,1)S(1)} %copy-done.26), custom_call_target="tpu_custom_call" | custom-call | flops 3355443200 | bytes 8388608 | tf_op jit(solution)/shard_map/pallas_call | solution.py:474
  121.3 1.1 reshape.78.far_ref
  124.4 1.0 copy-done.12
  127.5 12.8 %shard_map.283 = bf16[320,512]{1,0:T(8,128)(2,1)} custom-call(s32[20,128]{1,0:T(8,128)S(1)} %bitcast.41, s32[20,128]{1,0:T(8,128)S(1)} %bitcast.43, bf16[2560,512]{1,0:T(8,128)(2,1)S(1)} %copy-done, f32[2560,512]{1,0:T(8,128)} %shard_map.282.pre_ref, bf16[256,512]{1,0:T(8,128)(2,1)} %bitcast.17.near0_ref, bf16[256,512]{1,0:T(8,128)(2,1)S(1)} %bitcast.34, ...), custom_call_target="tpu_custom_call" | custom-call | flops 5368709120 | bytes 12582912 | tf_op jit(solution)/shard_map/pallas_call | solution.py:481
  (69 shorter events, 17.7 us)
Async XLA Ops:
  2.2 33.1 %copy-start.1 = (bf16[512,512]{1,0:T(8,128)(2,1)S(1)}, bf16[512,512]{1,0:T(8,128)(2,1)}, u32[]{:S(2)}) copy-start(bf16[512,512]{1,0:T(8,128)(2,1)} %enc_out_ref.1) | copy-start | bytes 1572868
  2.2 33.0 %copy-start.2 = (bf16[512,512]{1,0:T(8,128)(2,1)S(1)}, bf16[512,512]{1,0:T(8,128)(2,1)}, u32[]{:S(2)}) copy-start(bf16[512,512]{1,0:T(8,128)(2,1)} %send_proj_ref.1) | copy-start | bytes 1572868
  2.2 33.0 %copy-start.3 = (bf16[512,512]{1,0:T(8,128)(2,1)S(1)}, bf16[512,512]{1,0:T(8,128)(2,1)}, u32[]{:S(2)}) copy-start(bf16[512,512]{1,0:T(8,128)(2,1)} %recv_proj_ref.1) | copy-start | bytes 1572868
  2.2 33.0 %copy-start.4 = (bf16[512,512]{1,0:T(8,128)(2,1)S(1)}, bf16[512,512]{1,0:T(8,128)(2,1)}, u32[]{:S(2)}) copy-start(bf16[512,512]{1,0:T(8,128)(2,1)} %msg_ref.1) | copy-start | bytes 1572868
  2.2 33.0 %copy-start.14 = (bf16[320,512]{1,0:T(8,128)(2,1)S(1)}, bf16[320,512]{1,0:T(8,128)(2,1)}, u32[]{:S(2)}) copy-start(bf16[320,512]{1,0:T(8,128)(2,1)} %embed_ref.1) | copy-start | bytes 983044
  2.2 33.0 %copy-start.18 = (bf16[4,8192]{1,0:T(4,128)(2,1)S(1)}, bf16[4,8192]{1,0:T(4,128)(2,1)}, u32[]{:S(2)}) copy-start(bf16[4,8192]{1,0:T(4,128)(2,1)} %geo_ref.1) | copy-start | bytes 196612
  2.2 33.0 %copy-start.23 = (bf16[4,512]{1,0:T(4,128)(2,1)S(1)}, bf16[4,512]{1,0:T(4,128)(2,1)}, u32[]{:S(2)}) copy-start(bf16[4,512]{1,0:T(4,128)(2,1)} %geo_proj_ref.1) | copy-start | bytes 12292
  2.2 33.0 %copy-start.24 = (f32[512]{0:T(512)S(1)}, f32[512]{0:T(512)}, u32[]{:S(2)}) copy-start(f32[512]{0:T(512)} %param.51) | copy-start | bytes 6148
  22.7 10.5 %collective-permute-start.1 = (bf16[4,128,256]{2,1,0:T(8,128)(2,1)}, bf16[4,128,256]{2,1,0:T(8,128)(2,1)S(1)}, u32[]{:S(2)}, u32[]{:S(2)}) collective-permute-start(bf16[4,128,256]{2,1,0:T(8,128)(2,1)} %get-tuple-element.14), channel_id=1, source_target_pairs={{0,4},{4,8},{8,12},{12,16},{16,20},{20,24},{24,28},{28,32},{32,36}... | collective-permute-start | bytes 786440 | tf_op jit(solution)/shard_map/ppermute | solution.py:18
  24.6 9.9 %collective-permute-start = (bf16[4,128,256]{2,1,0:T(8,128)(2,1)}, bf16[4,128,256]{2,1,0:T(8,128)(2,1)S(1)}, u32[]{:S(2)}, u32[]{:S(2)}) collective-permute-start(bf16[4,128,256]{2,1,0:T(8,128)(2,1)} %get-tuple-element.16), channel_id=1, source_target_pairs={{4,0},{8,4},{12,8},{16,12},{20,16},{24,20},{28,24},{32,28},{36,32}... | collective-permute-start | bytes 786440 | tf_op jit(solution)/shard_map/ppermute | solution.py:18
  35.3 1.0 copy-start.5
  36.3 1.0 copy-start.6
  59.5 51.8 %copy-start = (bf16[2560,512]{1,0:T(8,128)(2,1)S(1)}, bf16[2560,512]{1,0:T(8,128)(2,1)}, u32[]{:S(2)}) copy-start(bf16[2560,512]{1,0:T(8,128)(2,1)} %lat_ref.3) | copy-start | bytes 7864324
  59.5 51.8 %copy-start.21 = (s32[2560]{0:T(1024)S(1)}, s32[2560]{0:T(1024)}, u32[]{:S(2)}) copy-start(s32[2560]{0:T(1024)} %param.39) | copy-start | bytes 30724
  59.5 51.8 %copy-start.22 = (s32[2560]{0:T(1024)S(1)}, s32[2560]{0:T(1024)}, u32[]{:S(2)}) copy-start(s32[2560]{0:T(1024)} %param.40) | copy-start | bytes 30724
  61.3 11.5 %all-to-all-start.2 = ((bf16[4,64,512]{2,1,0:T(8,128)(2,1)}), bf16[4,64,512]{2,1,0:T(8,128)(2,1)S(1)}, u32[]{:S(2)}, u32[]{:S(2)}) async-start(bf16[4,64,512]{2,1,0:T(8,128)(2,1)} %bitcast.21), calls=%async_computation.2 | async-start | bytes 524288 | tf_op jit(solution)/shard_map/all_to_all | solution.py:464
  72.8 17.1 %all-to-all-start.1 = ((bf16[4,192,512]{2,1,0:T(8,128)(2,1)}), bf16[4,192,512]{2,1,0:T(8,128)(2,1)}, u32[]{:S(2)}, u32[]{:S(2)}) async-start(bf16[4,192,512]{2,1,0:T(8,128)(2,1)} %bitcast.14), calls=%async_computation.1 | async-start | bytes 1572864 | tf_op jit(solution)/shard_map/all_to_all | solution.py:457
  89.9 30.5 %all-to-all-start.3 = ((bf16[32,4,2,512]{3,1,2,0:T(4,128)(2,1)}), bf16[32,4,2,512]{3,1,2,0:T(4,128)(2,1)S(1)}, u32[]{:S(2)}, u32[]{:S(2)}) async-start(bf16[32,4,2,512]{3,1,2,0:T(4,128)(2,1)} %bitcast.23), calls=%async_computation.3 | async-start | bytes 524288 | tf_op jit(solution)/shard_map/all_to_all | solution.py:465
  103.4 18.9 %collective-permute-start.3 = (bf16[4,64,512]{2,1,0:T(8,128)(2,1)}, bf16[4,64,512]{2,1,0:T(8,128)(2,1)S(1)}, u32[]{:S(2)}, u32[]{:S(2)}) collective-permute-start(bf16[4,64,512]{2,1,0:T(8,128)(2,1)} %get-tuple-element.11), channel_id=1, source_target_pairs={{0,4},{4,8},{8,12},{12,16},{16,20},{20,24},{24,28},{28,32},{32,36}... | collective-permute-start | bytes 786440 | tf_op jit(solution)/shard_map/ppermute | solution.py:18
  105.4 16.9 %collective-permute-start.2 = (bf16[4,64,512]{2,1,0:T(8,128)(2,1)}, bf16[4,64,512]{2,1,0:T(8,128)(2,1)}, u32[]{:S(2)}, u32[]{:S(2)}) collective-permute-start(bf16[4,64,512]{2,1,0:T(8,128)(2,1)} %get-tuple-element.13), channel_id=1, source_target_pairs={{4,0},{8,4},{12,8},{16,12},{20,16},{24,20},{28,24},{32,28},{36,32}... | collective-permute-start | bytes 786440 | tf_op jit(solution)/shard_map/ppermute | solution.py:18
  111.3 1.0 copy-start.9
  112.3 1.1 copy-start.26
  113.4 8.9 %copy-start.25 = (f32[512]{0:T(512)S(1)}, f32[512]{0:T(512)}, u32[]{:S(2)}) copy-start(f32[512]{0:T(512)} %param.59) | copy-start | bytes 6148
  122.4 1.0 copy-start.10
  (12 other events, 11.0 us)

commit v2 on v1

--- a/solution.py
+++ b/solution.py
@@ -9,13 +9,35 @@
 
 LANES = 128
 EDGE_BLOCK = 512
-VMEM_BYTES = 48 * 1024 * 1024
-
-
-def shifted(value, steps):
+VMEM_BYTES = 28 * 1024 * 1024
+
+
+def sub_swap(value, step):
+    count = lax.axis_size("sub")
+    return lax.ppermute(value, "sub", [(t, t ^ step) for t in range(count)])
+
+
+def mate(band):
+    return band ^ 1
+
+
+def cross(band, count):
+    return (((band + 1) ^ 1) - 1) % count
+
+
+def band_swap(value, partner):
     count = lax.axis_size("band")
-    first, last = (max(0, -steps), min(count, count - steps))
-    return lax.ppermute(value, "band", [(source, source + steps) for source in range(first, last)])
+    return lax.ppermute(value, "band", [(b, partner(b)) for b in range(count)])
+
+
+def offsets():
+    even = lax.rem(lax.axis_index("band"), 2) == 0
+    return (1, jnp.where(even, 2, 0), jnp.where(even, 0, 2))
+
+
+def sources():
+    even = lax.rem(lax.axis_index("band"), 2) == 0
+    return (1, jnp.where(even, 0, 2), jnp.where(even, 2, 0))
 
 
 def layer_norm(values):
@@ -65,12 +87,16 @@
     return half(jnp.where(sub == jnp.broadcast_to(row, shape), 1.0, 0.0))
 
 
-def whole(*shape):
+def whole():
     return pl.BlockSpec(memory_space=pltpu.VMEM)
 
 
 def in_smem():
     return pl.BlockSpec(memory_space=pltpu.SMEM)
+
+
+def in_hbm():
+    return pl.BlockSpec(memory_space=pltpu.HBM)
 
 
 def local_call(kernel, out_shape, in_specs, scratch=(), flops=0, nbytes=0):
@@ -85,27 +111,52 @@
     )
 
 
-def pick_grid_kernel(send_ref, grid_ref, out_ref):
-    rows, width = grid_ref.shape
-    slots = send_ref.shape[0]
-    out_ref[...] = jnp.zeros_like(out_ref)
-
-    def step(k, carry):
-        onehot = picks(columns(send_ref, 2 * k, 2), rows)
-        out_ref[pl.ds(pl.multiple_of(2 * k * LANES, 2 * LANES), 2 * LANES), 0:width] = half(
-            dot(onehot, grid_ref[...])
-        )
-        return carry
-
-    lax.fori_loop(0, slots // 2, step, 0)
+class Fetch:
+    def __init__(self, refs, slots, sems):
+        self.copies = [
+            pltpu.make_async_copy(ref, slots.at[k], sems.at[k]) for k, ref in enumerate(refs)
+        ]
+        self.slots, self.ready = slots, set()
+        for copy in self.copies:
+            copy.start()
+
+    def __call__(self, k):
+        if k not in self.ready:
+            self.copies[k].wait()
+            self.ready.add(k)
+        return self.slots[k]
+
+
+def pick_grid_kernel(send_ref, grid_ref, *out_refs):
+    width, rows = grid_ref.shape
+    wide = out_refs[0].shape[-1]
+    me = lax.axis_index("sub")
+    index = jnp.concatenate(
+        [
+            send_ref[offset, pl.ds(me ^ k, 1), :]
+            for k in range(len(out_refs))
+            for offset in offsets()
+        ],
+        axis=1,
+    )
+    for k, out_ref in enumerate(out_refs):
+        three = index[:, 3 * LANES * k : 3 * LANES * (k + 1)]
+        columns_of = dot(grid_ref[...], scatter_picks(three, rows))
+        padded = jnp.concatenate(
+            [columns_of, jnp.zeros((wide - width, 3 * LANES), jnp.float32)], axis=0
+        )
+        for w in range(3):
+            out_ref[w] = half(padded[:, w * LANES : (w + 1) * LANES].T)
 
 
 def encoder_kernel(
-    place_ref,
     live_ref,
-    first_ref,
-    second_ref,
-    third_ref,
+    own0_ref,
+    own1_ref,
+    own2_ref,
+    own3_ref,
+    mate_ref,
+    cross_ref,
     src_ref,
     dst_ref,
     geo_ref,
@@ -113,36 +164,81 @@
     near_ref,
     far_ref,
     enc_in_ref,
+    geo_proj_ref,
+    gain_ref,
     enc_out_ref,
     send_proj_ref,
     recv_proj_ref,
-    geo_proj_ref,
     msg_ref,
     node_self_ref,
     node_agg_ref,
     node_out_ref,
-    gain_ref,
     proc_send_ref,
     proc_recv_ref,
     latent_ref,
     pair_ref,
-    out_ref,
+    out0_ref,
+    out1_ref,
+    out2_ref,
+    out3_ref,
+    out_far_ref,
     table_ref,
     enc_ref,
     sum_ref,
+    flat_ref,
+    slots_ref,
+    sems,
 ):
+    weight = Fetch(
+        (
+            enc_out_ref,
+            send_proj_ref,
+            recv_proj_ref,
+            msg_ref,
+            node_self_ref,
+            node_agg_ref,
+            node_out_ref,
+            proc_send_ref,
+            proc_recv_ref,
+        ),
+        slots_ref,
+        sems,
+    )
     mesh_rows, latent = embed_ref.shape
-    chunk = first_ref.shape[0]
+    subs, cap, wide = mate_ref.shape
+    chunk = subs * cap
     base = table_ref.shape[0] - 3 * chunk
     geo_rows = geo_ref.shape[0]
-    is_first = place_ref[0] == 0
-    is_last = place_ref[0] == place_ref[1] - 1
+    band, me = lax.axis_index("band"), lax.axis_index("sub")
+    is_first = band == 0
+    is_last = band == lax.axis_size("band") - 1
     polar = is_first | is_last
     live = live_ref[0]
 
     enc_ref[...] = jnp.zeros_like(enc_ref)
     enc_ref[0 : enc_in_ref.shape[0], :] = enc_in_ref[...]
-    table_ref[0:mesh_rows, :] = half(dot(embed_ref[...], recv_proj_ref[...]))
+
+    start = jnp.where(is_last, base - chunk, base)
+    places = sources()
+
+    def encode(rows, w):
+        hidden = half(silu(dot(rows, enc_ref[...])))
+        lat = half(layer_norm(dot(hidden, weight(0))))
+        sent = half(dot(lat, weight(1)))
+        for k in range(subs):
+            place = pl.multiple_of(start + places[w] * chunk + (me ^ k) * cap, cap)
+            table_ref[pl.ds(place, cap), :] = sent[k * cap : (k + 1) * cap]
+
+    encode(
+        jnp.concatenate([ref[0] for ref in (own0_ref, own1_ref, own2_ref, own3_ref)], axis=0), 0
+    )
+    encode(mate_ref[...].reshape(chunk, wide), 1)
+
+    @pl.when(jnp.logical_not(polar))
+    def _():
+        encode(cross_ref[...].reshape(chunk, wide), 2)
+
+    table_ref[0:mesh_rows, :] = half(dot(embed_ref[...], weight(2)))
     table_ref[mesh_rows:base, :] = jnp.concatenate(
         [
             geo_proj_ref[...].astype(jnp.float32),
@@ -150,23 +246,6 @@
         ],
         axis=0,
     ).astype(jnp.bfloat16)
-
-    def encode(rows_ref, place):
-        hidden = half(silu(dot(rows_ref[...], enc_ref[...])))
-        lat = half(layer_norm(dot(hidden, enc_out_ref[...])))
-        table_ref[pl.ds(place, chunk), :] = half(dot(lat, send_proj_ref[...]))
-
-    start = jnp.where(is_last, base - chunk, base)
-
-    @pl.when(jnp.logical_not(is_last))
-    def _():
-        encode(first_ref, base)
-
-    encode(second_ref, pl.multiple_of(start + chunk, chunk))
-
-    @pl.when(jnp.logical_not(is_first))
-    def _():
-        encode(third_ref, pl.multiple_of(start + 2 * chunk, chunk))
 
     sum_ref[...] = jnp.zeros_like(sum_ref)
     per = EDGE_BLOCK // LANES
@@ -238,29 +317,43 @@
     total = sum_ref[...]
     high = half(total)
     low = half(total - high.astype(jnp.float32))
-    inflow = half(dot(high, msg_ref[...]) + dot(low, msg_ref[...]))
+    inflow = half(dot(high, weight(3)) + dot(low, weight(3)))
     embed = embed_ref[...]
-    node_act = half(silu(dot(embed, node_self_ref[...]) + dot(inflow, node_agg_ref[...])))
+    node_act = half(silu(dot(embed, weight(4)) + dot(inflow, weight(5))))
     mesh_latent = half(
-        embed.astype(jnp.float32) + layer_norm(dot(node_act, node_out_ref[...])) * gain_ref[...]
+        embed.astype(jnp.float32) + layer_norm(dot(node_act, weight(6))) * gain_ref[...]
     )
     latent_ref[...] = mesh_latent
-    sender = half(dot(mesh_latent, proc_send_ref[...]))
+    sender = half(dot(mesh_latent, weight(7)))
     pair_ref[0:mesh_rows, :] = sender
-    pair_ref[mesh_rows : 2 * mesh_rows, :] = half(dot(mesh_latent, proc_recv_ref[...]))
+    pair_ref[mesh_rows : 2 * mesh_rows, :] = half(dot(mesh_latent, weight(8)))
     padded = -(-mesh_rows // LANES) * LANES
     sender_pad = jnp.concatenate(
         [sender, jnp.zeros((padded - mesh_rows, latent), jnp.bfloat16)], axis=0
     )
-    near_slots = near_ref.shape[0]
-    for k in range(near_slots):
-        out_ref[k * LANES : (k + 1) * LANES, :] = half(
-            dot(picks(column(near_ref[k : k + 1, :]), padded), sender_pad)
-        )
-    for k in range(far_ref.shape[0]):
-        out_ref[(near_slots + k) * LANES : (near_slots + k + 1) * LANES, :] = half(
-            dot(picks(column(far_ref[k : k + 1, :]), padded), sender_pad)
-        )
+    near = near_ref.shape[2]
+    shares = offsets()
+    for k, out_ref in enumerate((out0_ref, out1_ref, out2_ref, out3_ref)):
+        index = [near_ref[offset, pl.ds(me ^ k, 1), :] for offset in shares]
+        index.append(jnp.zeros((1, 4 * near - 3 * near), jnp.int32))
+        index = jnp.concatenate(index, axis=1)
+        onehot = jnp.concatenate(
+            [
+                picks(column(index[:, first : first + LANES]), padded)
+                for first in range(0, 4 * near, LANES)
+            ],
+            axis=0,
+        )
+        out_ref[...] = half(dot(onehot[0 : 3 * near], sender_pad)).reshape(out_ref.shape)
+    lanes = latent // LANES
+    spread = far_ref.shape[0] * lanes
+    for c in range(far_ref.shape[0]):
+        rows = dot(picks(column(far_ref[c : c + 1, :]), padded), sender_pad)
+        for j in range(lanes):
+            flat_ref[pl.ds(c * lanes + j, LANES, stride=spread), :] = rows[
+                :, j * LANES : (j + 1) * LANES
+            ]
+    out_far_ref[...] = half(flat_ref[...])
 
 
 def edge_start_kernel(src_ref, dst_ref, lat_ref, self_ref, pair_ref, out_ref):
@@ -298,40 +391,68 @@
     dst_ref,
     lat_ref,
     pre_ref,
-    near0_ref,
-    near1_ref,
-    near2_ref,
+    own0_ref,
+    own1_ref,
+    own2_ref,
+    own3_ref,
+    mate_ref,
+    cross_ref,
     far_ref,
     latent_ref,
+    gain_ref,
     edge_out_ref,
     upd_self_ref,
     upd_agg_ref,
     upd_out_ref,
-    gain_ref,
     out_ref,
     table_ref,
     sum_ref,
+    flat_ref,
+    slots_ref,
+    sems,
 ):
-    mesh_rows = latent_ref.shape[0]
+    weight = Fetch((edge_out_ref, upd_self_ref, upd_agg_ref, upd_out_ref), slots_ref, sems)
+    mesh_rows, latent = latent_ref.shape
     block_rows = 512
     per = block_rows // LANES
-    near = near0_ref.shape[0]
-    table_ref[0:near, :] = near0_ref[...]
-    table_ref[near : 2 * near, :] = near1_ref[...]
-    table_ref[2 * near : 3 * near, :] = near2_ref[...]
-    table_ref[3 * near :, :] = far_ref[...]
+    subs, near, _ = mate_ref.shape
+    near_total = 3 * subs * near
+    me = lax.axis_index("sub")
+    owns = (own0_ref, own1_ref, own2_ref, own3_ref)
+    for w, offset in enumerate(sources()):
+        for k in range(subs):
+            rows = owns[k][0] if w == 0 else (mate_ref, cross_ref)[w - 1][k]
+            place = pl.multiple_of((offset * subs + (me ^ k)) * near, near)
+            table_ref[pl.ds(place, near), :] = rows
+    lanes = latent // LANES
+    devices = far_ref.shape[0] // (2 * lanes)
+    flat_ref[...] = far_ref[...].astype(jnp.float32)
+    for c in range(2):
+        table_ref[pl.ds(near_total + c * devices, devices), :] = half(
+            jnp.concatenate(
+                [
+                    flat_ref[pl.ds(c * lanes + j, devices, stride=2 * lanes), :]
+                    for j in range(lanes)
+                ],
+                axis=1,
+            )
+        )
+    edge_out = weight(0)
     sum_ref[...] = jnp.zeros_like(sum_ref)
 
     def step(block, carry):
         row0 = pl.multiple_of(block * block_rows, block_rows)
         source = columns(src_ref, block * per, per) - mesh_rows
+        far = source - near_total
+        far = near_total + (far & 1) * devices + (far >> 1)
+        source = jnp.where(source < near_total, source, far)
         pre = pre_ref[pl.ds(row0, block_rows), :] + dot(
             picks(source, table_ref.shape[0]), table_ref[...]
         )
         hidden = half(silu(pre))
         new = half(
             lat_ref[pl.ds(row0, block_rows), :].astype(jnp.float32)
-            + layer_norm(dot(hidden, edge_out_ref[...]))
+            + layer_norm(dot(hidden, edge_out))
         )
         sum_ref[...] += dot(scatter_picks(row_of(dst_ref, block * per, per), mesh_rows), new)
         return carry
@@ -339,9 +460,9 @@
     lax.fori_loop(0, lat_ref.shape[0] // block_rows, step, 0)
     inflow = half(sum_ref[...])
     latent = latent_ref[...]
-    act = half(silu(dot(latent, upd_self_ref[...]) + dot(inflow, upd_agg_ref[...])))
+    act = half(silu(dot(latent, weight(1)) + dot(inflow, weight(2))))
     out_ref[...] = half(
-        latent.astype(jnp.float32) + layer_norm(dot(act, upd_out_ref[...])) * gain_ref[...]
+        latent.astype(jnp.float32) + layer_norm(dot(act, weight(3))) * gain_ref[...]
     )
 
 
@@ -377,8 +498,8 @@
     upd_out,
     out_gain,
 ):
-    band_count = lax.axis_size("band")
     sub_count = lax.axis_size("sub")
+    devices = lax.axis_size("band") * sub_count
     slot_cap = grid_send.shape[2]
     near_cap = mesh_near_send.shape[2]
     far_cap = mesh_far_send.shape[1]
@@ -388,88 +509,78 @@
     wide = 256
     bf16, f32 = jnp.bfloat16, jnp.float32
 
+    def exchange(parts):
+        arrived = [parts[0]] + [sub_swap(parts[k], k) for k in range(1, sub_count)]
+        mates = band_swap(jnp.stack([part[1] for part in arrived]), mate)
+        crosses = band_swap(
+            jnp.stack([part[2] for part in arrived]),
+            functools.partial(cross, count=lax.axis_size("band")),
+        )
+        return *arrived, mates, crosses
+
     sent = 3 * sub_count * slot_cap
-    payload = local_call(
+    parts = local_call(
         pick_grid_kernel,
-        jax.ShapeDtypeStruct((sent, wide), bf16),
+        (jax.ShapeDtypeStruct((3, slot_cap, wide), bf16),) * sub_count,
         [whole()] * 2,
         flops=2 * sent * grid_input.shape[0] * wide,
         nbytes=2 * wide * (sent + grid_input.shape[0]),
-    )(grid_send.reshape(sent // LANES, LANES), grid_input)
-    in_sub = lax.all_to_all(
-        payload.reshape(3, sub_count, slot_cap, wide), "sub", split_axis=1, concat_axis=1, tiled=True
-    )
-    arrived = [
-        part.reshape(sub_count * slot_cap, wide)
-        for part in (shifted(in_sub[0], -1), in_sub[1], shifted(in_sub[2], 1))
-    ]
-
-    near_index = mesh_near_send.transpose(1, 0, 2).reshape(-1, LANES)
-    far_index = (
-        mesh_far_send.reshape(band_count, sub_count, far_cap).transpose(1, 0, 2).reshape(-1, LANES)
-    )
-    place = jnp.stack([lax.axis_index("band"), jnp.int32(band_count)]).astype(jnp.int32)
-    near_total = 3 * sub_count * near_cap
-    far_total = band_count * sub_count * far_cap
-    mesh_latent, pairs, outgoing = local_call(
+    )(grid_send, grid_input.T)
+    arrived = exchange(parts)
+
+    far_total = devices * far_cap
+    mesh_latent, pairs, *near_parts, far_out = local_call(
         encoder_kernel,
         (
             jax.ShapeDtypeStruct((mesh_rows, latent), bf16),
             jax.ShapeDtypeStruct((2 * mesh_rows, latent), bf16),
-            jax.ShapeDtypeStruct((near_total + far_total, latent), bf16),
-        ),
-        [in_smem()] * 2 + [whole()] * 21,
+        )
+        + (jax.ShapeDtypeStruct((3, near_cap, latent), bf16),) * sub_count
+        + (jax.ShapeDtypeStruct((far_total * latent // LANES, LANES), bf16),),
+        [in_smem()] + [whole()] * 15 + [in_hbm()] * 9,
         scratch=[
             pltpu.VMEM((512 + sent, latent), bf16),
             pltpu.VMEM((wide, latent), bf16),
             pltpu.VMEM((mesh_rows, latent), f32),
+            pltpu.VMEM((far_total * latent // LANES, LANES), f32),
+            pltpu.VMEM((9, latent, latent), bf16),
+            pltpu.SemaphoreType.DMA((9,)),
         ],
         flops=2 * edges * 2048 * latent,
         nbytes=16 << 20,
     )(
-        place,
         edge_count,
         *arrived,
         grid_edge_src.reshape(-1, LANES),
         grid_edge_dst.reshape(-1, LANES),
         grid_edge_geo,
         mesh_embed,
-        near_index,
-        far_index,
+        mesh_near_send,
+        mesh_far_send.T,
         enc_in,
+        geo_proj,
+        mesh_gain.reshape(1, latent),
         enc_out,
         send_proj,
         recv_proj,
-        geo_proj,
         msg_weight,
         node_self,
         node_agg,
         node_out,
-        mesh_gain.reshape(1, latent),
         proc_send,
         proc_recv,
     )
 
     mesh_src = mesh_edge_src.reshape(-1, LANES)
     mesh_dst = mesh_edge_dst.reshape(-1, LANES)
-    near_out = outgoing[:near_total].reshape(sub_count, 3 * near_cap, latent)
-    far_out = outgoing[near_total:].reshape(sub_count, band_count * far_cap, latent)
-    near_sub = lax.all_to_all(near_out, "sub", split_axis=0, concat_axis=0, tiled=True).reshape(
-        sub_count, 3, near_cap, latent
-    )
-    near_parts = [
-        part.reshape(sub_count * near_cap, latent)
-        for part in (shifted(near_sub[:, 0], -1), near_sub[:, 1], shifted(near_sub[:, 2], 1))
-    ]
-    far_sub = lax.all_to_all(far_out, "sub", split_axis=0, concat_axis=0, tiled=True)
-    far_band = lax.all_to_all(
-        far_sub.reshape(sub_count, band_count, far_cap, latent).transpose(1, 0, 2, 3),
-        "band",
+    near_arrived = exchange(near_parts)
+    far_rows = lax.all_to_all(
+        far_out.reshape(devices, -1, LANES),
+        ("band", "sub"),
         split_axis=0,
         concat_axis=0,
         tiled=True,
-    )
-    far_rows = far_band.reshape(far_total, latent)
+    ).reshape(-1, LANES)
 
     pre = local_call(
         edge_start_kernel,
@@ -478,13 +589,17 @@
         flops=2 * mesh_edges * 1280 * latent,
         nbytes=8 << 20,
     )(mesh_src, mesh_dst, mesh_edge_lat, edge_self, pairs)
+    near_total = 3 * sub_count * near_cap
     return local_call(
         edge_finish_kernel,
         jax.ShapeDtypeStruct((mesh_rows, latent), bf16),
-        [whole()] * 14,
+        [whole()] * 13 + [in_hbm()] * 4,
         scratch=[
             pltpu.VMEM((near_total + far_total, latent), bf16),
             pltpu.VMEM((mesh_rows, latent), f32),
+            pltpu.VMEM((far_total * latent // LANES, LANES), f32),
+            pltpu.VMEM((4, latent, latent), bf16),
+            pltpu.SemaphoreType.DMA((4,)),
         ],
         flops=2 * mesh_edges * 2048 * latent,
         nbytes=12 << 20,
@@ -493,14 +608,14 @@
         mesh_dst,
         mesh_edge_lat,
         pre,
-        *near_parts,
+        *near_arrived,
         far_rows,
         mesh_latent,
+        out_gain.reshape(1, latent),
         edge_out,
         upd_self,
         upd_agg,
         upd_out,
-        out_gain.reshape(1, latent),
     )
 
 

time: 141 us -> 108 us (0.77)
  the two profiles are of different devices: /device:TPU:6 before, /device:TPU:0 now
where the time goes in v2:
time: 108 us
  Pallas kernels  47.9 us (44%)
  starting transfers between devices  27.2 us (25%)
  local copies, waits for them, and re-layouts  15 us (14%)
  waiting for transfers between devices  14.8 us (14%)
  other arithmetic  1.57 us (1%)
  between operations  1.31 us (1%)
    pallas_call x1, Pallas kernels, body(): local_call(encoder_kernel, (jax.ShapeDtypeStruct((mesh_rows, latent), bf1...  29.2 us
    unnamed x72, local copies, waits for them, and re-layouts  14.9 us
    pallas_call x1, Pallas kernels, body(): local_call(edge_finish_kernel, jax.ShapeDtypeStruct((mesh_rows, latent),...  11.7 us
    ppermute x4, starting transfers between devices, band_swap(): return lax.ppermute(value, 'band', [(b, partner(b)) for b in range(count)])  11.6 us
    ppermute x6, waiting for transfers between devices, sub_swap(): return lax.ppermute(value, 'sub', [(t, t ^ step) for t in range(count)])  11.4 us
    ppermute x6, starting transfers between devices, sub_swap(): return lax.ppermute(value, 'sub', [(t, t ^ step) for t in range(count)])  9.48 us
    all_to_all x1, starting transfers between devices, body(): lax.all_to_all(far_out.reshape(devices, -1, LANES), ('band', 'sub'), spli...  6.16 us
    pallas_call x1, Pallas kernels, body(): local_call(edge_start_kernel, jax.ShapeDtypeStruct((mesh_edges, latent),...  4.63 us
  transfers between devices with their start and end apart: 11, of which 2 were waited for; matrix products, arithmetic and copies ran while one was open for 1% of the time, Pallas kernels for 4%

profile of v2, /device:TPU:0, one launch (start us, length us, event | category | flops | bytes accessed | tf_op | source)
XLA Modules:
  0.0 107.8 jit_solution(14290079906121772813)
XLA Ops:
  0.0 1.2 %copy-done.2 = bf16[2048,227]{0,1:T(8,128)(2,1)S(1)} copy-done((bf16[2048,227]{0,1:T(8,128)(2,1)S(1)}, bf16[2048,227]{0,1:T(8,128)(2,1)}, u32[]{:S(2)}) %copy-start.2) | copy-done | bytes 929816
  2.0 2.4 %shard_map.280 = (bf16[3,128,256]{2,1,0:T(8,128)(2,1)S(1)}, bf16[3,128,256]{2,1,0:T(8,128)(2,1)S(1)}, bf16[3,128,256]{2,1,0:T(8,128)(2,1)S(1)}, bf16[3,128,256]{2,1,0:T(8,128)(2,1)S(1)}) custom-call(s32[3,4,128]{2,1,0:T(4,128)S(1)} %copy-done.24, bf16[227,2048]{1,0:T(8,128)(2,1)S(1)} %bitcast.11), custom_call_target="tpu_custom_call" | custom-call | flops 1610612736 | bytes 1835008 | tf_op jit(solution)/shard_map/pallas_call | solution.py:522
  4.4 1.7 %collective-permute-start = (bf16[3,128,256]{2,1,0:T(8,128)(2,1)S(1)}, bf16[3,128,256]{2,1,0:T(8,128)(2,1)S(1)}, u32[]{:S(2)}, u32[]{:S(2)}) collective-permute-start(bf16[3,128,256]{2,1,0:T(8,128)(2,1)S(1)} %get-tuple-element.17), channel_id=1, source_target_pairs={{0,1},{1,0},{2,3},{3,2},{4,5},{5,4},{6,7},{7,6},{8,9},{9,8},{10,11... | collective-permute-start | bytes 589832 | tf_op jit(solution)/shard_map/ppermute | solution.py:17
  6.2 2.9 %collective-permute-start.1 = (bf16[3,128,256]{2,1,0:T(8,128)(2,1)S(1)}, bf16[3,128,256]{2,1,0:T(8,128)(2,1)S(1)}, u32[]{:S(2)}, u32[]{:S(2)}) collective-permute-start(bf16[3,128,256]{2,1,0:T(8,128)(2,1)S(1)} %get-tuple-element.18), channel_id=1, source_target_pairs={{0,2},{1,3},{2,0},{3,1},{4,6},{5,7},{6,4},{7,5},{8,10},{9,11},{10,... | collective-permute-start | bytes 589832 | tf_op jit(solution)/shard_map/ppermute | solution.py:17
  9.2 11.4 %collective-permute-done.2.own3_ref = bf16[3,128,256]{2,1,0:T(8,128)(2,1)S(1)} collective-permute-done((bf16[3,128,256]{2,1,0:T(8,128)(2,1)S(1)}, bf16[3,128,256]{2,1,0:T(8,128)(2,1)S(1)}, u32[]{:S(2)}, u32[]{:S(2)}) %collective-permute-start.2) | collective-permute-done | bytes 196640 | tf_op jit(solution)/shard_map/ppermute | solution.py:17
  20.8 6.4 %collective-permute-start.4 = (bf16[4,128,256]{2,1,0:T(8,128)(2,1)S(1)}, bf16[4,128,256]{2,1,0:T(8,128)(2,1)S(1)}, u32[]{:S(2)}, u32[]{:S(2)}) collective-permute-start(bf16[4,128,256]{2,1,0:T(8,128)(2,1)S(1)} %pad_maximum_fusion.1), channel_id=1, source_target_pairs={{0,124},{4,8},{8,4},{12,16},{16,12},{20,24},{24,20},{28,32},{32,28... | collective-permute-start | bytes 786440 | tf_op jit(solution)/shard_map/ppermute | solution.py:30
  27.9 3.4 %collective-permute-done.4.cross_ref = bf16[4,128,256]{2,1,0:T(8,128)(2,1)S(1)} collective-permute-done((bf16[4,128,256]{2,1,0:T(8,128)(2,1)S(1)}, bf16[4,128,256]{2,1,0:T(8,128)(2,1)S(1)}, u32[]{:S(2)}, u32[]{:S(2)}) %collective-permute-start.4) | collective-permute-done | bytes 262176 | tf_op jit(solution)/shard_map/ppermute | solution.py:30
  31.5 29.2 %shard_map.281 = (bf16[320,512]{1,0:T(8,128)(2,1)S(1)}, bf16[640,512]{1,0:T(8,128)(2,1)S(1)}, bf16[3,64,512]{2,1,0:T(8,128)(2,1)S(1)}, bf16[3,64,512]{2,1,0:T(8,...) custom-call(s32[1]{0:T(128)S(6)} %copy.31.live_ref, ...), custom_call_target="tpu_custom_call" | custom-call | flops 17179869184 | bytes 16777216 | tf_op jit(solution)/shard_map/pallas_call | solution.py:532
  60.7 0.8 copy-done.32
  62.2 1.7 %collective-permute-start.6 = (bf16[3,64,512]{2,1,0:T(8,128)(2,1)S(1)}, bf16[3,64,512]{2,1,0:T(8,128)(2,1)S(1)}, u32[]{:S(2)}, u32[]{:S(2)}) collective-permute-start(bf16[3,64,512]{2,1,0:T(8,128)(2,1)S(1)} %get-tuple-element.23), channel_id=1, source_target_pairs={{0,2},{1,3},{2,0},{3,1},{4,6},{5,7},{6,4},{7,5},{8,10},{9,11},{10,... | collective-permute-start | bytes 589832 | tf_op jit(solution)/shard_map/ppermute | solution.py:17
  64.0 2.9 %collective-permute-start.7 = (bf16[3,64,512]{2,1,0:T(8,128)(2,1)S(1)}, bf16[3,64,512]{2,1,0:T(8,128)(2,1)S(1)}, u32[]{:S(2)}, u32[]{:S(2)}) collective-permute-start(bf16[3,64,512]{2,1,0:T(8,128)(2,1)S(1)} %get-tuple-element.24), channel_id=1, source_target_pairs={{0,3},{1,2},{2,1},{3,0},{4,7},{5,6},{6,5},{7,4},{8,11},{9,10},{10,... | collective-permute-start | bytes 589832 | tf_op jit(solution)/shard_map/ppermute | solution.py:17
  66.9 6.2 %all-to-all-start = ((bf16[128,8,128]{2,1,0:T(8,128)(2,1)}), bf16[128,8,128]{2,1,0:T(8,128)(2,1)S(1)}, u32[]{:S(2)}, u32[]{:S(2)}) async-start(bf16[128,8,128]{2,1,0:T(8,128)(2,1)} %bitcast.7), calls=%async_computation | async-start | bytes 524288 | tf_op jit(solution)/shard_map/all_to_all | solution.py:577
  73.2 0.8 pad_maximum_fusion.2
  74.0 0.7 pad_maximum_fusion.3
  74.7 5.1 %collective-permute-start.9 = (bf16[4,64,512]{2,1,0:T(8,128)(2,1)}, bf16[4,64,512]{2,1,0:T(8,128)(2,1)}, u32[]{:S(2)}, u32[]{:S(2)}) collective-permute-start(bf16[4,64,512]{2,1,0:T(8,128)(2,1)} %pad_maximum_fusion.3), channel_id=1, source_target_pairs={{0,124},{4,8},{8,4},{12,16},{16,12},{20,24},{24,20},{28,32},{32,28... | collective-permute-start | bytes 786440 | tf_op jit(solution)/shard_map/ppermute | solution.py:30
  79.8 1.7 %copy-done = bf16[2560,512]{1,0:T(8,128)(2,1)S(1)} copy-done((bf16[2560,512]{1,0:T(8,128)(2,1)S(1)}, bf16[2560,512]{1,0:T(8,128)(2,1)}, u32[]{:S(2)}) %copy-start) | copy-done | bytes 2621464
  81.5 1.1 %copy-done.33 = bf16[640,512]{1,0:T(8,128)(2,1)S(1)} copy-done((bf16[640,512]{1,0:T(8,128)(2,1)S(1)}, bf16[640,512]{1,0:T(8,128)(2,1)}, u32[]{:S(2)}) %copy-start.33) | copy-done | bytes 655384
  82.6 4.6 %shard_map.282.pre_ref = f32[2560,512]{1,0:T(8,128)S(1)} custom-call(s32[20,128]{1,0:T(8,128)S(1)} %bitcast.14, s32[20,128]{1,0:T(8,128)S(1)} %bitcast.16, bf16[2560,512]{1,0:T(8,128)(2,1)S(1)} %copy-done, bf16[512,512]{1,0:T(8,128)(2,1)S(1)} %copy-done.12, bf16[640,512]{1,0:T(8,128)(2,1)S(1)} %copy-done.33), custom_call_target="tpu_custom_call" | custom-call | flops 3355443200 | bytes 8388608 | tf_op jit(solution)/shard_map/pallas_call | solution.py:585
  87.3 2.3 %copy-done.30 = f32[2560,512]{1,0:T(8,128)} copy-done((f32[2560,512]{1,0:T(8,128)}, f32[2560,512]{1,0:T(8,128)S(1)}, u32[]{:S(2)}) %copy-start.30) | copy-done | bytes 5242904
  89.7 1.7 %copy-done.1 = bf16[2560,512]{1,0:T(8,128)(2,1)S(1)} copy-done((bf16[2560,512]{1,0:T(8,128)(2,1)S(1)}, bf16[2560,512]{1,0:T(8,128)(2,1)}, u32[]{:S(2)}) %copy-start.1) | copy-done | bytes 2621464
  91.4 1.0 copy-done.16
  92.4 2.5 %copy-done.31 = f32[2560,512]{1,0:T(8,128)S(1)} copy-done((f32[2560,512]{1,0:T(8,128)S(1)}, f32[2560,512]{1,0:T(8,128)}, u32[]{:S(2)}) %copy-start.31) | copy-done | bytes 5242904
  94.9 1.0 copy-done.35
  95.9 11.7 %shard_map.283 = bf16[320,512]{1,0:T(8,128)(2,1)} custom-call(s32[20,128]{1,0:T(8,128)S(1)} %bitcast.15, s32[20,128]{1,0:T(8,128)S(1)} %bitcast.17, bf16[2560,512]{1,0:T(8,128)(2,1)S(1)} %copy-done.1, f32[2560,512]{1,0:T(8,128)S(1)} %copy-done.31, bf16[3,64,512]{2,1,0:T(8,128)(2,1)S(1)} %get-tuple-element.21.own0_ref, ...), custom_call_target="tpu_custom_call" | custom-call | flops 5368709120 | bytes 12582912 | tf_op jit(solution)/shard_map/pallas_call | solution.py:593
  (86 shorter events, 1.9 us)
Async XLA Ops:
  0.0 31.3 %copy-start.29 = (s32[128,2]{0,1:T(2,128)S(1)}, s32[128,2]{0,1:T(2,128)}, u32[]{:S(2)}) copy-start(s32[128,2]{0,1:T(2,128)} %param.38) | copy-start | bytes 3076
  1.9 29.4 %copy-start.7 = (bf16[512,512]{1,0:T(8,128)(2,1)S(1)}, bf16[512,512]{1,0:T(8,128)(2,1)}, u32[]{:S(2)}) copy-start(bf16[512,512]{1,0:T(8,128)(2,1)} %node_self_ref.1) | copy-start | bytes 1572868
  1.9 29.4 %copy-start.8 = (bf16[512,512]{1,0:T(8,128)(2,1)S(1)}, bf16[512,512]{1,0:T(8,128)(2,1)}, u32[]{:S(2)}) copy-start(bf16[512,512]{1,0:T(8,128)(2,1)} %node_agg_ref.1) | copy-start | bytes 1572868
  1.9 29.4 %copy-start.9 = (bf16[512,512]{1,0:T(8,128)(2,1)S(1)}, bf16[512,512]{1,0:T(8,128)(2,1)}, u32[]{:S(2)}) copy-start(bf16[512,512]{1,0:T(8,128)(2,1)} %node_out_ref.1) | copy-start | bytes 1572868
  1.9 29.4 %copy-start.10 = (bf16[512,512]{1,0:T(8,128)(2,1)S(1)}, bf16[512,512]{1,0:T(8,128)(2,1)}, u32[]{:S(2)}) copy-start(bf16[512,512]{1,0:T(8,128)(2,1)} %proc_send_ref.1) | copy-start | bytes 1572868
  2.0 29.4 %copy-start.11 = (bf16[512,512]{1,0:T(8,128)(2,1)S(1)}, bf16[512,512]{1,0:T(8,128)(2,1)}, u32[]{:S(2)}) copy-start(bf16[512,512]{1,0:T(8,128)(2,1)} %proc_recv_ref.1) | copy-start | bytes 1572868
  2.0 29.4 %copy-start.17 = (bf16[320,512]{1,0:T(8,128)(2,1)S(1)}, bf16[320,512]{1,0:T(8,128)(2,1)}, u32[]{:S(2)}) copy-start(bf16[320,512]{1,0:T(8,128)(2,1)} %embed_ref.1) | copy-start | bytes 983044
  2.0 29.4 %copy-start.18 = (bf16[227,512]{1,0:T(8,128)(2,1)S(1)}, bf16[227,512]{1,0:T(8,128)(2,1)}, u32[]{:S(2)}) copy-start(bf16[227,512]{1,0:T(8,128)(2,1)} %enc_in_ref.1) | copy-start | bytes 697348
  2.0 29.4 %copy-start.19 = (bf16[4,8192]{1,0:T(4,128)(2,1)S(1)}, bf16[4,8192]{1,0:T(4,128)(2,1)}, u32[]{:S(2)}) copy-start(bf16[4,8192]{1,0:T(4,128)(2,1)} %geo_ref.1) | copy-start | bytes 196612
  2.0 29.4 %copy-start.20 = (s32[8192]{0:T(1024)S(1)}, s32[8192]{0:T(1024)}, u32[]{:S(2)}) copy-start(s32[8192]{0:T(1024)} %param.32) | copy-start | bytes 98308
  4.4 16.2 %collective-permute-start = (bf16[3,128,256]{2,1,0:T(8,128)(2,1)S(1)}, bf16[3,128,256]{2,1,0:T(8,128)(2,1)S(1)}, u32[]{:S(2)}, u32[]{:S(2)}) collective-permute-start(bf16[3,128,256]{2,1,0:T(8,128)(2,1)S(1)} %get-tuple-element.17), channel_id=1, source_target_pairs={{0,1},{1,0},{2,3},{3,2},{4,5},{5,4},{6,7},{7,6},{8,9},{9,8},{10,11... | collective-permute-start | bytes 589832 | tf_op jit(solution)/shard_map/ppermute | solution.py:17
  6.2 14.4 %collective-permute-start.1 = (bf16[3,128,256]{2,1,0:T(8,128)(2,1)S(1)}, bf16[3,128,256]{2,1,0:T(8,128)(2,1)S(1)}, u32[]{:S(2)}, u32[]{:S(2)}) collective-permute-start(bf16[3,128,256]{2,1,0:T(8,128)(2,1)S(1)} %get-tuple-element.18), channel_id=1, source_target_pairs={{0,2},{1,3},{2,0},{3,1},{4,6},{5,7},{6,4},{7,5},{8,10},{9,11},{10,... | collective-permute-start | bytes 589832 | tf_op jit(solution)/shard_map/ppermute | solution.py:17
  9.1 11.5 %collective-permute-start.2 = (bf16[3,128,256]{2,1,0:T(8,128)(2,1)S(1)}, bf16[3,128,256]{2,1,0:T(8,128)(2,1)S(1)}, u32[]{:S(2)}, u32[]{:S(2)}) collective-permute-start(bf16[3,128,256]{2,1,0:T(8,128)(2,1)S(1)} %get-tuple-element.19), channel_id=1, source_target_pairs={{0,3},{1,2},{2,1},{3,0},{4,7},{5,6},{6,5},{7,4},{8,11},{9,10},{10,... | collective-permute-start | bytes 589832 | tf_op jit(solution)/shard_map/ppermute | solution.py:17
  20.7 7.2 %collective-permute-start.3 = (bf16[4,128,256]{2,1,0:T(8,128)(2,1)S(1)}, bf16[4,128,256]{2,1,0:T(8,128)(2,1)S(1)}, u32[]{:S(2)}, u32[]{:S(2)}) collective-permute-start(bf16[4,128,256]{2,1,0:T(8,128)(2,1)S(1)} %pad_maximum_fusion), channel_id=1, source_target_pairs={{0,4},{4,0},{8,12},{12,8},{16,20},{20,16},{24,28},{28,24},{32,36},... | collective-permute-start | bytes 786440 | tf_op jit(solution)/shard_map/ppermute | solution.py:30
  20.8 10.5 %collective-permute-start.4 = (bf16[4,128,256]{2,1,0:T(8,128)(2,1)S(1)}, bf16[4,128,256]{2,1,0:T(8,128)(2,1)S(1)}, u32[]{:S(2)}, u32[]{:S(2)}) collective-permute-start(bf16[4,128,256]{2,1,0:T(8,128)(2,1)S(1)} %pad_maximum_fusion.1), channel_id=1, source_target_pairs={{0,124},{4,8},{8,4},{12,16},{16,12},{20,24},{24,20},{28,32},{32,28... | collective-permute-start | bytes 786440 | tf_op jit(solution)/shard_map/ppermute | solution.py:30
  31.4 48.4 %copy-start.12 = (bf16[512,512]{1,0:T(8,128)(2,1)S(1)}, bf16[512,512]{1,0:T(8,128)(2,1)}, u32[]{:S(2)}) copy-start(bf16[512,512]{1,0:T(8,128)(2,1)} %self_ref.1) | copy-start | bytes 1572868
  31.5 48.3 %copy-start.22 = (s32[2560]{0:T(1024)S(1)}, s32[2560]{0:T(1024)}, u32[]{:S(2)}) copy-start(s32[2560]{0:T(1024)} %param.39) | copy-start | bytes 30724
  31.5 48.3 %copy-start.23 = (s32[2560]{0:T(1024)S(1)}, s32[2560]{0:T(1024)}, u32[]{:S(2)}) copy-start(s32[2560]{0:T(1024)} %param.40) | copy-start | bytes 30724
  62.2 10.9 %collective-permute-start.5 = (bf16[3,64,512]{2,1,0:T(8,128)(2,1)S(1)}, bf16[3,64,512]{2,1,0:T(8,128)(2,1)S(1)}, u32[]{:S(2)}, u32[]{:S(2)}) collective-permute-start(bf16[3,64,512]{2,1,0:T(8,128)(2,1)S(1)} %get-tuple-element.22), channel_id=1, source_target_pairs={{0,1},{1,0},{2,3},{3,2},{4,5},{5,4},{6,7},{7,6},{8,9},{9,8},{10,11... | collective-permute-start | bytes 589832 | tf_op jit(solution)/shard_map/ppermute | solution.py:17
  62.2 10.9 %collective-permute-start.6 = (bf16[3,64,512]{2,1,0:T(8,128)(2,1)S(1)}, bf16[3,64,512]{2,1,0:T(8,128)(2,1)S(1)}, u32[]{:S(2)}, u32[]{:S(2)}) collective-permute-start(bf16[3,64,512]{2,1,0:T(8,128)(2,1)S(1)} %get-tuple-element.23), channel_id=1, source_target_pairs={{0,2},{1,3},{2,0},{3,1},{4,6},{5,7},{6,4},{7,5},{8,10},{9,11},{10,... | collective-permute-start | bytes 589832 | tf_op jit(solution)/shard_map/ppermute | solution.py:17
  64.0 9.1 %collective-permute-start.7 = (bf16[3,64,512]{2,1,0:T(8,128)(2,1)S(1)}, bf16[3,64,512]{2,1,0:T(8,128)(2,1)S(1)}, u32[]{:S(2)}, u32[]{:S(2)}) collective-permute-start(bf16[3,64,512]{2,1,0:T(8,128)(2,1)S(1)} %get-tuple-element.24), channel_id=1, source_target_pairs={{0,3},{1,2},{2,1},{3,0},{4,7},{5,6},{6,5},{7,4},{8,11},{9,10},{10,... | collective-permute-start | bytes 589832 | tf_op jit(solution)/shard_map/ppermute | solution.py:17
  66.9 22.7 %all-to-all-start = ((bf16[128,8,128]{2,1,0:T(8,128)(2,1)}), bf16[128,8,128]{2,1,0:T(8,128)(2,1)S(1)}, u32[]{:S(2)}, u32[]{:S(2)}) async-start(bf16[128,8,128]{2,1,0:T(8,128)(2,1)} %bitcast.7), calls=%async_computation | async-start | bytes 524288 | tf_op jit(solution)/shard_map/all_to_all | solution.py:577
  73.9 15.7 %collective-permute-start.8 = (bf16[4,64,512]{2,1,0:T(8,128)(2,1)}, bf16[4,64,512]{2,1,0:T(8,128)(2,1)S(1)}, u32[]{:S(2)}, u32[]{:S(2)}) collective-permute-start(bf16[4,64,512]{2,1,0:T(8,128)(2,1)} %pad_maximum_fusion.2), channel_id=1, source_target_pairs={{0,4},{4,0},{8,12},{12,8},{16,20},{20,16},{24,28},{28,24},{32,36},... | collective-permute-start | bytes 786440 | tf_op jit(solution)/shard_map/ppermute | solution.py:30
  74.7 14.9 %collective-permute-start.9 = (bf16[4,64,512]{2,1,0:T(8,128)(2,1)}, bf16[4,64,512]{2,1,0:T(8,128)(2,1)}, u32[]{:S(2)}, u32[]{:S(2)}) collective-permute-start(bf16[4,64,512]{2,1,0:T(8,128)(2,1)} %pad_maximum_fusion.3), channel_id=1, source_target_pairs={{0,124},{4,8},{8,4},{12,16},{16,12},{20,24},{24,20},{28,32},{32,28... | collective-permute-start | bytes 786440 | tf_op jit(solution)/shard_map/ppermute | solution.py:30
  (23 other events, 278.0 us)

commit v3 on v2

v3 whole, which is shorter than its diff:
```python
import functools

import jax
import jax.numpy as jnp
from jax import lax
from jax.experimental import pallas as pl
from jax.experimental.pallas import tpu as pltpu
from jax.sharding import PartitionSpec as P

LANES = 128
EDGE_BLOCK = 512
PAIR = 2 * EDGE_BLOCK
VMEM_BYTES = 24 * 1024 * 1024
VMEM_ALL = 60 * 1024 * 1024
START_FLOPS = 2 * 10**9
START_BYTES = 8 << 20


def sub_swap(value, step):
    count = lax.axis_size("sub")
    return lax.ppermute(value, "sub", [(t, t ^ step) for t in range(count)])


def mate(band):
    return band ^ 1


def cross(band, count):
    return (((band + 1) ^ 1) - 1) % count


def band_swap(value, partner):
    count = lax.axis_size("band")
    return lax.ppermute(value, "band", [(b, partner(b)) for b in range(count)])


def offsets():
    even = lax.rem(lax.axis_index("band"), 2) == 0
    return (1, jnp.where(even, 2, 0), jnp.where(even, 0, 2))


def sources():
    even = lax.rem(lax.axis_index("band"), 2) == 0
    return (1, jnp.where(even, 0, 2), jnp.where(even, 2, 0))


def layer_norm(values):
    row_mean = jnp.mean(values, axis=-1, keepdims=True)
    centred = values - row_mean
    variance = jnp.mean(centred * centred, axis=-1, keepdims=True)
    return centred * lax.rsqrt(variance + 1e-05)


def silu(values):
    half = 0.5 * values
    return half + half * jnp.tanh(half)


def dot(left, right):
    return jnp.dot(left, right, preferred_element_type=jnp.float32)


def half(values):
    return values.astype(jnp.bfloat16)


def column(row):
    return jnp.broadcast_to(row, (LANES, LANES)).T


def row_of(ref, first, count):
    return jnp.concatenate([ref[pl.ds(first + k, 1), :] for k in range(count)], axis=1)


def spread(rows, places):
    lanes = sum(1 for _ in places) * LANES
    lane = lax.broadcasted_iota(jnp.int32, (8, lanes), 1)
    row = lax.broadcasted_iota(jnp.int32, (8, lanes), 0)
    factors = jnp.zeros((8, lanes), jnp.float32)
    for k, entries in enumerate(places):
        for index, low, high, factor in entries:
            here = (row == index) & (lane >= k * LANES + low) & (lane < k * LANES + high)
            factors = jnp.where(here, factor, factors)
    return dot(half(rows.T), half(factors))


def digits(row):
    return [(row >> 7).astype(jnp.float32), (row & (LANES - 1)).astype(jnp.float32)]


def index_entry(first):
    return [(first, 0, LANES, float(LANES)), (first + 1, 0, LANES, 1.0)]


def lanes_of(indices):
    return lax.broadcasted_iota(jnp.int32, indices.shape, 1).astype(jnp.float32)


def picks(indices, width):
    lane = lanes_of(indices)
    indices = indices.astype(jnp.float32)
    parts = [
        half(jnp.where(indices == lane + float(first), 1.0, 0.0))
        for first in range(0, width, LANES)
    ]
    return jnp.concatenate(parts, axis=1)


def scatter_picks(row, height):
    shape = (height, row.shape[1])
    sub = lax.broadcasted_iota(jnp.int32, shape, 0)
    return half(jnp.where(sub == jnp.broadcast_to(row, shape), 1.0, 0.0))


def whole():
    return pl.BlockSpec(memory_space=pltpu.VMEM)


def in_smem():
    return pl.BlockSpec(memory_space=pltpu.SMEM)


def in_hbm():
    return pl.BlockSpec(memory_space=pltpu.HBM)


def local_call(
    kernel, out_shape, in_specs, scratch=(), flops=0, nbytes=0, out_specs=None, vmem=VMEM_BYTES
):
    return pl.pallas_call(
        kernel,
        out_shape=out_shape,
        in_specs=in_specs,
        out_specs=out_specs or jax.tree.map(lambda _: whole(), out_shape),
        scratch_shapes=list(scratch),
        compiler_params=pltpu.CompilerParams(vmem_limit_bytes=vmem),
        cost_estimate=pl.CostEstimate(flops=flops, bytes_accessed=nbytes, transcendentals=0),
    )


class Fetch:
    def __init__(self, refs, slots, sems):
        self.copies = [
            pltpu.make_async_copy(ref, slots.at[k], sems.at[k]) for k, ref in enumerate(refs)
        ]
        self.slots, self.ready = slots, set()
        for copy in self.copies:
            copy.start()

    def __call__(self, k):
        if k not in self.ready:
            self.copies[k].wait()
            self.ready.add(k)
        return self.slots.at[k]


def pick_grid_kernel(send_ref, grid_ref, *refs):
    out_refs, sum_ref = refs[:-1], refs[-1]
    width, rows = grid_ref.shape
    wide = out_refs[0].shape[-1]
    me = lax.axis_index("sub")
    part = pl.program_id(0)
    index = jnp.concatenate(
        [
            send_ref[offset, pl.ds(me ^ k, 1), :]
            for k in range(len(out_refs))
            for offset in offsets()
        ],
        axis=1,
    )
    picked = dot(grid_ref[...], scatter_picks(index - part * rows, rows))

    @pl.when(part == 0)
    def _():
        sum_ref[0:width, :] = picked
        sum_ref[width:, :] = jnp.zeros((wide - width, picked.shape[1]), jnp.float32)

    @pl.when(part > 0)
    def _():
        sum_ref[0:width, :] += picked

    @pl.when(part == pl.num_programs(0) - 1)
    def _():
        for k, out_ref in enumerate(out_refs):
            for w in range(3):
                first = (3 * k + w) * LANES
                out_ref[w] = half(sum_ref[:, first : first + LANES].T)


def prepare_grid_kernel(
    live_ref,
    src_ref,
    dst_ref,
    geo_ref,
    embed_ref,
    recv_proj_ref,
    geo_proj_ref,
    node_self_ref,
    place_ref,
    own_ref,
    node_ref,
    table_ref,
):
    mesh_rows, latent = embed_ref.shape
    base = table_ref.shape[0]
    geo_rows = geo_ref.shape[0]
    received = 3 * lax.axis_size("sub") * LANES
    is_last = lax.axis_index("band") == lax.axis_size("band") - 1
    src_shift = jnp.where(is_last, received // 3, 0)
    node_ref[...] = dot(embed_ref[...], node_self_ref[...])
    table_ref[0:mesh_rows, :] = half(dot(embed_ref[...], recv_proj_ref[...]))
    table_ref[mesh_rows:base, :] = half(
        jnp.concatenate(
            [
                geo_proj_ref[...].astype(jnp.float32),
                jnp.zeros((base - mesh_rows - geo_rows, latent), jnp.float32),
            ],
            axis=0,
        )
    )
    low = mesh_rows % LANES
    places = [
        index_entry(0),
        index_entry(2),
        [(4 + k, low + k, low + k + 1, 1.0) for k in range(geo_rows)],
    ]
    per = EDGE_BLOCK // LANES

    def step(block, carry):
        row0 = pl.multiple_of(block * EDGE_BLOCK, EDGE_BLOCK)
        rows = jnp.concatenate(
            digits(row_of(src_ref, block * per, per) - src_shift)
            + digits(row_of(dst_ref, block * per, per))
            + [geo_ref[:, pl.ds(row0, EDGE_BLOCK)].astype(jnp.float32)],
            axis=0,
        )
        wide = spread(rows, places)
        place_ref[pl.ds(row0, EDGE_BLOCK), :] = wide[:, 0:LANES]
        target = wide[:, LANES : 2 * LANES]
        lane = lanes_of(target)
        parts = []
        for k in range(base // LANES):
            part = jnp.where(target == lane + float(k * LANES), 1.0, 0.0)
            if k == mesh_rows // LANES:
                part = part + wide[:, 2 * LANES :]
            parts.append(half(part))
        own = dot(jnp.concatenate(parts, axis=1), table_ref[...])
        own_ref[pl.ds(row0, EDGE_BLOCK), :] = half(own)
        return carry

    lax.fori_loop(0, pl.cdiv(live_ref[0], PAIR) * (PAIR // EDGE_BLOCK), step, 0)


def encode_rows(rows, enc_in, enc_out, send_proj):
    hidden = half(silu(dot(rows, enc_in)))
    lat = half(layer_norm(dot(hidden, enc_out)))
    return half(dot(lat, send_proj))


def padded_rows(ref, rows):
    values = ref[...].astype(jnp.float32)
    zeros = jnp.zeros((rows - values.shape[0], values.shape[1]), jnp.float32)
    return half(jnp.concatenate([values, zeros], axis=0))


def encode_own_kernel(
    own0_ref, own1_ref, own2_ref, own3_ref, enc_in_ref, enc_out_ref, send_proj_ref, out_ref
):
    owns = (own0_ref, own1_ref, own2_ref, own3_ref)
    cap, wide = own0_ref.shape[1:]
    me = lax.axis_index("sub")
    sent = encode_rows(
        jnp.concatenate([ref[0] for ref in owns], axis=0),
        padded_rows(enc_in_ref, wide),
        enc_out_ref[...],
        send_proj_ref[...],
    )
    for k in range(len(owns)):
        out_ref[pl.ds(pl.multiple_of((me ^ k) * cap, cap), cap), :] = sent[
            k * cap : (k + 1) * cap
        ]


def encoder_kernel(
    live_ref,
    own_rows_ref,
    mate_ref,
    cross_ref,
    place_ref,
    own_ref,
    dst_ref,
    embed_ref,
    node_ref,
    near_ref,
    far_ref,
    enc_in_ref,
    gain_ref,
    enc_out_ref,
    send_proj_ref,
    msg_ref,
    node_agg_ref,
    node_out_ref,
    proc_send_ref,
    proc_recv_ref,
    latent_ref,
    pair_ref,
    out0_ref,
    out1_ref,
    out2_ref,
    out3_ref,
    out_far_ref,
    table_ref,
    sum_ref,
    flat_ref,
    act_ref,
    slots_ref,
    sems,
):
    weight = Fetch(
        (
            enc_out_ref,
            send_proj_ref,
            msg_ref,
            node_agg_ref,
            node_out_ref,
            proc_send_ref,
            proc_recv_ref,
        ),
        slots_ref,
        sems,
    )
    mesh_rows, latent = embed_ref.shape
    subs, cap, wide = mate_ref.shape
    chunk = subs * cap
    band, me = lax.axis_index("band"), lax.axis_index("sub")
    is_first = band == 0
    is_last = band == lax.axis_size("band") - 1
    polar = is_first | is_last
    live = live_ref[0]
    enc_in = padded_rows(enc_in_ref, wide)

    start = jnp.where(is_last, -chunk, 0)
    _, mate_place, cross_place = sources()
    table_ref[pl.ds(pl.multiple_of(start + chunk, chunk), chunk), :] = own_rows_ref[...]

    def encode(ref, offset):
        sent = encode_rows(ref[...].reshape(chunk, wide), enc_in, weight(0)[...], weight(1)[...])
        for k in range(subs):
            place = pl.multiple_of(start + offset * chunk + (me ^ k) * cap, cap)
            table_ref[pl.ds(place, cap), :] = sent[k * cap : (k + 1) * cap]

    encode(mate_ref, mate_place)

    @pl.when(jnp.logical_not(polar))
    def _():
        encode(cross_ref, cross_place)

    sum_ref[...] = jnp.zeros_like(sum_ref)

    def scatter(pair):
        lane = lax.broadcasted_iota(jnp.int32, (1, PAIR), 1)
        target = row_of(dst_ref, pair * (PAIR // LANES), PAIR // LANES)
        target = jnp.where(pair * PAIR + lane < live, target, -1)
        sum_ref[...] += dot(scatter_picks(target, mesh_rows), act_ref[...])

    act_ref[...] = half(
        silu(table_ref[0:PAIR, :].astype(jnp.float32) + own_ref[0:PAIR, :].astype(jnp.float32))
    )
    scatter(0)

    def edges(lookup_rows):
        def step(pair, carry):
            for k in range(PAIR // EDGE_BLOCK):
                row0 = pl.multiple_of(pair * PAIR + k * EDGE_BLOCK, EDGE_BLOCK)
                onehot = picks(place_ref[pl.ds(row0, EDGE_BLOCK), :], lookup_rows)
                pre = dot(onehot, table_ref[0:lookup_rows, :]) + own_ref[
                    pl.ds(row0, EDGE_BLOCK), :
                ].astype(jnp.float32)
                act_ref[k * EDGE_BLOCK : (k + 1) * EDGE_BLOCK, :] = half(silu(pre))
            scatter(pair)
            return carry

        lax.fori_loop(1, pl.cdiv(live, PAIR), step, 0)

    @pl.when(polar)
    def _():
        edges(2 * chunk)

    @pl.when(jnp.logical_not(polar))
    def _():
        edges(3 * chunk)

    total = sum_ref[...]
    high = half(total)
    low = half(total - high.astype(jnp.float32))
    inflow = half(dot(high, weight(2)[...]) + dot(low, weight(2)[...]))
    embed = embed_ref[...]
    node_act = half(silu(node_ref[...] + dot(inflow, weight(3)[...])))
    mesh_latent = half(
        embed.astype(jnp.float32) + layer_norm(dot(node_act, weight(4)[...])) * gain_ref[...]
    )
    latent_ref[...] = mesh_latent
    sender = half(dot(mesh_latent, weight(5)[...]))
    pair_ref[0:mesh_rows, :] = sender
    pair_ref[mesh_rows : 2 * mesh_rows, :] = half(dot(mesh_latent, weight(6)[...]))
    padded = -(-mesh_rows // LANES) * LANES
    sender_pad = jnp.concatenate(
        [sender, jnp.zeros((padded - mesh_rows, latent), jnp.bfloat16)], axis=0
    )
    near = near_ref.shape[2]
    shares = offsets()
    for k, out_ref in enumerate((out0_ref, out1_ref, out2_ref, out3_ref)):
        index = [near_ref[offset, pl.ds(me ^ k, 1), :] for offset in shares]
        index.append(jnp.zeros((1, 4 * near - 3 * near), jnp.int32))
        index = jnp.concatenate(index, axis=1)
        onehot = jnp.concatenate(
            [
                picks(column(index[:, first : first + LANES]), padded)
                for first in range(0, 4 * near, LANES)
            ],
            axis=0,
        )
        out_ref[...] = half(dot(onehot[0 : 3 * near], sender_pad)).reshape(out_ref.shape)
    lanes = latent // LANES
    spread = far_ref.shape[0] * lanes
    for c in range(far_ref.shape[0]):
        rows = dot(picks(column(far_ref[c : c + 1, :]), padded), sender_pad)
        for j in range(lanes):
            flat_ref[pl.ds(c * lanes + j, LANES, stride=spread), :] = rows[
                :, j * LANES : (j + 1) * LANES
            ]
    out_far_ref[...] = half(flat_ref[...])


def edge_start_kernel(
    src_ref,
    dst_ref,
    pair_ref,
    lat_hbm,
    self_hbm,
    pre_hbm,
    place_hbm,
    lat_ref,
    self_ref,
    pre_ref,
    place_ref,
    read_sems,
    write_sems,
):
    mesh_rows = pair_ref.shape[0] // 2
    subs = lax.axis_size("sub")
    devices = lax.axis_size("band") * subs
    near_total = 3 * subs * (LANES // 2)
    blocks = lat_ref.shape[0] // EDGE_BLOCK
    per = EDGE_BLOCK // LANES
    spans = [pl.ds(block * EDGE_BLOCK, EDGE_BLOCK) for block in range(blocks)]
    weight = pltpu.make_async_copy(self_hbm, self_ref, read_sems.at[blocks])
    reads = [
        pltpu.make_async_copy(lat_hbm.at[span], lat_ref.at[span], read_sems.at[k])
        for k, span in enumerate(spans)
    ]
    writes = []
    for copy in [weight, *reads]:
        copy.start()
    places = [index_entry(0), index_entry(2), index_entry(4)]
    for block, span in enumerate(spans):
        source = row_of(src_ref, block * per, per)
        target = row_of(dst_ref, block * per, per)
        other = source - mesh_rows
        far = other - near_total
        far = near_total + (far & 1) * devices + (far >> 1)
        rows = jnp.concatenate(
            digits(jnp.where(source < mesh_rows, source, -1))
            + digits(target + mesh_rows)
            + digits(jnp.where(other < near_total, other, far))
            + [jnp.zeros((2, EDGE_BLOCK), jnp.float32)],
            axis=0,
        )
        wide = spread(rows, places)
        own, mine = wide[:, 0:LANES], wide[:, LANES : 2 * LANES]
        place_ref[span, :] = wide[:, 2 * LANES :]
        lane = lanes_of(own)
        parts = []
        for first in range(0, 2 * mesh_rows, LANES):
            hit = None
            if first < mesh_rows:
                hit = own == lane + float(first)
            if first + LANES > mesh_rows:
                match = mine == lane + float(first)
                hit = match if hit is None else hit | match
            parts.append(half(jnp.where(hit, 1.0, 0.0)))
        picked = dot(jnp.concatenate(parts, axis=1), pair_ref[...])
        if block == 0:
            weight.wait()
        reads[block].wait()
        pre_ref[span, :] = half(picked + dot(lat_ref[span, :], self_ref[...]))
        for j, (ref, hbm) in enumerate(((pre_ref, pre_hbm), (place_ref, place_hbm))):
            writes.append(
                pltpu.make_async_copy(ref.at[span], hbm.at[span], write_sems.at[2 * block + j])
            )
            writes[-1].start()
    for copy in writes:
        copy.wait()


def edge_finish_kernel(
    dst_ref,
    far_ref,
    latent_ref,
    gain_ref,
    pre_hbm,
    place_hbm,
    lat_hbm,
    own0_hbm,
    own1_hbm,
    own2_hbm,
    own3_hbm,
    mate_hbm,
    cross_hbm,
    edge_out_ref,
    upd_self_ref,
    upd_agg_ref,
    upd_out_ref,
    out_ref,
    table_ref,
    flat_ref,
    new_ref,
    pre_ref,
    place_ref,
    lat_ref,
    slots_ref,
    sems,
    table_sems,
    block_sems,
):
    mesh_rows, latent = latent_ref.shape
    blocks = lat_ref.shape[0] // EDGE_BLOCK
    spans = [pl.ds(block * EDGE_BLOCK, EDGE_BLOCK) for block in range(blocks)]
    subs, near, _ = mate_hbm.shape
    near_total = 3 * subs * near
    me = lax.axis_index("sub")
    owns = (own0_hbm, own1_hbm, own2_hbm, own3_hbm)
    rows = []
    for w, offset in enumerate(sources()):
        for k in range(subs):
            source = owns[k].at[0] if w == 0 else (mate_hbm, cross_hbm)[w - 1].at[k]
            place = pl.multiple_of((offset * subs + (me ^ k)) * near, near)
            rows.append(
                pltpu.make_async_copy(
                    source, table_ref.at[pl.ds(place, near)], table_sems.at[w * subs + k]
                )
            )
    moved = ((pre_hbm, pre_ref), (place_hbm, place_ref), (lat_hbm, lat_ref))
    reads = [
        [
            pltpu.make_async_copy(hbm.at[span], ref.at[span], block_sems.at[3 * k + j])
            for j, (hbm, ref) in enumerate(moved)
        ]
        for k, span in enumerate(spans)
    ]
    for copy in rows + reads[0]:
        copy.start()
    weight = Fetch((edge_out_ref, upd_self_ref, upd_agg_ref, upd_out_ref), slots_ref, sems)
    for block in reads[1:]:
        for copy in block:
            copy.start()
    lanes = latent // LANES
    devices = far_ref.shape[0] // (2 * lanes)
    flat_ref[...] = far_ref[...].astype(jnp.float32)
    for c in range(2):
        table_ref[pl.ds(near_total + c * devices, devices), :] = half(
            jnp.concatenate(
                [
                    flat_ref[pl.ds(c * lanes + j, devices, stride=2 * lanes), :]
                    for j in range(lanes)
                ],
                axis=1,
            )
        )
    for copy in rows:
        copy.wait()
    edge_out = weight(0)[...]
    upd_self = dot(latent_ref[...], weight(1)[...])

    def gathered(block):
        span = spans[block]
        for copy in reads[block]:
            copy.wait()
        return pre_ref[span, :].astype(jnp.float32) + dot(
            picks(place_ref[span, :], table_ref.shape[0]), table_ref[...]
        )

    def settle(block, pre):
        span = spans[block]
        out = layer_norm(dot(half(silu(pre)), edge_out))
        new_ref[span, :] = half(lat_ref[span, :].astype(jnp.float32) + out)

    pre = gathered(0)
    for block in range(1, blocks):
        later = gathered(block)
        settle(block - 1, pre)
        pre = later
    settle(blocks - 1, pre)
    target = row_of(dst_ref, 0, lat_ref.shape[0] // LANES)
    inflow = half(dot(scatter_picks(target, mesh_rows), new_ref[...]))
    latent = latent_ref[...]
    act = half(silu(upd_self + dot(inflow, weight(2)[...])))
    out_ref[...] = half(
        latent.astype(jnp.float32) + layer_norm(dot(act, weight(3)[...])) * gain_ref[...]
    )


def body(
    grid_input,
    grid_send,
    grid_edge_src,
    grid_edge_dst,
    edge_count,
    grid_edge_geo,
    mesh_embed,
    mesh_near_send,
    mesh_far_send,
    mesh_edge_src,
    mesh_edge_dst,
    mesh_edge_lat,
    enc_in,
    enc_out,
    send_proj,
    recv_proj,
    geo_proj,
    msg_weight,
    node_self,
    node_agg,
    node_out,
    mesh_gain,
    proc_send,
    proc_recv,
    edge_self,
    edge_out,
    upd_self,
    upd_agg,
    upd_out,
    out_gain,
):
    sub_count = lax.axis_size("sub")
    devices = lax.axis_size("band") * sub_count
    slot_cap = grid_send.shape[2]
    near_cap = mesh_near_send.shape[2]
    far_cap = mesh_far_send.shape[1]
    mesh_rows, latent = mesh_embed.shape
    edges = grid_edge_src.shape[0]
    mesh_edges = mesh_edge_src.shape[0]
    wide = 256
    bf16, f32 = jnp.bfloat16, jnp.float32

    def across_subs(parts):
        return [parts[0]] + [sub_swap(parts[k], k) for k in range(1, sub_count)]

    def across_bands(arrived):
        mates = band_swap(jnp.stack([part[1] for part in arrived]), mate)
        crosses = band_swap(
            jnp.stack([part[2] for part in arrived]),
            functools.partial(cross, count=lax.axis_size("band")),
        )
        return mates, crosses

    def shape(*dims, dtype=bf16):
        return jax.ShapeDtypeStruct(dims, dtype)

    received = sub_count * slot_cap
    halves = grid_input.shape[0] // 2
    parts = pl.pallas_call(
        pick_grid_kernel,
        grid=(2,),
        out_shape=(shape(3, slot_cap, wide),) * sub_count,
        in_specs=[
            pl.BlockSpec(grid_send.shape, lambda i: (0, 0, 0)),
            pl.BlockSpec((grid_input.shape[1], halves), lambda i: (0, i)),
        ],
        out_specs=(pl.BlockSpec((3, slot_cap, wide), lambda i: (0, 0, 0)),) * sub_count,
        scratch_shapes=[pltpu.VMEM((wide, 3 * received), f32)],
        compiler_params=pltpu.CompilerParams(vmem_limit_bytes=VMEM_ALL),
        cost_estimate=pl.CostEstimate(
            flops=6 * received * grid_input.shape[0] * wide,
            bytes_accessed=2 * wide * (3 * received + grid_input.shape[0]),
            transcendentals=0,
        ),
    )(grid_send, grid_input.T)
    arrived = across_subs(parts)

    far_total = devices * far_cap
    others = 3 * sub_count * near_cap + far_total
    blocks = mesh_edges // EDGE_BLOCK
    edge_src, _ = lax.optimization_barrier((grid_edge_src, parts[0]))
    edge_dst = grid_edge_dst.reshape(-1, LANES)
    mesh_src = mesh_edge_src.reshape(-1, LANES)
    mesh_dst = mesh_edge_dst.reshape(-1, LANES)
    place, own, node = local_call(
        prepare_grid_kernel,
        (
            shape(edges, LANES, dtype=f32),
            shape(edges, latent),
            shape(mesh_rows, latent, dtype=f32),
        ),
        [in_smem()] + [whole()] * 7,
        scratch=[pltpu.VMEM((384, latent), bf16)],
        flops=2 * edges * 1024 * latent,
        nbytes=16 << 20,
    )(
        edge_count,
        edge_src.reshape(-1, LANES),
        edge_dst,
        grid_edge_geo,
        mesh_embed,
        recv_proj,
        geo_proj,
        node_self,
    )

    arrived, place, own, node = lax.optimization_barrier((arrived, place, own, node))
    mates, crosses = across_bands(arrived)
    own_rows = local_call(
        encode_own_kernel,
        shape(received, latent),
        [whole()] * 7,
        flops=2 * received * 1280 * latent,
        nbytes=3 << 20,
    )(*arrived, enc_in, enc_out, send_proj)

    mesh_latent, pairs, *near_parts, far_out = local_call(
        encoder_kernel,
        (
            shape(mesh_rows, latent),
            shape(2 * mesh_rows, latent),
        )
        + (shape(3, near_cap, latent),) * sub_count
        + (shape(far_total * latent // LANES, LANES),),
        [in_smem()] + [whole()] * 12 + [in_hbm()] * 7,
        scratch=[
            pltpu.VMEM((3 * received, latent), bf16),
            pltpu.VMEM((mesh_rows, latent), f32),
            pltpu.VMEM((far_total * latent // LANES, LANES), f32),
            pltpu.VMEM((PAIR, latent), bf16),
            pltpu.VMEM((7, latent, latent), bf16),
            pltpu.SemaphoreType.DMA((7,)),
        ],
        flops=2 * edges * 2048 * latent,
        nbytes=16 << 20,
    )(
        edge_count,
        own_rows,
        mates,
        crosses,
        place,
        own,
        edge_dst,
        mesh_embed,
        node,
        mesh_near_send,
        mesh_far_send.T,
        enc_in,
        mesh_gain.reshape(1, latent),
        enc_out,
        send_proj,
        msg_weight,
        node_agg,
        node_out,
        proc_send,
        proc_recv,
    )

    near_arrived = across_subs(near_parts)
    far_rows = lax.all_to_all(
        far_out.reshape(devices, -1, LANES),
        ("band", "sub"),
        split_axis=0,
        concat_axis=0,
        tiled=True,
    ).reshape(-1, LANES)
    near_mates, near_crosses = across_bands(near_arrived)
    pre, mesh_place = local_call(
        edge_start_kernel,
        (shape(mesh_edges, latent), shape(mesh_edges, LANES, dtype=f32)),
        [whole()] * 3 + [in_hbm()] * 2,
        scratch=[
            pltpu.VMEM((mesh_edges, latent), bf16),
            pltpu.VMEM((latent, latent), bf16),
            pltpu.VMEM((mesh_edges, latent), bf16),
            pltpu.VMEM((mesh_edges, LANES), f32),
            pltpu.SemaphoreType.DMA((blocks + 1,)),
            pltpu.SemaphoreType.DMA((2 * blocks,)),
        ],
        flops=START_FLOPS,
        nbytes=START_BYTES,
        out_specs=(in_hbm(), in_hbm()),
        vmem=VMEM_ALL,
    )(mesh_src, mesh_dst, pairs, mesh_edge_lat, edge_self)
    return local_call(
        edge_finish_kernel,
        shape(mesh_rows, latent),
        [whole()] * 4 + [in_hbm()] * 13,
        scratch=[
            pltpu.VMEM((others, latent), bf16),
            pltpu.VMEM((far_total * latent // LANES, LANES), f32),
            pltpu.VMEM((mesh_edges, latent), bf16),
            pltpu.VMEM((mesh_edges, latent), bf16),
            pltpu.VMEM((mesh_edges, LANES), f32),
            pltpu.VMEM((mesh_edges, latent), bf16),
            pltpu.VMEM((4, latent, latent), bf16),
            pltpu.SemaphoreType.DMA((4,)),
            pltpu.SemaphoreType.DMA((3 * sub_count,)),
            pltpu.SemaphoreType.DMA((3 * blocks,)),
        ],
        flops=2 * mesh_edges * 2048 * latent,
        nbytes=12 << 20,
        vmem=VMEM_ALL,
    )(
        mesh_dst,
        far_rows,
        mesh_latent,
        out_gain.reshape(1, latent),
        pre,
        mesh_place,
        mesh_edge_lat,
        *near_arrived,
        near_mates,
        near_crosses,
        edge_out,
        upd_self,
        upd_agg,
        upd_out,
    )


def solution(mesh):
    rows = P(("band", "sub"), None)
    blocks = P(("band", "sub"), None, None)
    flat = P(("band", "sub"))
    return jax.shard_map(
        body,
        mesh=mesh,
        in_specs=(
            rows,
            blocks,
            flat,
            flat,
            flat,
            P(None, ("band", "sub")),
            rows,
            blocks,
            rows,
            flat,
            flat,
            rows,
        )
        + (P(),) * 18,
        out_specs=rows,
        check_vma=False,
    )
```

time: 108 us -> 98 us (0.907)
  the two profiles are of different devices: /device:TPU:0 before, /device:TPU:1 now
where the time goes in v3:
time: 98 us; the launch traced here: 97.8 us
  Pallas kernels  40.3 us (41%)
  starting transfers between devices  35.4 us (36%)
  waiting for transfers between devices  18.9 us (19%)
  local copies, waits for them, and re-layouts  1.9 us (2%)
  between operations  1.22 us (1%)
    ppermute x6, starting transfers between devices, sub_swap(): return lax.ppermute(value, 'sub', [(t, t ^ step) for t in range(count)])  14.7 us
    ppermute x4, starting transfers between devices, band_swap(): return lax.ppermute(value, 'band', [(b, partner(b)) for b in range(count)])  13.2 us
    pallas_call x1, Pallas kernels, body(): local_call(edge_finish_kernel, shape(mesh_rows, latent), [whole()] * 4 +...  13.2 us
    ppermute x6, waiting for transfers between devices, sub_swap(): return lax.ppermute(value, 'sub', [(t, t ^ step) for t in range(count)])  13 us
    pallas_call x1, Pallas kernels, body(): local_call(encoder_kernel, (shape(mesh_rows, latent), shape(2 * mesh_rows...  9.93 us
    pallas_call x1, Pallas kernels, body(): local_call(edge_start_kernel, (shape(mesh_edges, latent), shape(mesh_edge...  8.41 us
    all_to_all x1, starting transfers between devices, body(): lax.all_to_all(far_out.reshape(devices, -1, LANES), ('band', 'sub'), spli...  7.47 us
    pallas_call x1, Pallas kernels, body(): pl.pallas_call(pick_grid_kernel, grid=(2,), out_shape=(shape(3, slot_cap,...  4.55 us
  transfers between devices with their start and end apart: 11, of which 7 were waited for; matrix products, arithmetic and copies ran while one was open for 0% of the time, Pallas kernels for 13%

profile of v3, /device:TPU:1, one launch (start us, length us, event | category | flops | bytes accessed | tf_op | source)
XLA Modules:
  0.0 97.8 jit_solution(3715376342981174517)
XLA Ops:
  0.0 4.6 %shard_map.280 = (bf16[3,128,256]{2,1,0:T(8,128)(2,1)}, bf16[3,128,256]{2,1,0:T(8,128)(2,1)}, bf16[3,128,256]{2,1,0:T(8,128)(2,1)}, bf16[3,128,256]{2,1,0:T(8,128)(2,1)}) custom-call(s32[3,4,128]{2,1,0:T(4,128)} %send_ref.1, bf16[227,2048]{1,0:T(8,128)(2,1)} %bitcast.16), custom_call_target="tpu_custom_call" | custom-call | flops 1610612736 | bytes 1835008 | tf_op jit(solution)/shard_map/pallas_call | solution.py:672
  4.6 2.1 %collective-permute-start = (bf16[3,128,256]{2,1,0:T(8,128)(2,1)}, bf16[3,128,256]{2,1,0:T(8,128)(2,1)S(1)}, u32[]{:S(2)}, u32[]{:S(2)}) collective-permute-start(bf16[3,128,256]{2,1,0:T(8,128)(2,1)} %get-tuple-element.30), channel_id=1, source_target_pairs={{0,1},{1,0},{2,3},{3,2},{4,5},{5,4},{6,7},{7,6},{8,9},{9,8},{10,11... | collective-permute-start | bytes 589832 | tf_op jit(solution)/shard_map/ppermute | solution.py:21
  6.7 2.6 %collective-permute-start.1 = (bf16[3,128,256]{2,1,0:T(8,128)(2,1)}, bf16[3,128,256]{2,1,0:T(8,128)(2,1)S(1)}, u32[]{:S(2)}, u32[]{:S(2)}) collective-permute-start(bf16[3,128,256]{2,1,0:T(8,128)(2,1)} %get-tuple-element.31), channel_id=1, source_target_pairs={{0,2},{1,3},{2,0},{3,1},{4,6},{5,7},{6,4},{7,5},{8,10},{9,11},{10,... | collective-permute-start | bytes 589832 | tf_op jit(solution)/shard_map/ppermute | solution.py:21
  10.1 3.0 %shard_map.281 = (f32[8192,128]{1,0:T(8,128)S(1)}, bf16[8192,512]{1,0:T(8,128)(2,1)S(1)}, f32[320,512]{1,0:T(8,128)S(1)}) custom-call(s32[1]{0:T(128)S(6)} %copy.31.live_ref, s32[64,128]{1,0:T(8,128)S(1)} %bitcast.10, s32[64,128]{1,0:T(8,128)S(1)} %bitcast.11, bf16[4,8192]{1,0:T(4,128)(2,1)S(1)} %copy-done.13, bf16[320,512]{1,0:T(8,128)(2,1)S(1)} %copy-done.12, ...), custom_call_target="tpu_custom_call" | custom-call | flops 8589934592 | bytes 16777216 | tf_op jit(solution)/shard_map/pallas_call | solution.py:698
  13.2 4.9 %collective-permute-done.1.own2_ref = bf16[3,128,256]{2,1,0:T(8,128)(2,1)S(1)} collective-permute-done((bf16[3,128,256]{2,1,0:T(8,128)(2,1)}, bf16[3,128,256]{2,1,0:T(8,128)(2,1)S(1)}, u32[]{:S(2)}, u32[]{:S(2)}) %collective-permute-start.1) | collective-permute-done | bytes 196640 | tf_op jit(solution)/shard_map/ppermute | solution.py:21
  18.1 2.7 %collective-permute-done.2.own3_ref = bf16[3,128,256]{2,1,0:T(8,128)(2,1)S(1)} collective-permute-done((bf16[3,128,256]{2,1,0:T(8,128)(2,1)}, bf16[3,128,256]{2,1,0:T(8,128)(2,1)S(1)}, u32[]{:S(2)}, u32[]{:S(2)}) %collective-permute-start.2) | collective-permute-done | bytes 196640 | tf_op jit(solution)/shard_map/ppermute | solution.py:21
  20.9 1.6 %collective-permute-start.3 = (bf16[4,128,256]{2,1,0:T(8,128)(2,1)S(1)}, bf16[4,128,256]{2,1,0:T(8,128)(2,1)S(1)}, u32[]{:S(2)}, u32[]{:S(2)}) collective-permute-start(bf16[4,128,256]{2,1,0:T(8,128)(2,1)S(1)} %pad_maximum_fusion), channel_id=1, source_target_pairs={{0,4},{4,0},{8,12},{12,8},{16,20},{20,16},{24,28},{28,24},{32,36},... | collective-permute-start | bytes 786440 | tf_op jit(solution)/shard_map/ppermute | solution.py:34
  22.5 1.6 %collective-permute-start.4 = (bf16[4,128,256]{2,1,0:T(8,128)(2,1)S(1)}, bf16[4,128,256]{2,1,0:T(8,128)(2,1)S(1)}, u32[]{:S(2)}, u32[]{:S(2)}) collective-permute-start(bf16[4,128,256]{2,1,0:T(8,128)(2,1)S(1)} %pad_maximum_fusion.1), channel_id=1, source_target_pairs={{0,124},{4,8},{8,4},{12,16},{16,12},{20,24},{24,20},{28,32},{32,28... | collective-permute-start | bytes 786440 | tf_op jit(solution)/shard_map/ppermute | solution.py:34
  24.1 1.2 %shard_map.282.own_rows_ref = bf16[512,512]{1,0:T(8,128)(2,1)S(1)} custom-call(bf16[3,128,256]{2,1,0:T(8,128)(2,1)S(1)} %copy-done, bf16[3,128,256]{2,1,0:T(8,128)(2,1)S(1)} %collective-permute-done.own1_ref, bf16[3,128,256]{2,1,0:T(8,128)(2,1)S(1)} %collective-permute-done.1.own2_ref, bf16[3,128,256]{2,1,0:T(8,128)(2,1)S(1)} %collective-permute-done.2.own3_ref, ...), custom_call_target="tpu_custom_call" | custom-call | flops 671088640 | bytes 3145728 | tf_op jit(solution)/shard_map/pallas_call | solution.py:722
  25.4 3.0 %collective-permute-done.4.cross_ref = bf16[4,128,256]{2,1,0:T(8,128)(2,1)S(1)} collective-permute-done((bf16[4,128,256]{2,1,0:T(8,128)(2,1)S(1)}, bf16[4,128,256]{2,1,0:T(8,128)(2,1)S(1)}, u32[]{:S(2)}, u32[]{:S(2)}) %collective-permute-start.4) | collective-permute-done | bytes 262176 | tf_op jit(solution)/shard_map/ppermute | solution.py:34
  28.4 9.9 %shard_map.283 = (bf16[320,512]{1,0:T(8,128)(2,1)S(1)}, bf16[640,512]{1,0:T(8,128)(2,1)S(1)}, bf16[3,64,512]{2,1,0:T(8,128)(2,1)S(1)}, bf16[3,64,512]{2,1,0:T(8,...) custom-call(s32[1]{0:T(128)S(6)} %copy.31.live_ref, ...), custom_call_target="tpu_custom_call" | custom-call | flops 17179869184 | bytes 16777216 | tf_op jit(solution)/shard_map/pallas_call | solution.py:730
  38.4 0.8 copy-done.20
  39.2 7.6 %collective-permute-start.5 = (bf16[3,64,512]{2,1,0:T(8,128)(2,1)S(1)}, bf16[3,64,512]{2,1,0:T(8,128)(2,1)S(1)}, u32[]{:S(2)}, u32[]{:S(2)}) collective-permute-start(bf16[3,64,512]{2,1,0:T(8,128)(2,1)S(1)} %get-tuple-element.50), channel_id=1, source_target_pairs={{0,1},{1,0},{2,3},{3,2},{4,5},{5,4},{6,7},{7,6},{8,9},{9,8},{10,11... | collective-permute-start | bytes 589832 | tf_op jit(solution)/shard_map/ppermute | solution.py:21
  46.8 2.4 %collective-permute-start.7 = (bf16[3,64,512]{2,1,0:T(8,128)(2,1)S(1)}, bf16[3,64,512]{2,1,0:T(8,128)(2,1)S(1)}, u32[]{:S(2)}, u32[]{:S(2)}) collective-permute-start(bf16[3,64,512]{2,1,0:T(8,128)(2,1)S(1)} %get-tuple-element.52), channel_id=1, source_target_pairs={{0,3},{1,2},{2,1},{3,0},{4,7},{5,6},{6,5},{7,4},{8,11},{9,10},{10,... | collective-permute-start | bytes 589832 | tf_op jit(solution)/shard_map/ppermute | solution.py:21
  49.2 0.6 collective-permute-done.5.own1_hbm
  49.9 3.1 %collective-permute-done.6.own2_hbm = bf16[3,64,512]{2,1,0:T(8,128)(2,1)S(1)} collective-permute-done((bf16[3,64,512]{2,1,0:T(8,128)(2,1)S(1)}, bf16[3,64,512]{2,1,0:T(8,128)(2,1)S(1)}, u32[]{:S(2)}, u32[]{:S(2)}) %collective-permute-start.6) | collective-permute-done | bytes 196640 | tf_op jit(solution)/shard_map/ppermute | solution.py:21
  53.0 1.7 %collective-permute-done.7.own3_hbm = bf16[3,64,512]{2,1,0:T(8,128)(2,1)S(1)} collective-permute-done((bf16[3,64,512]{2,1,0:T(8,128)(2,1)S(1)}, bf16[3,64,512]{2,1,0:T(8,128)(2,1)S(1)}, u32[]{:S(2)}, u32[]{:S(2)}) %collective-permute-start.7) | collective-permute-done | bytes 196640 | tf_op jit(solution)/shard_map/ppermute | solution.py:21
  54.7 9.9 %collective-permute-start.8 = (bf16[4,64,512]{2,1,0:T(8,128)(2,1)S(1)}, bf16[4,64,512]{2,1,0:T(8,128)(2,1)S(1)}, u32[]{:S(2)}, u32[]{:S(2)}) collective-permute-start(bf16[4,64,512]{2,1,0:T(8,128)(2,1)S(1)} %pad_maximum_fusion.2), channel_id=1, source_target_pairs={{0,4},{4,0},{8,12},{12,8},{16,20},{20,16},{24,28},{28,24},{32,36},... | collective-permute-start | bytes 786440 | tf_op jit(solution)/shard_map/ppermute | solution.py:34
  64.8 7.5 %all-to-all-start = ((bf16[128,8,128]{2,1,0:T(8,128)(2,1)}), bf16[128,8,128]{2,1,0:T(8,128)(2,1)S(1)}, u32[]{:S(2)}, u32[]{:S(2)}) async-start(bf16[128,8,128]{2,1,0:T(8,128)(2,1)} %bitcast.6), calls=%async_computation | async-start | bytes 524288 | tf_op jit(solution)/shard_map/all_to_all | solution.py:773
  72.2 8.4 %shard_map.284 = (bf16[2560,512]{1,0:T(8,128)(2,1)}, f32[2560,128]{1,0:T(8,128)}) custom-call(s32[20,128]{1,0:T(8,128)} %bitcast.17, s32[20,128]{1,0:T(8,128)} %bitcast.18, bf16[640,512]{1,0:T(8,128)(2,1)} %copy-done.20, bf16[2560,512]{1,0:T(8,128)(2,1)} %lat_hbm.3, bf16[512,512]{1,0:T(8,128)(2,1)} %self_hbm.1), custom_call_target="tpu_custom_call" | custom-call | flops 2000000000 | bytes 8388608 | tf_op jit(solution)/shard_map/pallas_call | solution.py:781
  80.7 2.9 %all-to-all-done = bf16[128,8,128]{2,1,0:T(8,128)(2,1)S(1)} async-done(((bf16[128,8,128]{2,1,0:T(8,128)(2,1)}), bf16[128,8,128]{2,1,0:T(8,128)(2,1)S(1)}, u32[]{:S(2)}, u32[]{:S(2)}) %all-to-all-start) | async-done | bytes 262176 | tf_op jit(solution)/shard_map/all_to_all | solution.py:773
  83.6 0.7 copy-done.22
  84.4 0.1 copy-done.27
  84.5 13.2 %shard_map.285 = bf16[320,512]{1,0:T(8,128)(2,1)} custom-call(s32[20,128]{1,0:T(8,128)} %bitcast.19, bf16[1024,128]{1,0:T(8,128)(2,1)} %bitcast.15, bf16[320,512]{1,0:T(8,128)(2,1)} %copy-done.21, f32[1,512]{1,0:T(1,128)} %bitcast.20, bf16[2560,512]{1,0:T(8,128)(2,1)} %get-tuple-element.47.pre_hbm, f32[2560,128]{1,0:T(8,128)} %get-tuple-element.48.place_hbm, ...), custom_call_target="tpu_custom_call" | custom-call | flops 5368709120 | bytes 12582912 | tf_op jit(solution)/shard_map/pallas_call | solution.py:798
  (70 shorter events, 0.5 us)
Async XLA Ops:
  4.6 8.6 %collective-permute-start = (bf16[3,128,256]{2,1,0:T(8,128)(2,1)}, bf16[3,128,256]{2,1,0:T(8,128)(2,1)S(1)}, u32[]{:S(2)}, u32[]{:S(2)}) collective-permute-start(bf16[3,128,256]{2,1,0:T(8,128)(2,1)} %get-tuple-element.30), channel_id=1, source_target_pairs={{0,1},{1,0},{2,3},{3,2},{4,5},{5,4},{6,7},{7,6},{8,9},{9,8},{10,11... | collective-permute-start | bytes 589832 | tf_op jit(solution)/shard_map/ppermute | solution.py:21
  6.7 11.4 %collective-permute-start.1 = (bf16[3,128,256]{2,1,0:T(8,128)(2,1)}, bf16[3,128,256]{2,1,0:T(8,128)(2,1)S(1)}, u32[]{:S(2)}, u32[]{:S(2)}) collective-permute-start(bf16[3,128,256]{2,1,0:T(8,128)(2,1)} %get-tuple-element.31), channel_id=1, source_target_pairs={{0,2},{1,3},{2,0},{3,1},{4,6},{5,7},{6,4},{7,5},{8,10},{9,11},{10,... | collective-permute-start | bytes 589832 | tf_op jit(solution)/shard_map/ppermute | solution.py:21
  9.3 11.4 %collective-permute-start.2 = (bf16[3,128,256]{2,1,0:T(8,128)(2,1)}, bf16[3,128,256]{2,1,0:T(8,128)(2,1)S(1)}, u32[]{:S(2)}, u32[]{:S(2)}) collective-permute-start(bf16[3,128,256]{2,1,0:T(8,128)(2,1)} %get-tuple-element.32), channel_id=1, source_target_pairs={{0,3},{1,2},{2,1},{3,0},{4,7},{5,6},{6,5},{7,4},{8,11},{9,10},{10,... | collective-permute-start | bytes 589832 | tf_op jit(solution)/shard_map/ppermute | solution.py:21
  13.1 15.3 %copy-start.7 = (bf16[512,512]{1,0:T(8,128)(2,1)S(1)}, bf16[512,512]{1,0:T(8,128)(2,1)}, u32[]{:S(2)}) copy-start(bf16[512,512]{1,0:T(8,128)(2,1)} %msg_ref.1) | copy-start | bytes 1572868
  13.1 15.3 %copy-start.8 = (bf16[512,512]{1,0:T(8,128)(2,1)S(1)}, bf16[512,512]{1,0:T(8,128)(2,1)}, u32[]{:S(2)}) copy-start(bf16[512,512]{1,0:T(8,128)(2,1)} %node_agg_ref.1) | copy-start | bytes 1572868
  13.1 15.3 %copy-start.9 = (bf16[512,512]{1,0:T(8,128)(2,1)S(1)}, bf16[512,512]{1,0:T(8,128)(2,1)}, u32[]{:S(2)}) copy-start(bf16[512,512]{1,0:T(8,128)(2,1)} %node_out_ref.1) | copy-start | bytes 1572868
  13.1 15.3 %copy-start.10 = (bf16[512,512]{1,0:T(8,128)(2,1)S(1)}, bf16[512,512]{1,0:T(8,128)(2,1)}, u32[]{:S(2)}) copy-start(bf16[512,512]{1,0:T(8,128)(2,1)} %proc_send_ref.1) | copy-start | bytes 1572868
  13.2 15.3 %copy-start.11 = (bf16[512,512]{1,0:T(8,128)(2,1)S(1)}, bf16[512,512]{1,0:T(8,128)(2,1)}, u32[]{:S(2)}) copy-start(bf16[512,512]{1,0:T(8,128)(2,1)} %proc_recv_ref.1) | copy-start | bytes 1572868
  13.2 15.3 %copy-start.16 = (s32[3,4,64]{2,1,0:T(4,128)S(1)}, s32[3,4,64]{2,1,0:T(4,128)}, u32[]{:S(2)}) copy-start(s32[3,4,64]{2,1,0:T(4,128)} %near_ref.1) | copy-start | bytes 9220
  13.2 15.3 %copy-start.18 = (f32[512]{0:T(512)S(1)}, f32[512]{0:T(512)}, u32[]{:S(2)}) copy-start(f32[512]{0:T(512)} %param.51) | copy-start | bytes 6148
  13.2 15.3 %copy-start.19 = (s32[128,2]{0,1:T(2,128)S(1)}, s32[128,2]{0,1:T(2,128)}, u32[]{:S(2)}) copy-start(s32[128,2]{0,1:T(2,128)} %param.38) | copy-start | bytes 3076
  20.9 4.5 %collective-permute-start.3 = (bf16[4,128,256]{2,1,0:T(8,128)(2,1)S(1)}, bf16[4,128,256]{2,1,0:T(8,128)(2,1)S(1)}, u32[]{:S(2)}, u32[]{:S(2)}) collective-permute-start(bf16[4,128,256]{2,1,0:T(8,128)(2,1)S(1)} %pad_maximum_fusion), channel_id=1, source_target_pairs={{0,4},{4,0},{8,12},{12,8},{16,20},{20,16},{24,28},{28,24},{32,36},... | collective-permute-start | bytes 786440 | tf_op jit(solution)/shard_map/ppermute | solution.py:34
  22.5 5.9 %collective-permute-start.4 = (bf16[4,128,256]{2,1,0:T(8,128)(2,1)S(1)}, bf16[4,128,256]{2,1,0:T(8,128)(2,1)S(1)}, u32[]{:S(2)}, u32[]{:S(2)}) collective-permute-start(bf16[4,128,256]{2,1,0:T(8,128)(2,1)S(1)} %pad_maximum_fusion.1), channel_id=1, source_target_pairs={{0,124},{4,8},{8,4},{12,16},{16,12},{20,24},{24,20},{28,32},{32,28... | collective-permute-start | bytes 786440 | tf_op jit(solution)/shard_map/ppermute | solution.py:34
  39.2 15.4 %copy-start.21 = (bf16[320,512]{1,0:T(8,128)(2,1)}, bf16[320,512]{1,0:T(8,128)(2,1)S(1)}, u32[]{:S(2)}) copy-start(bf16[320,512]{1,0:T(8,128)(2,1)S(1)} %get-tuple-element.45.latent_ref) | copy-start | bytes 983044
  39.2 41.4 %copy-start.4 = (bf16[3,64,512]{2,1,0:T(8,128)(2,1)}, bf16[3,64,512]{2,1,0:T(8,128)(2,1)S(1)}, u32[]{:S(2)}) copy-start(bf16[3,64,512]{2,1,0:T(8,128)(2,1)S(1)} %get-tuple-element.49.own0_hbm) | copy-start | bytes 589828
  39.2 10.6 %collective-permute-start.5 = (bf16[3,64,512]{2,1,0:T(8,128)(2,1)S(1)}, bf16[3,64,512]{2,1,0:T(8,128)(2,1)S(1)}, u32[]{:S(2)}, u32[]{:S(2)}) collective-permute-start(bf16[3,64,512]{2,1,0:T(8,128)(2,1)S(1)} %get-tuple-element.50), channel_id=1, source_target_pairs={{0,1},{1,0},{2,3},{3,2},{4,5},{5,4},{6,7},{7,6},{8,9},{9,8},{10,11... | collective-permute-start | bytes 589832 | tf_op jit(solution)/shard_map/ppermute | solution.py:21
  46.8 6.1 %collective-permute-start.6 = (bf16[3,64,512]{2,1,0:T(8,128)(2,1)S(1)}, bf16[3,64,512]{2,1,0:T(8,128)(2,1)S(1)}, u32[]{:S(2)}, u32[]{:S(2)}) collective-permute-start(bf16[3,64,512]{2,1,0:T(8,128)(2,1)S(1)} %get-tuple-element.51), channel_id=1, source_target_pairs={{0,2},{1,3},{2,0},{3,1},{4,6},{5,7},{6,4},{7,5},{8,10},{9,11},{10,... | collective-permute-start | bytes 589832 | tf_op jit(solution)/shard_map/ppermute | solution.py:21
  46.8 7.8 %collective-permute-start.7 = (bf16[3,64,512]{2,1,0:T(8,128)(2,1)S(1)}, bf16[3,64,512]{2,1,0:T(8,128)(2,1)S(1)}, u32[]{:S(2)}, u32[]{:S(2)}) collective-permute-start(bf16[3,64,512]{2,1,0:T(8,128)(2,1)S(1)} %get-tuple-element.52), channel_id=1, source_target_pairs={{0,3},{1,2},{2,1},{3,0},{4,7},{5,6},{6,5},{7,4},{8,11},{9,10},{10,... | collective-permute-start | bytes 589832 | tf_op jit(solution)/shard_map/ppermute | solution.py:21
  49.9 30.8 %copy-start.23 = (bf16[3,64,512]{2,1,0:T(8,128)(2,1)}, bf16[3,64,512]{2,1,0:T(8,128)(2,1)S(1)}, u32[]{:S(2)}) copy-start(bf16[3,64,512]{2,1,0:T(8,128)(2,1)S(1)} %collective-permute-done.5.own1_hbm) | copy-start | bytes 589828
  52.9 27.7 %copy-start.24 = (bf16[3,64,512]{2,1,0:T(8,128)(2,1)}, bf16[3,64,512]{2,1,0:T(8,128)(2,1)S(1)}, u32[]{:S(2)}) copy-start(bf16[3,64,512]{2,1,0:T(8,128)(2,1)S(1)} %collective-permute-done.6.own2_hbm) | copy-start | bytes 589828
  54.7 26.0 %copy-start.25 = (bf16[3,64,512]{2,1,0:T(8,128)(2,1)}, bf16[3,64,512]{2,1,0:T(8,128)(2,1)S(1)}, u32[]{:S(2)}) copy-start(bf16[3,64,512]{2,1,0:T(8,128)(2,1)S(1)} %collective-permute-done.7.own3_hbm) | copy-start | bytes 589828
  54.7 28.9 %collective-permute-start.8 = (bf16[4,64,512]{2,1,0:T(8,128)(2,1)S(1)}, bf16[4,64,512]{2,1,0:T(8,128)(2,1)S(1)}, u32[]{:S(2)}, u32[]{:S(2)}) collective-permute-start(bf16[4,64,512]{2,1,0:T(8,128)(2,1)S(1)} %pad_maximum_fusion.2), channel_id=1, source_target_pairs={{0,4},{4,0},{8,12},{12,8},{16,20},{20,16},{24,28},{28,24},{32,36},... | collective-permute-start | bytes 786440 | tf_op jit(solution)/shard_map/ppermute | solution.py:34
  64.7 18.9 %collective-permute-start.9 = (bf16[4,64,512]{2,1,0:T(8,128)(2,1)S(1)}, bf16[4,64,512]{2,1,0:T(8,128)(2,1)S(1)}, u32[]{:S(2)}, u32[]{:S(2)}) collective-permute-start(bf16[4,64,512]{2,1,0:T(8,128)(2,1)S(1)} %pad_maximum_fusion.3), channel_id=1, source_target_pairs={{0,124},{4,8},{8,4},{12,16},{16,12},{20,24},{24,20},{28,32},{32,28... | collective-permute-start | bytes 786440 | tf_op jit(solution)/shard_map/ppermute | solution.py:34
  64.8 18.8 %all-to-all-start = ((bf16[128,8,128]{2,1,0:T(8,128)(2,1)}), bf16[128,8,128]{2,1,0:T(8,128)(2,1)S(1)}, u32[]{:S(2)}, u32[]{:S(2)}) async-start(bf16[128,8,128]{2,1,0:T(8,128)(2,1)} %bitcast.6), calls=%async_computation | async-start | bytes 524288 | tf_op jit(solution)/shard_map/all_to_all | solution.py:773
  (15 other events, 126.2 us)

commit v4 on v3

--- a/solution.py
+++ b/solution.py
@@ -12,8 +12,8 @@
 PAIR = 2 * EDGE_BLOCK
 VMEM_BYTES = 24 * 1024 * 1024
 VMEM_ALL = 60 * 1024 * 1024
-START_FLOPS = 2 * 10**9
-START_BYTES = 8 << 20
+START_FLOPS = 4 * 10**9
+START_BYTES = 16 << 20
 
 
 def sub_swap(value, step):
@@ -25,13 +25,14 @@
     return band ^ 1
 
 
-def cross(band, count):
-    return (((band + 1) ^ 1) - 1) % count
+def cross(band):
+    return ((band + 1) ^ 1) - 1
 
 
 def band_swap(value, partner):
     count = lax.axis_size("band")
-    return lax.ppermute(value, "band", [(b, partner(b)) for b in range(count)])
+    pairs = [(b, partner(b)) for b in range(count)]
+    return lax.ppermute(value, "band", [(b, other) for b, other in pairs if 0 <= other < count])
 
 
 def offsets():
@@ -343,17 +344,18 @@
     _, mate_place, cross_place = sources()
     table_ref[pl.ds(pl.multiple_of(start + chunk, chunk), chunk), :] = own_rows_ref[...]
 
-    def encode(ref, offset):
-        sent = encode_rows(ref[...].reshape(chunk, wide), enc_in, weight(0)[...], weight(1)[...])
+    sent = encode_rows(
+        jnp.concatenate([ref[...].reshape(chunk, wide) for ref in (mate_ref, cross_ref)], axis=0),
+        enc_in,
+        weight(0)[...],
+        weight(1)[...],
+    )
+    firsts = (start + mate_place * chunk, jnp.where(polar, 2, cross_place) * chunk)
+    for w, first in enumerate(firsts):
         for k in range(subs):
-            place = pl.multiple_of(start + offset * chunk + (me ^ k) * cap, cap)
-            table_ref[pl.ds(place, cap), :] = sent[k * cap : (k + 1) * cap]
-
-    encode(mate_ref, mate_place)
-
-    @pl.when(jnp.logical_not(polar))
-    def _():
-        encode(cross_ref, cross_place)
+            place = pl.multiple_of(first + (me ^ k) * cap, cap)
+            from_row = (w * subs + k) * cap
+            table_ref[pl.ds(place, cap), :] = sent[from_row : from_row + cap]
 
     sum_ref[...] = jnp.zeros_like(sum_ref)
 
@@ -393,7 +395,8 @@
     total = sum_ref[...]
     high = half(total)
     low = half(total - high.astype(jnp.float32))
-    inflow = half(dot(high, weight(2)[...]) + dot(low, weight(2)[...]))
+    both = dot(jnp.concatenate([high, low], axis=0), weight(2)[...])
+    inflow = half(both[0:mesh_rows] + both[mesh_rows:])
     embed = embed_ref[...]
     node_act = half(silu(node_ref[...] + dot(inflow, weight(3)[...])))
     mesh_latent = half(
@@ -409,25 +412,29 @@
     )
     near = near_ref.shape[2]
     shares = offsets()
-    for k, out_ref in enumerate((out0_ref, out1_ref, out2_ref, out3_ref)):
-        index = [near_ref[offset, pl.ds(me ^ k, 1), :] for offset in shares]
-        index.append(jnp.zeros((1, 4 * near - 3 * near), jnp.int32))
-        index = jnp.concatenate(index, axis=1)
-        onehot = jnp.concatenate(
-            [
-                picks(column(index[:, first : first + LANES]), padded)
-                for first in range(0, 4 * near, LANES)
-            ],
-            axis=0,
-        )
-        out_ref[...] = half(dot(onehot[0 : 3 * near], sender_pad)).reshape(out_ref.shape)
+    outs = (out0_ref, out1_ref, out2_ref, out3_ref)
+    index = jnp.concatenate(
+        [near_ref[offset, pl.ds(me ^ k, 1), :] for k in range(subs) for offset in shares]
+        + [far_ref[c : c + 1, :] for c in range(far_ref.shape[0])],
+        axis=1,
+    )
+    onehot = jnp.concatenate(
+        [
+            picks(column(index[:, first : first + LANES]), padded)
+            for first in range(0, index.shape[1], LANES)
+        ],
+        axis=0,
+    )
+    leaving = dot(onehot, sender_pad)
+    for k, out_ref in enumerate(outs):
+        out_ref[...] = half(leaving[3 * near * k : 3 * near * (k + 1)]).reshape(out_ref.shape)
     lanes = latent // LANES
-    spread = far_ref.shape[0] * lanes
+    spread_rows = far_ref.shape[0] * lanes
     for c in range(far_ref.shape[0]):
-        rows = dot(picks(column(far_ref[c : c + 1, :]), padded), sender_pad)
+        first = 3 * near * subs + c * LANES
         for j in range(lanes):
-            flat_ref[pl.ds(c * lanes + j, LANES, stride=spread), :] = rows[
-                :, j * LANES : (j + 1) * LANES
+            flat_ref[pl.ds(c * lanes + j, LANES, stride=spread_rows), :] = leaving[
+                first : first + LANES, j * LANES : (j + 1) * LANES
             ]
     out_far_ref[...] = half(flat_ref[...])
 
@@ -435,11 +442,12 @@
 def edge_start_kernel(
     src_ref,
     dst_ref,
-    pair_ref,
+    pair_hbm,
     lat_hbm,
     self_hbm,
     pre_hbm,
     place_hbm,
+    pair_ref,
     lat_ref,
     self_ref,
     pre_ref,
@@ -451,63 +459,63 @@
     subs = lax.axis_size("sub")
     devices = lax.axis_size("band") * subs
     near_total = 3 * subs * (LANES // 2)
-    blocks = lat_ref.shape[0] // EDGE_BLOCK
-    per = EDGE_BLOCK // LANES
-    spans = [pl.ds(block * EDGE_BLOCK, EDGE_BLOCK) for block in range(blocks)]
-    weight = pltpu.make_async_copy(self_hbm, self_ref, read_sems.at[blocks])
+    edges = lat_ref.shape[0]
+    halves = [pl.ds(first, edges // 2) for first in (0, edges // 2)]
+    pairs = pltpu.make_async_copy(pair_hbm, pair_ref, read_sems.at[3])
+    weight = pltpu.make_async_copy(self_hbm, self_ref, read_sems.at[2])
     reads = [
         pltpu.make_async_copy(lat_hbm.at[span], lat_ref.at[span], read_sems.at[k])
-        for k, span in enumerate(spans)
+        for k, span in enumerate(halves)
     ]
-    writes = []
-    for copy in [weight, *reads]:
+    for copy in [pairs, weight, *reads]:
         copy.start()
-    places = [index_entry(0), index_entry(2), index_entry(4)]
-    for block, span in enumerate(spans):
-        source = row_of(src_ref, block * per, per)
-        target = row_of(dst_ref, block * per, per)
-        other = source - mesh_rows
-        far = other - near_total
-        far = near_total + (far & 1) * devices + (far >> 1)
-        rows = jnp.concatenate(
-            digits(jnp.where(source < mesh_rows, source, -1))
-            + digits(target + mesh_rows)
-            + digits(jnp.where(other < near_total, other, far))
-            + [jnp.zeros((2, EDGE_BLOCK), jnp.float32)],
-            axis=0,
+    source = row_of(src_ref, 0, edges // LANES)
+    target = row_of(dst_ref, 0, edges // LANES)
+    other = source - mesh_rows
+    far = other - near_total
+    far = near_total + (far & 1) * devices + (far >> 1)
+    rows = jnp.concatenate(
+        digits(jnp.where(source < mesh_rows, source, -1))
+        + digits(target + mesh_rows)
+        + digits(jnp.where(other < near_total, other, far))
+        + [jnp.zeros((2, edges), jnp.float32)],
+        axis=0,
+    )
+    wide = spread(rows, [index_entry(0), index_entry(2), index_entry(4)])
+    own, mine = wide[:, 0:LANES], wide[:, LANES : 2 * LANES]
+    place_ref[...] = wide[:, 2 * LANES :]
+    writes = [pltpu.make_async_copy(place_ref, place_hbm, write_sems.at[2])]
+    writes[0].start()
+    lane = lanes_of(own)
+    parts = []
+    for first in range(0, 2 * mesh_rows, LANES):
+        hit = None
+        if first < mesh_rows:
+            hit = own == lane + float(first)
+        if first + LANES > mesh_rows:
+            match = mine == lane + float(first)
+            hit = match if hit is None else hit | match
+        parts.append(half(jnp.where(hit, 1.0, 0.0)))
+    onehot = jnp.concatenate(parts, axis=1)
+    pairs.wait()
+    weight.wait()
+    for k, span in enumerate(halves):
+        picked = dot(onehot[k * (edges // 2) : (k + 1) * (edges // 2)], pair_ref[...])
+        reads[k].wait()
+        pre_ref[span, :] = half(picked + dot(lat_ref[span, :], self_ref[...]))
+        writes.append(
+            pltpu.make_async_copy(pre_ref.at[span], pre_hbm.at[span], write_sems.at[k])
         )
-        wide = spread(rows, places)
-        own, mine = wide[:, 0:LANES], wide[:, LANES : 2 * LANES]
-        place_ref[span, :] = wide[:, 2 * LANES :]
-        lane = lanes_of(own)
-        parts = []
-        for first in range(0, 2 * mesh_rows, LANES):
-            hit = None
-            if first < mesh_rows:
-                hit = own == lane + float(first)
-            if first + LANES > mesh_rows:
-                match = mine == lane + float(first)
-                hit = match if hit is None else hit | match
-            parts.append(half(jnp.where(hit, 1.0, 0.0)))
-        picked = dot(jnp.concatenate(parts, axis=1), pair_ref[...])
-        if block == 0:
-            weight.wait()
-        reads[block].wait()
-        pre_ref[span, :] = half(picked + dot(lat_ref[span, :], self_ref[...]))
-        for j, (ref, hbm) in enumerate(((pre_ref, pre_hbm), (place_ref, place_hbm))):
-            writes.append(
-                pltpu.make_async_copy(ref.at[span], hbm.at[span], write_sems.at[2 * block + j])
-            )
-            writes[-1].start()
+        writes[-1].start()
     for copy in writes:
         copy.wait()
 
 
 def edge_finish_kernel(
     dst_ref,
-    far_ref,
-    latent_ref,
     gain_ref,
+    far_hbm,
+    latent_hbm,
     pre_hbm,
     place_hbm,
     lat_hbm,
@@ -522,6 +530,8 @@
     upd_agg_ref,
     upd_out_ref,
     out_ref,
+    far_ref,
+    latent_ref,
     table_ref,
     flat_ref,
     new_ref,
@@ -534,8 +544,9 @@
     block_sems,
 ):
     mesh_rows, latent = latent_ref.shape
-    blocks = lat_ref.shape[0] // EDGE_BLOCK
-    spans = [pl.ds(block * EDGE_BLOCK, EDGE_BLOCK) for block in range(blocks)]
+    blocks = 2
+    block_rows = lat_ref.shape[0] // blocks
+    spans = [pl.ds(block * block_rows, block_rows) for block in range(blocks)]
     subs, near, _ = mate_hbm.shape
     near_total = 3 * subs * near
     me = lax.axis_index("sub")
@@ -558,14 +569,18 @@
         ]
         for k, span in enumerate(spans)
     ]
-    for copy in rows + reads[0]:
+    far_read = pltpu.make_async_copy(far_hbm, far_ref, sems.at[4])
+    latent_read = pltpu.make_async_copy(latent_hbm, latent_ref, sems.at[5])
+    for copy in [far_read, *rows, reads[0][1], reads[0][0], latent_read]:
         copy.start()
     weight = Fetch((edge_out_ref, upd_self_ref, upd_agg_ref, upd_out_ref), slots_ref, sems)
+    reads[0][2].start()
     for block in reads[1:]:
         for copy in block:
             copy.start()
     lanes = latent // LANES
     devices = far_ref.shape[0] // (2 * lanes)
+    far_read.wait()
     flat_ref[...] = far_ref[...].astype(jnp.float32)
     for c in range(2):
         table_ref[pl.ds(near_total + c * devices, devices), :] = half(
@@ -580,6 +595,7 @@
     for copy in rows:
         copy.wait()
     edge_out = weight(0)[...]
+    latent_read.wait()
     upd_self = dot(latent_ref[...], weight(1)[...])
 
     def gathered(block):
@@ -658,10 +674,7 @@
 
     def across_bands(arrived):
         mates = band_swap(jnp.stack([part[1] for part in arrived]), mate)
-        crosses = band_swap(
-            jnp.stack([part[2] for part in arrived]),
-            functools.partial(cross, count=lax.axis_size("band")),
-        )
+        crosses = band_swap(jnp.stack([part[2] for part in arrived]), cross)
         return mates, crosses
 
     def shape(*dims, dtype=bf16):
@@ -770,6 +783,7 @@
     )
 
     near_arrived = across_subs(near_parts)
+    near_arrived[1], far_out = lax.optimization_barrier((near_arrived[1], far_out))
     far_rows = lax.all_to_all(
         far_out.reshape(devices, -1, LANES),
         ("band", "sub"),
@@ -781,14 +795,15 @@
     pre, mesh_place = local_call(
         edge_start_kernel,
         (shape(mesh_edges, latent), shape(mesh_edges, LANES, dtype=f32)),
-        [whole()] * 3 + [in_hbm()] * 2,
+        [whole()] * 2 + [in_hbm()] * 3,
         scratch=[
+            pltpu.VMEM((2 * mesh_rows, latent), bf16),
             pltpu.VMEM((mesh_edges, latent), bf16),
             pltpu.VMEM((latent, latent), bf16),
             pltpu.VMEM((mesh_edges, latent), bf16),
             pltpu.VMEM((mesh_edges, LANES), f32),
-            pltpu.SemaphoreType.DMA((blocks + 1,)),
-            pltpu.SemaphoreType.DMA((2 * blocks,)),
+            pltpu.SemaphoreType.DMA((4,)),
+            pltpu.SemaphoreType.DMA((3,)),
         ],
         flops=START_FLOPS,
         nbytes=START_BYTES,
@@ -798,8 +813,10 @@
     return local_call(
         edge_finish_kernel,
         shape(mesh_rows, latent),
-        [whole()] * 4 + [in_hbm()] * 13,
+        [whole()] * 2 + [in_hbm()] * 15,
         scratch=[
+            pltpu.VMEM(far_rows.shape, bf16),
+            pltpu.VMEM((mesh_rows, latent), bf16),
             pltpu.VMEM((others, latent), bf16),
             pltpu.VMEM((far_total * latent // LANES, LANES), f32),
             pltpu.VMEM((mesh_edges, latent), bf16),
@@ -807,7 +824,7 @@
             pltpu.VMEM((mesh_edges, LANES), f32),
             pltpu.VMEM((mesh_edges, latent), bf16),
             pltpu.VMEM((4, latent, latent), bf16),
-            pltpu.SemaphoreType.DMA((4,)),
+            pltpu.SemaphoreType.DMA((6,)),
             pltpu.SemaphoreType.DMA((3 * sub_count,)),
             pltpu.SemaphoreType.DMA((3 * blocks,)),
         ],
@@ -816,9 +833,9 @@
         vmem=VMEM_ALL,
     )(
         mesh_dst,
+        out_gain.reshape(1, latent),
         far_rows,
         mesh_latent,
-        out_gain.reshape(1, latent),
         pre,
         mesh_place,
         mesh_edge_lat,

time: 98 us -> 91.3 us (0.932)
  the two profiles are of different devices: /device:TPU:1 before, /device:TPU:6 now
where the time goes in v4:
time: 91.3 us; the launch traced here: 90.3 us
  Pallas kernels  45.6 us (50%)
  starting transfers between devices  31.4 us (34%)
  waiting for transfers between devices  9.21 us (10%)
  local copies, waits for them, and re-layouts  2.61 us (3%)
  between operations  1.34 us (1%)
    pallas_call x1, Pallas kernels, body(): local_call(encoder_kernel, (shape(mesh_rows, latent), shape(2 * mesh_rows...  14.4 us
    pallas_call x1, Pallas kernels, body(): local_call(edge_finish_kernel, shape(mesh_rows, latent), [whole()] * 2 +...  12.7 us
    ppermute x4, starting transfers between devices, band_swap(): lax.ppermute(value, 'band', [(b, other) for b, other in pairs if 0 <= oth...  12.2 us
    all_to_all x1, starting transfers between devices, body(): lax.all_to_all(far_out.reshape(devices, -1, LANES), ('band', 'sub'), spli...  9.83 us
    ppermute x6, starting transfers between devices, sub_swap(): return lax.ppermute(value, 'sub', [(t, t ^ step) for t in range(count)])  9.39 us
    pallas_call x1, Pallas kernels, body(): local_call(edge_start_kernel, (shape(mesh_edges, latent), shape(mesh_edge...  7.3 us
    ppermute x6, waiting for transfers between devices, sub_swap(): return lax.ppermute(value, 'sub', [(t, t ^ step) for t in range(count)])  6.4 us
    pallas_call x1, Pallas kernels, body(): local_call(prepare_grid_kernel, (shape(edges, LANES, dtype=f32), shape(ed...  5.45 us
  transfers between devices with their start and end apart: 11, of which 4 were waited for; matrix products, arithmetic and copies ran while one was open for 0% of the time, Pallas kernels for 15%

profile of v4, /device:TPU:6, one launch (start us, length us, event | category | flops | bytes accessed | tf_op | source)
XLA Modules:
  0.0 90.3 jit_solution(13791435986383757651)
XLA Ops:
  0.0 4.5 %shard_map.280 = (bf16[3,128,256]{2,1,0:T(8,128)(2,1)}, bf16[3,128,256]{2,1,0:T(8,128)(2,1)}, bf16[3,128,256]{2,1,0:T(8,128)(2,1)}, bf16[3,128,256]{2,1,0:T(8,128)(2,1)}) custom-call(s32[3,4,128]{2,1,0:T(4,128)} %send_ref.1, bf16[227,2048]{1,0:T(8,128)(2,1)} %bitcast.16), custom_call_target="tpu_custom_call" | custom-call | flops 1610612736 | bytes 1835008 | tf_op jit(solution)/shard_map/pallas_call | solution.py:685
  4.6 1.6 %collective-permute-start = (bf16[3,128,256]{2,1,0:T(8,128)(2,1)}, bf16[3,128,256]{2,1,0:T(8,128)(2,1)S(1)}, u32[]{:S(2)}, u32[]{:S(2)}) collective-permute-start(bf16[3,128,256]{2,1,0:T(8,128)(2,1)} %get-tuple-element.32), channel_id=1, source_target_pairs={{0,1},{1,0},{2,3},{3,2},{4,5},{5,4},{6,7},{7,6},{8,9},{9,8},{10,11... | collective-permute-start | bytes 589832 | tf_op jit(solution)/shard_map/ppermute | solution.py:21
  6.2 2.9 %collective-permute-start.1 = (bf16[3,128,256]{2,1,0:T(8,128)(2,1)}, bf16[3,128,256]{2,1,0:T(8,128)(2,1)S(1)}, u32[]{:S(2)}, u32[]{:S(2)}) collective-permute-start(bf16[3,128,256]{2,1,0:T(8,128)(2,1)} %get-tuple-element.33), channel_id=1, source_target_pairs={{0,2},{1,3},{2,0},{3,1},{4,6},{5,7},{6,4},{7,5},{8,10},{9,11},{10,... | collective-permute-start | bytes 589832 | tf_op jit(solution)/shard_map/ppermute | solution.py:21
  9.1 0.2 collective-permute-start.2
  10.1 5.4 %shard_map.281 = (f32[8192,128]{1,0:T(8,128)S(1)}, bf16[8192,512]{1,0:T(8,128)(2,1)S(1)}, f32[320,512]{1,0:T(8,128)S(1)}) custom-call(s32[1]{0:T(128)S(6)} %copy.31.live_ref, s32[64,128]{1,0:T(8,128)S(1)} %bitcast.10, s32[64,128]{1,0:T(8,128)S(1)} %bitcast.11, bf16[4,8192]{1,0:T(4,128)(2,1)S(1)} %copy-done.13, bf16[320,512]{1,0:T(8,128)(2,1)S(1)} %copy-done.12, ...), custom_call_target="tpu_custom_call" | custom-call | flops 8589934592 | bytes 16777216 | tf_op jit(solution)/shard_map/pallas_call | solution.py:711
  15.6 2.6 %collective-permute-done.1.own2_ref = bf16[3,128,256]{2,1,0:T(8,128)(2,1)S(1)} collective-permute-done((bf16[3,128,256]{2,1,0:T(8,128)(2,1)}, bf16[3,128,256]{2,1,0:T(8,128)(2,1)S(1)}, u32[]{:S(2)}, u32[]{:S(2)}) %collective-permute-start.1) | collective-permute-done | bytes 196640 | tf_op jit(solution)/shard_map/ppermute | solution.py:21
  18.2 2.6 %collective-permute-done.2.own3_ref = bf16[3,128,256]{2,1,0:T(8,128)(2,1)S(1)} collective-permute-done((bf16[3,128,256]{2,1,0:T(8,128)(2,1)}, bf16[3,128,256]{2,1,0:T(8,128)(2,1)S(1)}, u32[]{:S(2)}, u32[]{:S(2)}) %collective-permute-start.2) | collective-permute-done | bytes 196640 | tf_op jit(solution)/shard_map/ppermute | solution.py:21
  20.9 0.1 collective-permute-start.3
  21.0 6.3 %collective-permute-start.4 = (bf16[4,128,256]{2,1,0:T(8,128)(2,1)S(1)}, bf16[4,128,256]{2,1,0:T(8,128)(2,1)S(1)}, u32[]{:S(2)}, u32[]{:S(2)}) collective-permute-start(bf16[4,128,256]{2,1,0:T(8,128)(2,1)S(1)} %pad_maximum_fusion.1), channel_id=1, source_target_pairs={{4,8},{8,4},{12,16},{16,12},{20,24},{24,20},{28,32},{32,28},{36,40... | collective-permute-start | bytes 786440 | tf_op jit(solution)/shard_map/ppermute | solution.py:35
  27.4 1.2 %shard_map.282.own_rows_ref = bf16[512,512]{1,0:T(8,128)(2,1)S(1)} custom-call(bf16[3,128,256]{2,1,0:T(8,128)(2,1)S(1)} %copy-done, bf16[3,128,256]{2,1,0:T(8,128)(2,1)S(1)} %collective-permute-done.own1_ref, bf16[3,128,256]{2,1,0:T(8,128)(2,1)S(1)} %collective-permute-done.1.own2_ref, bf16[3,128,256]{2,1,0:T(8,128)(2,1)S(1)} %collective-permute-done.2.own3_ref, ...), custom_call_target="tpu_custom_call" | custom-call | flops 671088640 | bytes 3145728 | tf_op jit(solution)/shard_map/pallas_call | solution.py:735
  28.6 2.8 %collective-permute-done.4.cross_ref = bf16[4,128,256]{2,1,0:T(8,128)(2,1)S(1)} collective-permute-done((bf16[4,128,256]{2,1,0:T(8,128)(2,1)S(1)}, bf16[4,128,256]{2,1,0:T(8,128)(2,1)S(1)}, u32[]{:S(2)}, u32[]{:S(2)}) %collective-permute-start.4) | collective-permute-done | bytes 262176 | tf_op jit(solution)/shard_map/ppermute | solution.py:35
  31.4 14.4 %shard_map.283 = (bf16[320,512]{1,0:T(8,128)(2,1)S(1)}, bf16[640,512]{1,0:T(8,128)(2,1)S(1)}, bf16[3,64,512]{2,1,0:T(8,128)(2,1)S(1)}, bf16[3,64,512]{2,1,0:T(8,...) custom-call(s32[1]{0:T(128)S(6)} %copy.31.live_ref, ...), custom_call_target="tpu_custom_call" | custom-call | flops 17179869184 | bytes 16777216 | tf_op jit(solution)/shard_map/pallas_call | solution.py:743
  45.9 0.8 copy-done.20
  46.7 0.7 copy-done.21
  47.5 4.7 %collective-permute-start.7 = (bf16[3,64,512]{2,1,0:T(8,128)(2,1)S(1)}, bf16[3,64,512]{2,1,0:T(8,128)(2,1)S(1)}, u32[]{:S(2)}, u32[]{:S(2)}) collective-permute-start(bf16[3,64,512]{2,1,0:T(8,128)(2,1)S(1)} %get-tuple-element.56), channel_id=1, source_target_pairs={{0,3},{1,2},{2,1},{3,0},{4,7},{5,6},{6,5},{7,4},{8,11},{9,10},{10,... | collective-permute-start | bytes 589832 | tf_op jit(solution)/shard_map/ppermute | solution.py:21
  52.2 1.2 %collective-permute-done.5.own1_hbm = bf16[3,64,512]{2,1,0:T(8,128)(2,1)S(1)} collective-permute-done((bf16[3,64,512]{2,1,0:T(8,128)(2,1)S(1)}, bf16[3,64,512]{2,1,0:T(8,128)(2,1)S(1)}, u32[]{:S(2)}, u32[]{:S(2)}) %collective-permute-start.5) | collective-permute-done | bytes 196640 | tf_op jit(solution)/shard_map/ppermute | solution.py:21
  53.4 9.8 %all-to-all-start = ((bf16[128,8,128]{2,1,0:T(8,128)(2,1)}), bf16[128,8,128]{2,1,0:T(8,128)(2,1)S(1)}, u32[]{:S(2)}, u32[]{:S(2)}) async-start(bf16[128,8,128]{2,1,0:T(8,128)(2,1)} %bitcast.7), calls=%async_computation | async-start | bytes 524288 | tf_op jit(solution)/shard_map/all_to_all | solution.py:787
  63.4 0.2 collective-permute-start.8
  63.7 5.5 %collective-permute-start.9 = (bf16[4,64,512]{2,1,0:T(8,128)(2,1)S(1)}, bf16[4,64,512]{2,1,0:T(8,128)(2,1)S(1)}, u32[]{:S(2)}, u32[]{:S(2)}) collective-permute-start(bf16[4,64,512]{2,1,0:T(8,128)(2,1)S(1)} %pad_maximum_fusion.3), channel_id=1, source_target_pairs={{4,8},{8,4},{12,16},{16,12},{20,24},{24,20},{28,32},{32,28},{36,40... | collective-permute-start | bytes 786440 | tf_op jit(solution)/shard_map/ppermute | solution.py:35
  69.2 7.3 %shard_map.284 = (bf16[2560,512]{1,0:T(8,128)(2,1)}, f32[2560,128]{1,0:T(8,128)}) custom-call(s32[20,128]{1,0:T(8,128)} %bitcast.17, s32[20,128]{1,0:T(8,128)} %bitcast.18, bf16[640,512]{1,0:T(8,128)(2,1)} %copy-done.20, bf16[2560,512]{1,0:T(8,128)(2,1)} %lat_hbm.3, bf16[512,512]{1,0:T(8,128)(2,1)} %self_hbm.1), custom_call_target="tpu_custom_call" | custom-call | flops 4000000000 | bytes 16777216 | tf_op jit(solution)/shard_map/pallas_call | solution.py:795
  76.6 0.6 copy-done.22
  77.3 0.1 copy-done.26
  77.3 0.1 copy-done.27
  77.5 12.7 %shard_map.285 = bf16[320,512]{1,0:T(8,128)(2,1)} custom-call(s32[20,128]{1,0:T(8,128)} %bitcast.19, f32[1,512]{1,0:T(1,128)} %bitcast.20, bf16[1024,128]{1,0:T(8,128)(2,1)} %bitcast.15, bf16[320,512]{1,0:T(8,128)(2,1)} %copy-done.21, bf16[2560,512]{1,0:T(8,128)(2,1)} %get-tuple-element.51.pre_hbm, f32[2560,128]{1,0:T(8,128)} %get-tuple-element.52.place_hbm, ...), custom_call_target="tpu_custom_call" | custom-call | flops 5368709120 | bytes 12582912 | tf_op jit(solution)/shard_map/pallas_call | solution.py:813
  (70 shorter events, 0.4 us)
Async XLA Ops:
  4.6 11.0 %collective-permute-start = (bf16[3,128,256]{2,1,0:T(8,128)(2,1)}, bf16[3,128,256]{2,1,0:T(8,128)(2,1)S(1)}, u32[]{:S(2)}, u32[]{:S(2)}) collective-permute-start(bf16[3,128,256]{2,1,0:T(8,128)(2,1)} %get-tuple-element.32), channel_id=1, source_target_pairs={{0,1},{1,0},{2,3},{3,2},{4,5},{5,4},{6,7},{7,6},{8,9},{9,8},{10,11... | collective-permute-start | bytes 589832 | tf_op jit(solution)/shard_map/ppermute | solution.py:21
  6.2 12.0 %collective-permute-start.1 = (bf16[3,128,256]{2,1,0:T(8,128)(2,1)}, bf16[3,128,256]{2,1,0:T(8,128)(2,1)S(1)}, u32[]{:S(2)}, u32[]{:S(2)}) collective-permute-start(bf16[3,128,256]{2,1,0:T(8,128)(2,1)} %get-tuple-element.33), channel_id=1, source_target_pairs={{0,2},{1,3},{2,0},{3,1},{4,6},{5,7},{6,4},{7,5},{8,10},{9,11},{10,... | collective-permute-start | bytes 589832 | tf_op jit(solution)/shard_map/ppermute | solution.py:21
  9.1 11.7 %collective-permute-start.2 = (bf16[3,128,256]{2,1,0:T(8,128)(2,1)}, bf16[3,128,256]{2,1,0:T(8,128)(2,1)S(1)}, u32[]{:S(2)}, u32[]{:S(2)}) collective-permute-start(bf16[3,128,256]{2,1,0:T(8,128)(2,1)} %get-tuple-element.34), channel_id=1, source_target_pairs={{0,3},{1,2},{2,1},{3,0},{4,7},{5,6},{6,5},{7,4},{8,11},{9,10},{10,... | collective-permute-start | bytes 589832 | tf_op jit(solution)/shard_map/ppermute | solution.py:21
  10.0 17.3 %copy-start.1 = (bf16[512,512]{1,0:T(8,128)(2,1)S(1)}, bf16[512,512]{1,0:T(8,128)(2,1)}, u32[]{:S(2)}) copy-start(bf16[512,512]{1,0:T(8,128)(2,1)} %enc_out_ref.3) | copy-start | bytes 1572868
  10.0 17.3 %copy-start.2 = (bf16[512,512]{1,0:T(8,128)(2,1)S(1)}, bf16[512,512]{1,0:T(8,128)(2,1)}, u32[]{:S(2)}) copy-start(bf16[512,512]{1,0:T(8,128)(2,1)} %send_proj_ref.3) | copy-start | bytes 1572868
  10.1 17.3 %copy-start.3 = (bf16[227,512]{1,0:T(8,128)(2,1)S(1)}, bf16[227,512]{1,0:T(8,128)(2,1)}, u32[]{:S(2)}) copy-start(bf16[227,512]{1,0:T(8,128)(2,1)} %enc_in_ref.3) | copy-start | bytes 697348
  15.5 15.9 %copy-start.7 = (bf16[512,512]{1,0:T(8,128)(2,1)S(1)}, bf16[512,512]{1,0:T(8,128)(2,1)}, u32[]{:S(2)}) copy-start(bf16[512,512]{1,0:T(8,128)(2,1)} %msg_ref.1) | copy-start | bytes 1572868
  15.5 15.9 %copy-start.8 = (bf16[512,512]{1,0:T(8,128)(2,1)S(1)}, bf16[512,512]{1,0:T(8,128)(2,1)}, u32[]{:S(2)}) copy-start(bf16[512,512]{1,0:T(8,128)(2,1)} %node_agg_ref.1) | copy-start | bytes 1572868
  15.5 15.8 %copy-start.9 = (bf16[512,512]{1,0:T(8,128)(2,1)S(1)}, bf16[512,512]{1,0:T(8,128)(2,1)}, u32[]{:S(2)}) copy-start(bf16[512,512]{1,0:T(8,128)(2,1)} %node_out_ref.1) | copy-start | bytes 1572868
  15.6 15.8 %copy-start.10 = (bf16[512,512]{1,0:T(8,128)(2,1)S(1)}, bf16[512,512]{1,0:T(8,128)(2,1)}, u32[]{:S(2)}) copy-start(bf16[512,512]{1,0:T(8,128)(2,1)} %proc_send_ref.1) | copy-start | bytes 1572868
  15.6 15.8 %copy-start.11 = (bf16[512,512]{1,0:T(8,128)(2,1)S(1)}, bf16[512,512]{1,0:T(8,128)(2,1)}, u32[]{:S(2)}) copy-start(bf16[512,512]{1,0:T(8,128)(2,1)} %proc_recv_ref.1) | copy-start | bytes 1572868
  15.6 15.8 %copy-start.16 = (s32[3,4,64]{2,1,0:T(4,128)S(1)}, s32[3,4,64]{2,1,0:T(4,128)}, u32[]{:S(2)}) copy-start(s32[3,4,64]{2,1,0:T(4,128)} %near_ref.1) | copy-start | bytes 9220
  15.6 15.8 %copy-start.18 = (f32[512]{0:T(512)S(1)}, f32[512]{0:T(512)}, u32[]{:S(2)}) copy-start(f32[512]{0:T(512)} %param.51) | copy-start | bytes 6148
  15.6 15.8 %copy-start.19 = (s32[128,2]{0,1:T(2,128)S(1)}, s32[128,2]{0,1:T(2,128)}, u32[]{:S(2)}) copy-start(s32[128,2]{0,1:T(2,128)} %param.38) | copy-start | bytes 3076
  20.9 7.7 %collective-permute-start.3 = (bf16[4,128,256]{2,1,0:T(8,128)(2,1)S(1)}, bf16[4,128,256]{2,1,0:T(8,128)(2,1)S(1)}, u32[]{:S(2)}, u32[]{:S(2)}) collective-permute-start(bf16[4,128,256]{2,1,0:T(8,128)(2,1)S(1)} %pad_maximum_fusion), channel_id=1, source_target_pairs={{0,4},{4,0},{8,12},{12,8},{16,20},{20,16},{24,28},{28,24},{32,36},... | collective-permute-start | bytes 786440 | tf_op jit(solution)/shard_map/ppermute | solution.py:35
  21.0 10.4 %collective-permute-start.4 = (bf16[4,128,256]{2,1,0:T(8,128)(2,1)S(1)}, bf16[4,128,256]{2,1,0:T(8,128)(2,1)S(1)}, u32[]{:S(2)}, u32[]{:S(2)}) collective-permute-start(bf16[4,128,256]{2,1,0:T(8,128)(2,1)S(1)} %pad_maximum_fusion.1), channel_id=1, source_target_pairs={{4,8},{8,4},{12,16},{16,12},{20,24},{24,20},{28,32},{32,28},{36,40... | collective-permute-start | bytes 786440 | tf_op jit(solution)/shard_map/ppermute | solution.py:35
  47.5 29.1 %copy-start.4 = (bf16[3,64,512]{2,1,0:T(8,128)(2,1)}, bf16[3,64,512]{2,1,0:T(8,128)(2,1)S(1)}, u32[]{:S(2)}) copy-start(bf16[3,64,512]{2,1,0:T(8,128)(2,1)S(1)} %get-tuple-element.53.own0_hbm) | copy-start | bytes 589828
  47.5 6.0 %collective-permute-start.5 = (bf16[3,64,512]{2,1,0:T(8,128)(2,1)S(1)}, bf16[3,64,512]{2,1,0:T(8,128)(2,1)S(1)}, u32[]{:S(2)}, u32[]{:S(2)}) collective-permute-start(bf16[3,64,512]{2,1,0:T(8,128)(2,1)S(1)} %get-tuple-element.46), channel_id=1, source_target_pairs={{0,1},{1,0},{2,3},{3,2},{4,5},{5,4},{6,7},{7,6},{8,9},{9,8},{10,11... | collective-permute-start | bytes 589832 | tf_op jit(solution)/shard_map/ppermute | solution.py:21
  47.5 15.8 %collective-permute-start.6 = (bf16[3,64,512]{2,1,0:T(8,128)(2,1)S(1)}, bf16[3,64,512]{2,1,0:T(8,128)(2,1)S(1)}, u32[]{:S(2)}, u32[]{:S(2)}) collective-permute-start(bf16[3,64,512]{2,1,0:T(8,128)(2,1)S(1)} %get-tuple-element.55), channel_id=1, source_target_pairs={{0,2},{1,3},{2,0},{3,1},{4,6},{5,7},{6,4},{7,5},{8,10},{9,11},{10,... | collective-permute-start | bytes 589832 | tf_op jit(solution)/shard_map/ppermute | solution.py:21
  47.5 15.8 %collective-permute-start.7 = (bf16[3,64,512]{2,1,0:T(8,128)(2,1)S(1)}, bf16[3,64,512]{2,1,0:T(8,128)(2,1)S(1)}, u32[]{:S(2)}, u32[]{:S(2)}) collective-permute-start(bf16[3,64,512]{2,1,0:T(8,128)(2,1)S(1)} %get-tuple-element.56), channel_id=1, source_target_pairs={{0,3},{1,2},{2,1},{3,0},{4,7},{5,6},{6,5},{7,4},{8,11},{9,10},{10,... | collective-permute-start | bytes 589832 | tf_op jit(solution)/shard_map/ppermute | solution.py:21
  53.4 23.1 %copy-start.23 = (bf16[3,64,512]{2,1,0:T(8,128)(2,1)}, bf16[3,64,512]{2,1,0:T(8,128)(2,1)S(1)}, u32[]{:S(2)}) copy-start(bf16[3,64,512]{2,1,0:T(8,128)(2,1)S(1)} %collective-permute-done.5.own1_hbm) | copy-start | bytes 589828
  53.4 23.1 %all-to-all-start = ((bf16[128,8,128]{2,1,0:T(8,128)(2,1)}), bf16[128,8,128]{2,1,0:T(8,128)(2,1)S(1)}, u32[]{:S(2)}, u32[]{:S(2)}) async-start(bf16[128,8,128]{2,1,0:T(8,128)(2,1)} %bitcast.7), calls=%async_computation | async-start | bytes 524288 | tf_op jit(solution)/shard_map/all_to_all | solution.py:787
  63.4 13.2 %collective-permute-start.8 = (bf16[4,64,512]{2,1,0:T(8,128)(2,1)S(1)}, bf16[4,64,512]{2,1,0:T(8,128)(2,1)S(1)}, u32[]{:S(2)}, u32[]{:S(2)}) collective-permute-start(bf16[4,64,512]{2,1,0:T(8,128)(2,1)S(1)} %pad_maximum_fusion.2), channel_id=1, source_target_pairs={{0,4},{4,0},{8,12},{12,8},{16,20},{20,16},{24,28},{28,24},{32,36},... | collective-permute-start | bytes 786440 | tf_op jit(solution)/shard_map/ppermute | solution.py:35
  63.7 12.9 %collective-permute-start.9 = (bf16[4,64,512]{2,1,0:T(8,128)(2,1)S(1)}, bf16[4,64,512]{2,1,0:T(8,128)(2,1)S(1)}, u32[]{:S(2)}, u32[]{:S(2)}) collective-permute-start(bf16[4,64,512]{2,1,0:T(8,128)(2,1)S(1)} %pad_maximum_fusion.3), channel_id=1, source_target_pairs={{4,8},{8,4},{12,16},{16,12},{20,24},{24,20},{28,32},{32,28},{36,40... | collective-permute-start | bytes 786440 | tf_op jit(solution)/shard_map/ppermute | solution.py:35
  (15 other events, 110.9 us)

commit v5 on v4

--- a/solution.py
+++ b/solution.py
@@ -303,9 +303,7 @@
     node_out_ref,
     proc_send_ref,
     proc_recv_ref,
-    latent_ref,
-    pair_ref,
-    out0_ref,
+    trio_ref,
     out1_ref,
     out2_ref,
     out3_ref,
@@ -402,17 +400,17 @@
     mesh_latent = half(
         embed.astype(jnp.float32) + layer_norm(dot(node_act, weight(4)[...])) * gain_ref[...]
     )
-    latent_ref[...] = mesh_latent
+    trio_ref[2 * mesh_rows : 3 * mesh_rows, :] = mesh_latent
     sender = half(dot(mesh_latent, weight(5)[...]))
-    pair_ref[0:mesh_rows, :] = sender
-    pair_ref[mesh_rows : 2 * mesh_rows, :] = half(dot(mesh_latent, weight(6)[...]))
+    trio_ref[0:mesh_rows, :] = sender
+    trio_ref[mesh_rows : 2 * mesh_rows, :] = half(dot(mesh_latent, weight(6)[...]))
     padded = -(-mesh_rows // LANES) * LANES
     sender_pad = jnp.concatenate(
         [sender, jnp.zeros((padded - mesh_rows, latent), jnp.bfloat16)], axis=0
     )
     near = near_ref.shape[2]
     shares = offsets()
-    outs = (out0_ref, out1_ref, out2_ref, out3_ref)
+    outs = (out1_ref, out2_ref, out3_ref)
     index = jnp.concatenate(
         [near_ref[offset, pl.ds(me ^ k, 1), :] for k in range(subs) for offset in shares]
         + [far_ref[c : c + 1, :] for c in range(far_ref.shape[0])],
@@ -426,7 +424,8 @@
         axis=0,
     )
     leaving = dot(onehot, sender_pad)
-    for k, out_ref in enumerate(outs):
+    trio_ref[3 * mesh_rows :, :] = half(leaving[0 : 3 * near])
+    for k, out_ref in enumerate(outs, 1):
         out_ref[...] = half(leaving[3 * near * k : 3 * near * (k + 1)]).reshape(out_ref.shape)
     lanes = latent // LANES
     spread_rows = far_ref.shape[0] * lanes
@@ -442,7 +441,7 @@
 def edge_start_kernel(
     src_ref,
     dst_ref,
-    pair_hbm,
+    trio_hbm,
     lat_hbm,
     self_hbm,
     pre_hbm,
@@ -461,7 +460,9 @@
     near_total = 3 * subs * (LANES // 2)
     edges = lat_ref.shape[0]
     halves = [pl.ds(first, edges // 2) for first in (0, edges // 2)]
-    pairs = pltpu.make_async_copy(pair_hbm, pair_ref, read_sems.at[3])
+    pairs = pltpu.make_async_copy(
+        trio_hbm.at[pl.ds(0, pair_ref.shape[0])], pair_ref, read_sems.at[3]
+    )
     weight = pltpu.make_async_copy(self_hbm, self_ref, read_sems.at[2])
     reads = [
         pltpu.make_async_copy(lat_hbm.at[span], lat_ref.at[span], read_sems.at[k])
@@ -515,11 +516,10 @@
     dst_ref,
     gain_ref,
     far_hbm,
-    latent_hbm,
+    trio_hbm,
     pre_hbm,
     place_hbm,
     lat_hbm,
-    own0_hbm,
     own1_hbm,
     own2_hbm,
     own3_hbm,
@@ -550,11 +550,13 @@
     subs, near, _ = mate_hbm.shape
     near_total = 3 * subs * near
     me = lax.axis_index("sub")
-    owns = (own0_hbm, own1_hbm, own2_hbm, own3_hbm)
+    owns = (trio_hbm, own1_hbm, own2_hbm, own3_hbm)
+    stay = pl.ds(3 * latent_ref.shape[0], mate_hbm.shape[1])
     rows = []
     for w, offset in enumerate(sources()):
         for k in range(subs):
-            source = owns[k].at[0] if w == 0 else (mate_hbm, cross_hbm)[w - 1].at[k]
+            own = owns[k].at[stay] if k == 0 else owns[k].at[0]
+            source = own if w == 0 else (mate_hbm, cross_hbm)[w - 1].at[k]
             place = pl.multiple_of((offset * subs + (me ^ k)) * near, near)
             rows.append(
                 pltpu.make_async_copy(
@@ -570,7 +572,9 @@
         for k, span in enumerate(spans)
     ]
     far_read = pltpu.make_async_copy(far_hbm, far_ref, sems.at[4])
-    latent_read = pltpu.make_async_copy(latent_hbm, latent_ref, sems.at[5])
+    latent_read = pltpu.make_async_copy(
+        trio_hbm.at[pl.ds(2 * mesh_rows, mesh_rows)], latent_ref, sems.at[5]
+    )
     for copy in [far_read, *rows, reads[0][1], reads[0][0], latent_read]:
         copy.start()
     weight = Fetch((edge_out_ref, upd_self_ref, upd_agg_ref, upd_out_ref), slots_ref, sems)
@@ -594,14 +598,15 @@
         )
     for copy in rows:
         copy.wait()
-    edge_out = weight(0)[...]
     latent_read.wait()
+    for block in reads:
+        for copy in block:
+            copy.wait()
+    edge_out, _, upd_agg, upd_out = (weight(k)[...] for k in range(4))
     upd_self = dot(latent_ref[...], weight(1)[...])
 
     def gathered(block):
         span = spans[block]
-        for copy in reads[block]:
-            copy.wait()
         return pre_ref[span, :].astype(jnp.float32) + dot(
             picks(place_ref[span, :], table_ref.shape[0]), table_ref[...]
         )
@@ -620,9 +625,9 @@
     target = row_of(dst_ref, 0, lat_ref.shape[0] // LANES)
     inflow = half(dot(scatter_picks(target, mesh_rows), new_ref[...]))
     latent = latent_ref[...]
-    act = half(silu(upd_self + dot(inflow, weight(2)[...])))
+    act = half(silu(upd_self + dot(inflow, upd_agg)))
     out_ref[...] = half(
-        latent.astype(jnp.float32) + layer_norm(dot(act, weight(3)[...])) * gain_ref[...]
+        latent.astype(jnp.float32) + layer_norm(dot(act, upd_out)) * gain_ref[...]
     )
 
 
@@ -740,13 +745,12 @@
         nbytes=3 << 20,
     )(*arrived, enc_in, enc_out, send_proj)
 
-    mesh_latent, pairs, *near_parts, far_out = local_call(
+    trio, *near_parts, far_out = local_call(
         encoder_kernel,
         (
-            shape(mesh_rows, latent),
-            shape(2 * mesh_rows, latent),
+            shape(3 * mesh_rows + 3 * near_cap, latent),
         )
-        + (shape(3, near_cap, latent),) * sub_count
+        + (shape(3, near_cap, latent),) * (sub_count - 1)
         + (shape(far_total * latent // LANES, LANES),),
         [in_smem()] + [whole()] * 12 + [in_hbm()] * 7,
         scratch=[
@@ -782,7 +786,8 @@
         proc_recv,
     )
 
-    near_arrived = across_subs(near_parts)
+    stay = trio[3 * mesh_rows :].reshape(3, near_cap, latent)
+    near_arrived = across_subs([stay, *near_parts])
     near_arrived[1], far_out = lax.optimization_barrier((near_arrived[1], far_out))
     far_rows = lax.all_to_all(
         far_out.reshape(devices, -1, LANES),
@@ -809,11 +814,11 @@
         nbytes=START_BYTES,
         out_specs=(in_hbm(), in_hbm()),
         vmem=VMEM_ALL,
-    )(mesh_src, mesh_dst, pairs, mesh_edge_lat, edge_self)
+    )(mesh_src, mesh_dst, trio, mesh_edge_lat, edge_self)
     return local_call(
         edge_finish_kernel,
         shape(mesh_rows, latent),
-        [whole()] * 2 + [in_hbm()] * 15,
+        [whole()] * 2 + [in_hbm()] * 14,
         scratch=[
             pltpu.VMEM(far_rows.shape, bf16),
             pltpu.VMEM((mesh_rows, latent), bf16),
@@ -835,11 +840,11 @@
         mesh_dst,
         out_gain.reshape(1, latent),
         far_rows,
-        mesh_latent,
+        trio,
         pre,
         mesh_place,
         mesh_edge_lat,
-        *near_arrived,
+        *near_arrived[1:],
         near_mates,
         near_crosses,
         edge_out,

time: 91.3 us -> 88.6 us (0.970)
  local copies, waits for them, and re-layouts: 2.61 us -> 1.05 us
    unnamed x56 -> x52, local copies, waits for them, and re-layouts: 2.53 us -> 0.97 us
    all_to_all x1, starting transfers between devices: 9.83 us -> 8.82 us  [body(): lax.all_to_all(far_out.reshape(devices, -1, LANES), ('band', 'sub'), spli...]
  transfers between devices with their start and end apart: 11 -> 11, of which waited for: 4 -> 4; matrix products, arithmetic and copies ran while one was open for 0% -> 0% of each run, Pallas kernels for 15% -> 16%
where the time goes in v5:
time: 88.6 us; the launch traced here: 87.5 us
  Pallas kernels  45.6 us (51%)
  starting transfers between devices  30.5 us (34%)
  waiting for transfers between devices  8.92 us (10%)
  between operations  1.34 us (2%)
  local copies, waits for them, and re-layouts  1.05 us (1%)
    pallas_call x1, Pallas kernels, body(): local_call(encoder_kernel, (shape(3 * mesh_rows + 3 * near_cap, latent),)...  14.4 us
    pallas_call x1, Pallas kernels, body(): local_call(edge_finish_kernel, shape(mesh_rows, latent), [whole()] * 2 +...  12.6 us
    ppermute x4, starting transfers between devices, band_swap(): lax.ppermute(value, 'band', [(b, other) for b, other in pairs if 0 <= oth...  12.2 us
    ppermute x6, starting transfers between devices, sub_swap(): return lax.ppermute(value, 'sub', [(t, t ^ step) for t in range(count)])  9.47 us
    all_to_all x1, starting transfers between devices, body(): lax.all_to_all(far_out.reshape(devices, -1, LANES), ('band', 'sub'), spli...  8.82 us
    pallas_call x1, Pallas kernels, body(): local_call(edge_start_kernel, (shape(mesh_edges, latent), shape(mesh_edge...  7.3 us
    ppermute x6, waiting for transfers between devices, sub_swap(): return lax.ppermute(value, 'sub', [(t, t ^ step) for t in range(count)])  6.11 us
    pallas_call x1, Pallas kernels, body(): local_call(prepare_grid_kernel, (shape(edges, LANES, dtype=f32), shape(ed...  5.45 us
  transfers between devices with their start and end apart: 11, of which 4 were waited for; matrix products, arithmetic and copies ran while one was open for 0% of the time, Pallas kernels for 16%

profile of v5, /device:TPU:6, one launch (start us, length us, event | category | flops | bytes accessed | tf_op | source)
XLA Modules:
  0.0 87.5 jit_solution(14344578982347265645)
XLA Ops:
  0.0 4.5 %shard_map.280 = (bf16[3,128,256]{2,1,0:T(8,128)(2,1)}, bf16[3,128,256]{2,1,0:T(8,128)(2,1)}, bf16[3,128,256]{2,1,0:T(8,128)(2,1)}, bf16[3,128,256]{2,1,0:T(8,128)(2,1)}) custom-call(s32[3,4,128]{2,1,0:T(4,128)} %send_ref.1, bf16[227,2048]{1,0:T(8,128)(2,1)} %bitcast.20), custom_call_target="tpu_custom_call" | custom-call | flops 1610612736 | bytes 1835008 | tf_op jit(solution)/shard_map/pallas_call | solution.py:690
  4.6 1.6 %collective-permute-start = (bf16[3,128,256]{2,1,0:T(8,128)(2,1)}, bf16[3,128,256]{2,1,0:T(8,128)(2,1)S(1)}, u32[]{:S(2)}, u32[]{:S(2)}) collective-permute-start(bf16[3,128,256]{2,1,0:T(8,128)(2,1)} %get-tuple-element.30), channel_id=1, source_target_pairs={{0,1},{1,0},{2,3},{3,2},{4,5},{5,4},{6,7},{7,6},{8,9},{9,8},{10,11... | collective-permute-start | bytes 589832 | tf_op jit(solution)/shard_map/ppermute | solution.py:21
  6.2 2.9 %collective-permute-start.1 = (bf16[3,128,256]{2,1,0:T(8,128)(2,1)}, bf16[3,128,256]{2,1,0:T(8,128)(2,1)S(1)}, u32[]{:S(2)}, u32[]{:S(2)}) collective-permute-start(bf16[3,128,256]{2,1,0:T(8,128)(2,1)} %get-tuple-element.31), channel_id=1, source_target_pairs={{0,2},{1,3},{2,0},{3,1},{4,6},{5,7},{6,4},{7,5},{8,10},{9,11},{10,... | collective-permute-start | bytes 589832 | tf_op jit(solution)/shard_map/ppermute | solution.py:21
  9.1 0.2 collective-permute-start.2
  10.1 5.5 %shard_map.281 = (f32[8192,128]{1,0:T(8,128)S(1)}, bf16[8192,512]{1,0:T(8,128)(2,1)S(1)}, f32[320,512]{1,0:T(8,128)S(1)}) custom-call(s32[1]{0:T(128)S(6)} %copy.31.live_ref, s32[64,128]{1,0:T(8,128)S(1)} %bitcast.14, s32[64,128]{1,0:T(8,128)S(1)} %bitcast.15, bf16[4,8192]{1,0:T(4,128)(2,1)S(1)} %copy-done.13, bf16[320,512]{1,0:T(8,128)(2,1)S(1)} %copy-done.12, ...), custom_call_target="tpu_custom_call" | custom-call | flops 8589934592 | bytes 16777216 | tf_op jit(solution)/shard_map/pallas_call | solution.py:716
  15.6 2.6 %collective-permute-done.1.own2_ref = bf16[3,128,256]{2,1,0:T(8,128)(2,1)S(1)} collective-permute-done((bf16[3,128,256]{2,1,0:T(8,128)(2,1)}, bf16[3,128,256]{2,1,0:T(8,128)(2,1)S(1)}, u32[]{:S(2)}, u32[]{:S(2)}) %collective-permute-start.1) | collective-permute-done | bytes 196640 | tf_op jit(solution)/shard_map/ppermute | solution.py:21
  18.2 2.6 %collective-permute-done.2.own3_ref = bf16[3,128,256]{2,1,0:T(8,128)(2,1)S(1)} collective-permute-done((bf16[3,128,256]{2,1,0:T(8,128)(2,1)}, bf16[3,128,256]{2,1,0:T(8,128)(2,1)S(1)}, u32[]{:S(2)}, u32[]{:S(2)}) %collective-permute-start.2) | collective-permute-done | bytes 196640 | tf_op jit(solution)/shard_map/ppermute | solution.py:21
  20.9 0.1 collective-permute-start.3
  21.0 6.3 %collective-permute-start.4 = (bf16[4,128,256]{2,1,0:T(8,128)(2,1)S(1)}, bf16[4,128,256]{2,1,0:T(8,128)(2,1)S(1)}, u32[]{:S(2)}, u32[]{:S(2)}) collective-permute-start(bf16[4,128,256]{2,1,0:T(8,128)(2,1)S(1)} %pad_maximum_fusion.1), channel_id=1, source_target_pairs={{4,8},{8,4},{12,16},{16,12},{20,24},{24,20},{28,32},{32,28},{36,40... | collective-permute-start | bytes 786440 | tf_op jit(solution)/shard_map/ppermute | solution.py:35
  27.4 1.2 %shard_map.282.own_rows_ref = bf16[512,512]{1,0:T(8,128)(2,1)S(1)} custom-call(bf16[3,128,256]{2,1,0:T(8,128)(2,1)S(1)} %copy-done, bf16[3,128,256]{2,1,0:T(8,128)(2,1)S(1)} %collective-permute-done.own1_ref, bf16[3,128,256]{2,1,0:T(8,128)(2,1)S(1)} %collective-permute-done.1.own2_ref, bf16[3,128,256]{2,1,0:T(8,128)(2,1)S(1)} %collective-permute-done.2.own3_ref, ...), custom_call_target="tpu_custom_call" | custom-call | flops 671088640 | bytes 3145728 | tf_op jit(solution)/shard_map/pallas_call | solution.py:740
  28.6 2.8 %collective-permute-done.4.cross_ref = bf16[4,128,256]{2,1,0:T(8,128)(2,1)S(1)} collective-permute-done((bf16[4,128,256]{2,1,0:T(8,128)(2,1)S(1)}, bf16[4,128,256]{2,1,0:T(8,128)(2,1)S(1)}, u32[]{:S(2)}, u32[]{:S(2)}) %collective-permute-start.4) | collective-permute-done | bytes 262176 | tf_op jit(solution)/shard_map/ppermute | solution.py:35
  31.4 14.4 %shard_map.283 = (bf16[1152,512]{1,0:T(8,128)(2,1)S(1)}, bf16[3,64,512]{2,1,0:T(8,128)(2,1)S(1)}, bf16[3,64,512]{2,1,0:T(8,128)(2,1)S(1)}, bf16[3,64,512]{2,1,0:T(8,128)(2,1)S(1)}, bf16[1024,128]{1,0:T(8,128)(2,1)}) custom-call(s32[1]{0:T(128)S(6)} %copy.31.live_ref, bf16[512,512]{1,0:T(8,128)(2,1)S(1)} %shard_map.282.own_rows_ref, ...), custom_call_target="tpu_custom_call" | custom-call | flops 17179869184 | bytes 16777216 | tf_op jit(solution)/shard_map/pallas_call | solution.py:748
  45.9 0.1 collective-permute-start.5
  46.0 1.9 %collective-permute-start.6 = (bf16[3,64,512]{2,1,0:T(8,128)(2,1)S(1)}, bf16[3,64,512]{2,1,0:T(8,128)(2,1)S(1)}, u32[]{:S(2)}, u32[]{:S(2)}) collective-permute-start(bf16[3,64,512]{2,1,0:T(8,128)(2,1)S(1)} %get-tuple-element.51), channel_id=1, source_target_pairs={{0,2},{1,3},{2,0},{3,1},{4,6},{5,7},{6,4},{7,5},{8,10},{9,11},{10,... | collective-permute-start | bytes 589832 | tf_op jit(solution)/shard_map/ppermute | solution.py:21
  47.9 2.7 %collective-permute-start.7 = (bf16[3,64,512]{2,1,0:T(8,128)(2,1)S(1)}, bf16[3,64,512]{2,1,0:T(8,128)(2,1)S(1)}, u32[]{:S(2)}, u32[]{:S(2)}) collective-permute-start(bf16[3,64,512]{2,1,0:T(8,128)(2,1)S(1)} %get-tuple-element.52), channel_id=1, source_target_pairs={{0,3},{1,2},{2,1},{3,0},{4,7},{5,6},{6,5},{7,4},{8,11},{9,10},{10,... | collective-permute-start | bytes 589832 | tf_op jit(solution)/shard_map/ppermute | solution.py:21
  50.7 1.0 %collective-permute-done.5.own1_hbm = bf16[3,64,512]{2,1,0:T(8,128)(2,1)S(1)} collective-permute-done((bf16[3,64,512]{2,1,0:T(8,128)(2,1)S(1)}, bf16[3,64,512]{2,1,0:T(8,128)(2,1)S(1)}, u32[]{:S(2)}, u32[]{:S(2)}) %collective-permute-start.5) | collective-permute-done | bytes 196640 | tf_op jit(solution)/shard_map/ppermute | solution.py:21
  51.6 8.8 %all-to-all-start = ((bf16[128,8,128]{2,1,0:T(8,128)(2,1)}), bf16[128,8,128]{2,1,0:T(8,128)(2,1)S(1)}, u32[]{:S(2)}, u32[]{:S(2)}) async-start(bf16[128,8,128]{2,1,0:T(8,128)(2,1)} %bitcast.7), calls=%async_computation | async-start | bytes 524288 | tf_op jit(solution)/shard_map/all_to_all | solution.py:792
  60.6 0.2 collective-permute-start.8
  60.9 5.5 %collective-permute-start.9 = (bf16[4,64,512]{2,1,0:T(8,128)(2,1)S(1)}, bf16[4,64,512]{2,1,0:T(8,128)(2,1)S(1)}, u32[]{:S(2)}, u32[]{:S(2)}) collective-permute-start(bf16[4,64,512]{2,1,0:T(8,128)(2,1)S(1)} %pad_maximum_fusion.3), channel_id=1, source_target_pairs={{4,8},{8,4},{12,16},{16,12},{20,24},{24,20},{28,32},{32,28},{36,40... | collective-permute-start | bytes 786440 | tf_op jit(solution)/shard_map/ppermute | solution.py:35
  66.4 7.3 %shard_map.284 = (bf16[2560,512]{1,0:T(8,128)(2,1)}, f32[2560,128]{1,0:T(8,128)}) custom-call(s32[20,128]{1,0:T(8,128)} %bitcast.21, s32[20,128]{1,0:T(8,128)} %bitcast.22, bf16[1152,512]{1,0:T(8,128)(2,1)} %copy-done.4, bf16[2560,512]{1,0:T(8,128)(2,1)} %lat_hbm.3, bf16[512,512]{1,0:T(8,128)(2,1)} %self_hbm.1), custom_call_target="tpu_custom_call" | custom-call | flops 4000000000 | bytes 16777216 | tf_op jit(solution)/shard_map/pallas_call | solution.py:800
  73.8 0.6 copy-done.20
  74.5 0.1 copy-done.24
  74.6 0.1 copy-done.25
  74.7 12.6 %shard_map.285 = bf16[320,512]{1,0:T(8,128)(2,1)} custom-call(s32[20,128]{1,0:T(8,128)} %bitcast.23, f32[1,512]{1,0:T(1,128)} %bitcast.24, bf16[1024,128]{1,0:T(8,128)(2,1)} %bitcast.19, bf16[1152,512]{1,0:T(8,128)(2,1)} %copy-done.4, bf16[2560,512]{1,0:T(8,128)(2,1)} %get-tuple-element.48.pre_hbm, f32[2560,128]{1,0:T(8,128)} %get-tuple-element.49.place_hbm, ...), custom_call_target="tpu_custom_call" | custom-call | flops 5368709120 | bytes 12582912 | tf_op jit(solution)/shard_map/pallas_call | solution.py:818
  (66 shorter events, 0.4 us)
Async XLA Ops:
  4.6 11.0 %collective-permute-start = (bf16[3,128,256]{2,1,0:T(8,128)(2,1)}, bf16[3,128,256]{2,1,0:T(8,128)(2,1)S(1)}, u32[]{:S(2)}, u32[]{:S(2)}) collective-permute-start(bf16[3,128,256]{2,1,0:T(8,128)(2,1)} %get-tuple-element.30), channel_id=1, source_target_pairs={{0,1},{1,0},{2,3},{3,2},{4,5},{5,4},{6,7},{7,6},{8,9},{9,8},{10,11... | collective-permute-start | bytes 589832 | tf_op jit(solution)/shard_map/ppermute | solution.py:21
  6.2 12.0 %collective-permute-start.1 = (bf16[3,128,256]{2,1,0:T(8,128)(2,1)}, bf16[3,128,256]{2,1,0:T(8,128)(2,1)S(1)}, u32[]{:S(2)}, u32[]{:S(2)}) collective-permute-start(bf16[3,128,256]{2,1,0:T(8,128)(2,1)} %get-tuple-element.31), channel_id=1, source_target_pairs={{0,2},{1,3},{2,0},{3,1},{4,6},{5,7},{6,4},{7,5},{8,10},{9,11},{10,... | collective-permute-start | bytes 589832 | tf_op jit(solution)/shard_map/ppermute | solution.py:21
  9.1 11.7 %collective-permute-start.2 = (bf16[3,128,256]{2,1,0:T(8,128)(2,1)}, bf16[3,128,256]{2,1,0:T(8,128)(2,1)S(1)}, u32[]{:S(2)}, u32[]{:S(2)}) collective-permute-start(bf16[3,128,256]{2,1,0:T(8,128)(2,1)} %get-tuple-element.32), channel_id=1, source_target_pairs={{0,3},{1,2},{2,1},{3,0},{4,7},{5,6},{6,5},{7,4},{8,11},{9,10},{10,... | collective-permute-start | bytes 589832 | tf_op jit(solution)/shard_map/ppermute | solution.py:21
  10.0 17.3 %copy-start.1 = (bf16[512,512]{1,0:T(8,128)(2,1)S(1)}, bf16[512,512]{1,0:T(8,128)(2,1)}, u32[]{:S(2)}) copy-start(bf16[512,512]{1,0:T(8,128)(2,1)} %enc_out_ref.3) | copy-start | bytes 1572868
  10.0 17.3 %copy-start.2 = (bf16[512,512]{1,0:T(8,128)(2,1)S(1)}, bf16[512,512]{1,0:T(8,128)(2,1)}, u32[]{:S(2)}) copy-start(bf16[512,512]{1,0:T(8,128)(2,1)} %send_proj_ref.3) | copy-start | bytes 1572868
  10.1 17.3 %copy-start.3 = (bf16[227,512]{1,0:T(8,128)(2,1)S(1)}, bf16[227,512]{1,0:T(8,128)(2,1)}, u32[]{:S(2)}) copy-start(bf16[227,512]{1,0:T(8,128)(2,1)} %enc_in_ref.3) | copy-start | bytes 697348
  15.5 15.9 %copy-start.7 = (bf16[512,512]{1,0:T(8,128)(2,1)S(1)}, bf16[512,512]{1,0:T(8,128)(2,1)}, u32[]{:S(2)}) copy-start(bf16[512,512]{1,0:T(8,128)(2,1)} %msg_ref.1) | copy-start | bytes 1572868
  15.5 15.8 %copy-start.8 = (bf16[512,512]{1,0:T(8,128)(2,1)S(1)}, bf16[512,512]{1,0:T(8,128)(2,1)}, u32[]{:S(2)}) copy-start(bf16[512,512]{1,0:T(8,128)(2,1)} %node_agg_ref.1) | copy-start | bytes 1572868
  15.6 15.8 %copy-start.9 = (bf16[512,512]{1,0:T(8,128)(2,1)S(1)}, bf16[512,512]{1,0:T(8,128)(2,1)}, u32[]{:S(2)}) copy-start(bf16[512,512]{1,0:T(8,128)(2,1)} %node_out_ref.1) | copy-start | bytes 1572868
  15.6 15.8 %copy-start.10 = (bf16[512,512]{1,0:T(8,128)(2,1)S(1)}, bf16[512,512]{1,0:T(8,128)(2,1)}, u32[]{:S(2)}) copy-start(bf16[512,512]{1,0:T(8,128)(2,1)} %proc_send_ref.1) | copy-start | bytes 1572868
  15.6 15.8 %copy-start.11 = (bf16[512,512]{1,0:T(8,128)(2,1)S(1)}, bf16[512,512]{1,0:T(8,128)(2,1)}, u32[]{:S(2)}) copy-start(bf16[512,512]{1,0:T(8,128)(2,1)} %proc_recv_ref.1) | copy-start | bytes 1572868
  15.6 15.8 %copy-start.16 = (s32[3,4,64]{2,1,0:T(4,128)S(1)}, s32[3,4,64]{2,1,0:T(4,128)}, u32[]{:S(2)}) copy-start(s32[3,4,64]{2,1,0:T(4,128)} %near_ref.1) | copy-start | bytes 9220
  15.6 15.8 %copy-start.18 = (f32[512]{0:T(512)S(1)}, f32[512]{0:T(512)}, u32[]{:S(2)}) copy-start(f32[512]{0:T(512)} %param.51) | copy-start | bytes 6148
  15.6 15.8 %copy-start.19 = (s32[128,2]{0,1:T(2,128)S(1)}, s32[128,2]{0,1:T(2,128)}, u32[]{:S(2)}) copy-start(s32[128,2]{0,1:T(2,128)} %param.38) | copy-start | bytes 3076
  20.9 7.7 %collective-permute-start.3 = (bf16[4,128,256]{2,1,0:T(8,128)(2,1)S(1)}, bf16[4,128,256]{2,1,0:T(8,128)(2,1)S(1)}, u32[]{:S(2)}, u32[]{:S(2)}) collective-permute-start(bf16[4,128,256]{2,1,0:T(8,128)(2,1)S(1)} %pad_maximum_fusion), channel_id=1, source_target_pairs={{0,4},{4,0},{8,12},{12,8},{16,20},{20,16},{24,28},{28,24},{32,36},... | collective-permute-start | bytes 786440 | tf_op jit(solution)/shard_map/ppermute | solution.py:35
  21.0 10.4 %collective-permute-start.4 = (bf16[4,128,256]{2,1,0:T(8,128)(2,1)S(1)}, bf16[4,128,256]{2,1,0:T(8,128)(2,1)S(1)}, u32[]{:S(2)}, u32[]{:S(2)}) collective-permute-start(bf16[4,128,256]{2,1,0:T(8,128)(2,1)S(1)} %pad_maximum_fusion.1), channel_id=1, source_target_pairs={{4,8},{8,4},{12,16},{16,12},{20,24},{24,20},{28,32},{32,28},{36,40... | collective-permute-start | bytes 786440 | tf_op jit(solution)/shard_map/ppermute | solution.py:35
  45.9 20.5 %copy-start.4 = (bf16[1152,512]{1,0:T(8,128)(2,1)}, bf16[1152,512]{1,0:T(8,128)(2,1)S(1)}, u32[]{:S(2)}) copy-start(bf16[1152,512]{1,0:T(8,128)(2,1)S(1)} %get-tuple-element.47.trio_hbm) | copy-start | bytes 3538948
  45.9 5.7 %collective-permute-start.5 = (bf16[3,64,512]{2,1,0:T(8,128)(2,1)S(1)}, bf16[3,64,512]{2,1,0:T(8,128)(2,1)S(1)}, u32[]{:S(2)}, u32[]{:S(2)}) collective-permute-start(bf16[3,64,512]{2,1,0:T(8,128)(2,1)S(1)} %get-tuple-element.44), channel_id=1, source_target_pairs={{0,1},{1,0},{2,3},{3,2},{4,5},{5,4},{6,7},{7,6},{8,9},{9,8},{10,11... | collective-permute-start | bytes 589832 | tf_op jit(solution)/shard_map/ppermute | solution.py:21
  46.0 14.5 %collective-permute-start.6 = (bf16[3,64,512]{2,1,0:T(8,128)(2,1)S(1)}, bf16[3,64,512]{2,1,0:T(8,128)(2,1)S(1)}, u32[]{:S(2)}, u32[]{:S(2)}) collective-permute-start(bf16[3,64,512]{2,1,0:T(8,128)(2,1)S(1)} %get-tuple-element.51), channel_id=1, source_target_pairs={{0,2},{1,3},{2,0},{3,1},{4,6},{5,7},{6,4},{7,5},{8,10},{9,11},{10,... | collective-permute-start | bytes 589832 | tf_op jit(solution)/shard_map/ppermute | solution.py:21
  47.9 12.6 %collective-permute-start.7 = (bf16[3,64,512]{2,1,0:T(8,128)(2,1)S(1)}, bf16[3,64,512]{2,1,0:T(8,128)(2,1)S(1)}, u32[]{:S(2)}, u32[]{:S(2)}) collective-permute-start(bf16[3,64,512]{2,1,0:T(8,128)(2,1)S(1)} %get-tuple-element.52), channel_id=1, source_target_pairs={{0,3},{1,2},{2,1},{3,0},{4,7},{5,6},{6,5},{7,4},{8,11},{9,10},{10,... | collective-permute-start | bytes 589832 | tf_op jit(solution)/shard_map/ppermute | solution.py:21
  51.6 22.1 %copy-start.21 = (bf16[3,64,512]{2,1,0:T(8,128)(2,1)}, bf16[3,64,512]{2,1,0:T(8,128)(2,1)S(1)}, u32[]{:S(2)}) copy-start(bf16[3,64,512]{2,1,0:T(8,128)(2,1)S(1)} %collective-permute-done.5.own1_hbm) | copy-start | bytes 589828
  51.6 22.1 %all-to-all-start = ((bf16[128,8,128]{2,1,0:T(8,128)(2,1)}), bf16[128,8,128]{2,1,0:T(8,128)(2,1)S(1)}, u32[]{:S(2)}, u32[]{:S(2)}) async-start(bf16[128,8,128]{2,1,0:T(8,128)(2,1)} %bitcast.7), calls=%async_computation | async-start | bytes 524288 | tf_op jit(solution)/shard_map/all_to_all | solution.py:792
  60.6 13.2 %collective-permute-start.8 = (bf16[4,64,512]{2,1,0:T(8,128)(2,1)S(1)}, bf16[4,64,512]{2,1,0:T(8,128)(2,1)S(1)}, u32[]{:S(2)}, u32[]{:S(2)}) collective-permute-start(bf16[4,64,512]{2,1,0:T(8,128)(2,1)S(1)} %pad_maximum_fusion.2), channel_id=1, source_target_pairs={{0,4},{4,0},{8,12},{12,8},{16,20},{20,16},{24,28},{28,24},{32,36},... | collective-permute-start | bytes 786440 | tf_op jit(solution)/shard_map/ppermute | solution.py:35
  60.9 12.9 %collective-permute-start.9 = (bf16[4,64,512]{2,1,0:T(8,128)(2,1)S(1)}, bf16[4,64,512]{2,1,0:T(8,128)(2,1)S(1)}, u32[]{:S(2)}, u32[]{:S(2)}) collective-permute-start(bf16[4,64,512]{2,1,0:T(8,128)(2,1)S(1)} %pad_maximum_fusion.3), channel_id=1, source_target_pairs={{4,8},{8,4},{12,16},{16,12},{20,24},{24,20},{28,32},{32,28},{36,40... | collective-permute-start | bytes 786440 | tf_op jit(solution)/shard_map/ppermute | solution.py:35
  (13 other events, 109.3 us)

commit v6 on v5

--- a/solution.py
+++ b/solution.py
@@ -12,6 +12,7 @@
 PAIR = 2 * EDGE_BLOCK
 VMEM_BYTES = 24 * 1024 * 1024
 VMEM_ALL = 60 * 1024 * 1024
+VMEM_LAST = 62650000
 START_FLOPS = 4 * 10**9
 START_BYTES = 16 << 20
 
@@ -835,7 +836,7 @@
         ],
         flops=2 * mesh_edges * 2048 * latent,
         nbytes=12 << 20,
-        vmem=VMEM_ALL,
+        vmem=VMEM_LAST,
     )(
         mesh_dst,
         out_gain.reshape(1, latent),

time: 88.6 us -> 89.5 us (1.010); the launches traced: 87.5 us -> 89.8 us
  starting transfers between devices: 30.5 us -> 38.3 us
  Pallas kernels: 45.6 us -> 38.2 us
  waiting for transfers between devices: 8.92 us -> 10.8 us
    pallas_call x1, Pallas kernels: 14.4 us -> 9.51 us  [body(): local_call(encoder_kernel, (shape(3 * mesh_rows + 3 * near_cap, latent),)...]
    ppermute x6, starting transfers between devices: 9.47 us -> 13.9 us  [sub_swap(): return lax.ppermute(value, 'sub', [(t, t ^ step) for t in range(count)])]
    all_to_all x1, starting transfers between devices: 8.82 us -> 12.3 us  [body(): lax.all_to_all(far_out.reshape(devices, -1, LANES), ('band', 'sub'), spli...]
    pallas_call x1, Pallas kernels: 5.45 us -> 2.98 us  [body(): local_call(prepare_grid_kernel, (shape(edges, LANES, dtype=f32), shape(ed...]
    ppermute x6, waiting for transfers between devices: 6.11 us -> 7.97 us  [sub_swap(): return lax.ppermute(value, 'sub', [(t, t ^ step) for t in range(count)])]
  transfers between devices with their start and end apart: 11 -> 11, of which waited for: 4 -> 4; matrix products, arithmetic and copies ran while one was open for 0% -> 0% of each run, Pallas kernels for 16% -> 13%
where the time goes in v6:
time: 89.5 us; the launch traced here: 89.8 us
  starting transfers between devices  38.3 us (43%)
  Pallas kernels  38.2 us (43%)
  waiting for transfers between devices  10.8 us (12%)
  between operations  1.34 us (1%)
  local copies, waits for them, and re-layouts  1.05 us (1%)
    ppermute x6, starting transfers between devices, sub_swap(): return lax.ppermute(value, 'sub', [(t, t ^ step) for t in range(count)])  13.9 us
    pallas_call x1, Pallas kernels, body(): local_call(edge_finish_kernel, shape(mesh_rows, latent), [whole()] * 2 +...  12.6 us
    all_to_all x1, starting transfers between devices, body(): lax.all_to_all(far_out.reshape(devices, -1, LANES), ('band', 'sub'), spli...  12.3 us
    ppermute x4, starting transfers between devices, band_swap(): lax.ppermute(value, 'band', [(b, other) for b, other in pairs if 0 <= oth...  12.2 us
    pallas_call x1, Pallas kernels, body(): local_call(encoder_kernel, (shape(3 * mesh_rows + 3 * near_cap, latent),)...  9.51 us
    ppermute x6, waiting for transfers between devices, sub_swap(): return lax.ppermute(value, 'sub', [(t, t ^ step) for t in range(count)])  7.97 us
    pallas_call x1, Pallas kernels, body(): local_call(edge_start_kernel, (shape(mesh_edges, latent), shape(mesh_edge...  7.29 us
    pallas_call x1, Pallas kernels, body(): pl.pallas_call(pick_grid_kernel, grid=(2,), out_shape=(shape(3, slot_cap,...  4.55 us
  transfers between devices with their start and end apart: 11, of which 4 were waited for; matrix products, arithmetic and copies ran while one was open for 0% of the time, Pallas kernels for 13%

profile of v6, /device:TPU:6, one launch (start us, length us, event | category | flops | bytes accessed | tf_op | source)
XLA Modules:
  0.0 89.8 jit_solution(14344578982347265645)
XLA Ops:
  0.0 4.5 %shard_map.280 = (bf16[3,128,256]{2,1,0:T(8,128)(2,1)}, bf16[3,128,256]{2,1,0:T(8,128)(2,1)}, bf16[3,128,256]{2,1,0:T(8,128)(2,1)}, bf16[3,128,256]{2,1,0:T(8,128)(2,1)}) custom-call(s32[3,4,128]{2,1,0:T(4,128)} %send_ref.1, bf16[227,2048]{1,0:T(8,128)(2,1)} %bitcast.20), custom_call_target="tpu_custom_call" | custom-call | flops 1610612736 | bytes 1835008 | tf_op jit(solution)/shard_map/pallas_call | solution.py:691
  4.6 1.6 %collective-permute-start = (bf16[3,128,256]{2,1,0:T(8,128)(2,1)}, bf16[3,128,256]{2,1,0:T(8,128)(2,1)S(1)}, u32[]{:S(2)}, u32[]{:S(2)}) collective-permute-start(bf16[3,128,256]{2,1,0:T(8,128)(2,1)} %get-tuple-element.30), channel_id=1, source_target_pairs={{0,1},{1,0},{2,3},{3,2},{4,5},{5,4},{6,7},{7,6},{8,9},{9,8},{10,11... | collective-permute-start | bytes 589832 | tf_op jit(solution)/shard_map/ppermute | solution.py:22
  6.2 2.9 %collective-permute-start.1 = (bf16[3,128,256]{2,1,0:T(8,128)(2,1)}, bf16[3,128,256]{2,1,0:T(8,128)(2,1)S(1)}, u32[]{:S(2)}, u32[]{:S(2)}) collective-permute-start(bf16[3,128,256]{2,1,0:T(8,128)(2,1)} %get-tuple-element.31), channel_id=1, source_target_pairs={{0,2},{1,3},{2,0},{3,1},{4,6},{5,7},{6,4},{7,5},{8,10},{9,11},{10,... | collective-permute-start | bytes 589832 | tf_op jit(solution)/shard_map/ppermute | solution.py:22
  9.1 0.2 collective-permute-start.2
  10.0 0.0 copy-start
  10.1 3.0 %shard_map.281 = (f32[8192,128]{1,0:T(8,128)S(1)}, bf16[8192,512]{1,0:T(8,128)(2,1)S(1)}, f32[320,512]{1,0:T(8,128)S(1)}) custom-call(s32[1]{0:T(128)S(6)} %copy.31.live_ref, s32[64,128]{1,0:T(8,128)S(1)} %bitcast.14, s32[64,128]{1,0:T(8,128)S(1)} %bitcast.15, bf16[4,8192]{1,0:T(4,128)(2,1)S(1)} %copy-done.13, bf16[320,512]{1,0:T(8,128)(2,1)S(1)} %copy-done.12, ...), custom_call_target="tpu_custom_call" | custom-call | flops 8589934592 | bytes 16777216 | tf_op jit(solution)/shard_map/pallas_call | solution.py:717
  13.2 5.0 %collective-permute-done.1.own2_ref = bf16[3,128,256]{2,1,0:T(8,128)(2,1)S(1)} collective-permute-done((bf16[3,128,256]{2,1,0:T(8,128)(2,1)}, bf16[3,128,256]{2,1,0:T(8,128)(2,1)S(1)}, u32[]{:S(2)}, u32[]{:S(2)}) %collective-permute-start.1) | collective-permute-done | bytes 196640 | tf_op jit(solution)/shard_map/ppermute | solution.py:22
  18.2 2.6 %collective-permute-done.2.own3_ref = bf16[3,128,256]{2,1,0:T(8,128)(2,1)S(1)} collective-permute-done((bf16[3,128,256]{2,1,0:T(8,128)(2,1)}, bf16[3,128,256]{2,1,0:T(8,128)(2,1)S(1)}, u32[]{:S(2)}, u32[]{:S(2)}) %collective-permute-start.2) | collective-permute-done | bytes 196640 | tf_op jit(solution)/shard_map/ppermute | solution.py:22
  20.9 0.1 collective-permute-start.3
  21.0 6.3 %collective-permute-start.4 = (bf16[4,128,256]{2,1,0:T(8,128)(2,1)S(1)}, bf16[4,128,256]{2,1,0:T(8,128)(2,1)S(1)}, u32[]{:S(2)}, u32[]{:S(2)}) collective-permute-start(bf16[4,128,256]{2,1,0:T(8,128)(2,1)S(1)} %pad_maximum_fusion.1), channel_id=1, source_target_pairs={{4,8},{8,4},{12,16},{16,12},{20,24},{24,20},{28,32},{32,28},{36,40... | collective-permute-start | bytes 786440 | tf_op jit(solution)/shard_map/ppermute | solution.py:36
  27.4 1.2 %shard_map.282.own_rows_ref = bf16[512,512]{1,0:T(8,128)(2,1)S(1)} custom-call(bf16[3,128,256]{2,1,0:T(8,128)(2,1)S(1)} %copy-done, bf16[3,128,256]{2,1,0:T(8,128)(2,1)S(1)} %collective-permute-done.own1_ref, bf16[3,128,256]{2,1,0:T(8,128)(2,1)S(1)} %collective-permute-done.1.own2_ref, bf16[3,128,256]{2,1,0:T(8,128)(2,1)S(1)} %collective-permute-done.2.own3_ref, ...), custom_call_target="tpu_custom_call" | custom-call | flops 671088640 | bytes 3145728 | tf_op jit(solution)/shard_map/pallas_call | solution.py:741
  28.6 2.8 %collective-permute-done.4.cross_ref = bf16[4,128,256]{2,1,0:T(8,128)(2,1)S(1)} collective-permute-done((bf16[4,128,256]{2,1,0:T(8,128)(2,1)S(1)}, bf16[4,128,256]{2,1,0:T(8,128)(2,1)S(1)}, u32[]{:S(2)}, u32[]{:S(2)}) %collective-permute-start.4) | collective-permute-done | bytes 262176 | tf_op jit(solution)/shard_map/ppermute | solution.py:36
  31.4 9.5 %shard_map.283 = (bf16[1152,512]{1,0:T(8,128)(2,1)S(1)}, bf16[3,64,512]{2,1,0:T(8,128)(2,1)S(1)}, bf16[3,64,512]{2,1,0:T(8,128)(2,1)S(1)}, bf16[3,64,512]{2,1,0:T(8,128)(2,1)S(1)}, bf16[1024,128]{1,0:T(8,128)(2,1)}) custom-call(s32[1]{0:T(128)S(6)} %copy.31.live_ref, bf16[512,512]{1,0:T(8,128)(2,1)S(1)} %shard_map.282.own_rows_ref, ...), custom_call_target="tpu_custom_call" | custom-call | flops 17179869184 | bytes 16777216 | tf_op jit(solution)/shard_map/pallas_call | solution.py:749
  41.0 3.9 %collective-permute-start.5 = (bf16[3,64,512]{2,1,0:T(8,128)(2,1)S(1)}, bf16[3,64,512]{2,1,0:T(8,128)(2,1)S(1)}, u32[]{:S(2)}, u32[]{:S(2)}) collective-permute-start(bf16[3,64,512]{2,1,0:T(8,128)(2,1)S(1)} %get-tuple-element.44), channel_id=1, source_target_pairs={{0,1},{1,0},{2,3},{3,2},{4,5},{5,4},{6,7},{7,6},{8,9},{9,8},{10,11... | collective-permute-start | bytes 589832 | tf_op jit(solution)/shard_map/ppermute | solution.py:22
  44.9 5.3 %collective-permute-start.6 = (bf16[3,64,512]{2,1,0:T(8,128)(2,1)S(1)}, bf16[3,64,512]{2,1,0:T(8,128)(2,1)S(1)}, u32[]{:S(2)}, u32[]{:S(2)}) collective-permute-start(bf16[3,64,512]{2,1,0:T(8,128)(2,1)S(1)} %get-tuple-element.51), channel_id=1, source_target_pairs={{0,2},{1,3},{2,0},{3,1},{4,6},{5,7},{6,4},{7,5},{8,10},{9,11},{10,... | collective-permute-start | bytes 589832 | tf_op jit(solution)/shard_map/ppermute | solution.py:22
  50.2 0.3 collective-permute-done.5.own1_hbm
  50.5 12.3 %all-to-all-start = ((bf16[128,8,128]{2,1,0:T(8,128)(2,1)}), bf16[128,8,128]{2,1,0:T(8,128)(2,1)S(1)}, u32[]{:S(2)}, u32[]{:S(2)}) async-start(bf16[128,8,128]{2,1,0:T(8,128)(2,1)} %bitcast.7), calls=%async_computation | async-start | bytes 524288 | tf_op jit(solution)/shard_map/all_to_all | solution.py:793
  62.9 0.2 collective-permute-start.8
  63.2 5.5 %collective-permute-start.9 = (bf16[4,64,512]{2,1,0:T(8,128)(2,1)S(1)}, bf16[4,64,512]{2,1,0:T(8,128)(2,1)S(1)}, u32[]{:S(2)}, u32[]{:S(2)}) collective-permute-start(bf16[4,64,512]{2,1,0:T(8,128)(2,1)S(1)} %pad_maximum_fusion.3), channel_id=1, source_target_pairs={{4,8},{8,4},{12,16},{16,12},{20,24},{24,20},{28,32},{32,28},{36,40... | collective-permute-start | bytes 786440 | tf_op jit(solution)/shard_map/ppermute | solution.py:36
  68.8 7.3 %shard_map.284 = (bf16[2560,512]{1,0:T(8,128)(2,1)}, f32[2560,128]{1,0:T(8,128)}) custom-call(s32[20,128]{1,0:T(8,128)} %bitcast.21, s32[20,128]{1,0:T(8,128)} %bitcast.22, bf16[1152,512]{1,0:T(8,128)(2,1)} %copy-done.4, bf16[2560,512]{1,0:T(8,128)(2,1)} %lat_hbm.3, bf16[512,512]{1,0:T(8,128)(2,1)} %self_hbm.1), custom_call_target="tpu_custom_call" | custom-call | flops 4000000000 | bytes 16777216 | tf_op jit(solution)/shard_map/pallas_call | solution.py:801
  76.2 0.6 copy-done.20
  76.8 0.1 copy-done.24
  76.9 0.1 copy-done.25
  77.0 12.6 %shard_map.285 = bf16[320,512]{1,0:T(8,128)(2,1)} custom-call(s32[20,128]{1,0:T(8,128)} %bitcast.23, f32[1,512]{1,0:T(1,128)} %bitcast.24, bf16[1024,128]{1,0:T(8,128)(2,1)} %bitcast.19, bf16[1152,512]{1,0:T(8,128)(2,1)} %copy-done.4, bf16[2560,512]{1,0:T(8,128)(2,1)} %get-tuple-element.48.pre_hbm, f32[2560,128]{1,0:T(8,128)} %get-tuple-element.49.place_hbm, ...), custom_call_target="tpu_custom_call" | custom-call | flops 5368709120 | bytes 12582912 | tf_op jit(solution)/shard_map/pallas_call | solution.py:819
  (66 shorter events, 0.4 us)
Async XLA Ops:
  4.6 8.6 %collective-permute-start = (bf16[3,128,256]{2,1,0:T(8,128)(2,1)}, bf16[3,128,256]{2,1,0:T(8,128)(2,1)S(1)}, u32[]{:S(2)}, u32[]{:S(2)}) collective-permute-start(bf16[3,128,256]{2,1,0:T(8,128)(2,1)} %get-tuple-element.30), channel_id=1, source_target_pairs={{0,1},{1,0},{2,3},{3,2},{4,5},{5,4},{6,7},{7,6},{8,9},{9,8},{10,11... | collective-permute-start | bytes 589832 | tf_op jit(solution)/shard_map/ppermute | solution.py:22
  6.2 12.0 %collective-permute-start.1 = (bf16[3,128,256]{2,1,0:T(8,128)(2,1)}, bf16[3,128,256]{2,1,0:T(8,128)(2,1)S(1)}, u32[]{:S(2)}, u32[]{:S(2)}) collective-permute-start(bf16[3,128,256]{2,1,0:T(8,128)(2,1)} %get-tuple-element.31), channel_id=1, source_target_pairs={{0,2},{1,3},{2,0},{3,1},{4,6},{5,7},{6,4},{7,5},{8,10},{9,11},{10,... | collective-permute-start | bytes 589832 | tf_op jit(solution)/shard_map/ppermute | solution.py:22
  9.1 11.7 %collective-permute-start.2 = (bf16[3,128,256]{2,1,0:T(8,128)(2,1)}, bf16[3,128,256]{2,1,0:T(8,128)(2,1)S(1)}, u32[]{:S(2)}, u32[]{:S(2)}) collective-permute-start(bf16[3,128,256]{2,1,0:T(8,128)(2,1)} %get-tuple-element.32), channel_id=1, source_target_pairs={{0,3},{1,2},{2,1},{3,0},{4,7},{5,6},{6,5},{7,4},{8,11},{9,10},{10,... | collective-permute-start | bytes 589832 | tf_op jit(solution)/shard_map/ppermute | solution.py:22
  10.0 17.3 %copy-start.1 = (bf16[512,512]{1,0:T(8,128)(2,1)S(1)}, bf16[512,512]{1,0:T(8,128)(2,1)}, u32[]{:S(2)}) copy-start(bf16[512,512]{1,0:T(8,128)(2,1)} %enc_out_ref.3) | copy-start | bytes 1572868
  10.0 17.3 %copy-start.2 = (bf16[512,512]{1,0:T(8,128)(2,1)S(1)}, bf16[512,512]{1,0:T(8,128)(2,1)}, u32[]{:S(2)}) copy-start(bf16[512,512]{1,0:T(8,128)(2,1)} %send_proj_ref.3) | copy-start | bytes 1572868
  10.1 17.3 %copy-start.3 = (bf16[227,512]{1,0:T(8,128)(2,1)S(1)}, bf16[227,512]{1,0:T(8,128)(2,1)}, u32[]{:S(2)}) copy-start(bf16[227,512]{1,0:T(8,128)(2,1)} %enc_in_ref.3) | copy-start | bytes 697348
  13.1 18.3 %copy-start.7 = (bf16[512,512]{1,0:T(8,128)(2,1)S(1)}, bf16[512,512]{1,0:T(8,128)(2,1)}, u32[]{:S(2)}) copy-start(bf16[512,512]{1,0:T(8,128)(2,1)} %msg_ref.1) | copy-start | bytes 1572868
  13.1 18.3 %copy-start.8 = (bf16[512,512]{1,0:T(8,128)(2,1)S(1)}, bf16[512,512]{1,0:T(8,128)(2,1)}, u32[]{:S(2)}) copy-start(bf16[512,512]{1,0:T(8,128)(2,1)} %node_agg_ref.1) | copy-start | bytes 1572868
  13.1 18.3 %copy-start.9 = (bf16[512,512]{1,0:T(8,128)(2,1)S(1)}, bf16[512,512]{1,0:T(8,128)(2,1)}, u32[]{:S(2)}) copy-start(bf16[512,512]{1,0:T(8,128)(2,1)} %node_out_ref.1) | copy-start | bytes 1572868
  13.1 18.3 %copy-start.10 = (bf16[512,512]{1,0:T(8,128)(2,1)S(1)}, bf16[512,512]{1,0:T(8,128)(2,1)}, u32[]{:S(2)}) copy-start(bf16[512,512]{1,0:T(8,128)(2,1)} %proc_send_ref.1) | copy-start | bytes 1572868
  13.1 18.3 %copy-start.11 = (bf16[512,512]{1,0:T(8,128)(2,1)S(1)}, bf16[512,512]{1,0:T(8,128)(2,1)}, u32[]{:S(2)}) copy-start(bf16[512,512]{1,0:T(8,128)(2,1)} %proc_recv_ref.1) | copy-start | bytes 1572868
  13.1 18.3 %copy-start.16 = (s32[3,4,64]{2,1,0:T(4,128)S(1)}, s32[3,4,64]{2,1,0:T(4,128)}, u32[]{:S(2)}) copy-start(s32[3,4,64]{2,1,0:T(4,128)} %near_ref.1) | copy-start | bytes 9220
  13.1 18.3 %copy-start.18 = (f32[512]{0:T(512)S(1)}, f32[512]{0:T(512)}, u32[]{:S(2)}) copy-start(f32[512]{0:T(512)} %param.51) | copy-start | bytes 6148
  13.1 18.3 %copy-start.19 = (s32[128,2]{0,1:T(2,128)S(1)}, s32[128,2]{0,1:T(2,128)}, u32[]{:S(2)}) copy-start(s32[128,2]{0,1:T(2,128)} %param.38) | copy-start | bytes 3076
  20.9 7.7 %collective-permute-start.3 = (bf16[4,128,256]{2,1,0:T(8,128)(2,1)S(1)}, bf16[4,128,256]{2,1,0:T(8,128)(2,1)S(1)}, u32[]{:S(2)}, u32[]{:S(2)}) collective-permute-start(bf16[4,128,256]{2,1,0:T(8,128)(2,1)S(1)} %pad_maximum_fusion), channel_id=1, source_target_pairs={{0,4},{4,0},{8,12},{12,8},{16,20},{20,16},{24,28},{28,24},{32,36},... | collective-permute-start | bytes 786440 | tf_op jit(solution)/shard_map/ppermute | solution.py:36
  21.0 10.4 %collective-permute-start.4 = (bf16[4,128,256]{2,1,0:T(8,128)(2,1)S(1)}, bf16[4,128,256]{2,1,0:T(8,128)(2,1)S(1)}, u32[]{:S(2)}, u32[]{:S(2)}) collective-permute-start(bf16[4,128,256]{2,1,0:T(8,128)(2,1)S(1)} %pad_maximum_fusion.1), channel_id=1, source_target_pairs={{4,8},{8,4},{12,16},{16,12},{20,24},{24,20},{28,32},{32,28},{36,40... | collective-permute-start | bytes 786440 | tf_op jit(solution)/shard_map/ppermute | solution.py:36
  41.0 27.8 %copy-start.4 = (bf16[1152,512]{1,0:T(8,128)(2,1)}, bf16[1152,512]{1,0:T(8,128)(2,1)S(1)}, u32[]{:S(2)}) copy-start(bf16[1152,512]{1,0:T(8,128)(2,1)S(1)} %get-tuple-element.47.trio_hbm) | copy-start | bytes 3538948
  41.0 9.6 %collective-permute-start.5 = (bf16[3,64,512]{2,1,0:T(8,128)(2,1)S(1)}, bf16[3,64,512]{2,1,0:T(8,128)(2,1)S(1)}, u32[]{:S(2)}, u32[]{:S(2)}) collective-permute-start(bf16[3,64,512]{2,1,0:T(8,128)(2,1)S(1)} %get-tuple-element.44), channel_id=1, source_target_pairs={{0,1},{1,0},{2,3},{3,2},{4,5},{5,4},{6,7},{7,6},{8,9},{9,8},{10,11... | collective-permute-start | bytes 589832 | tf_op jit(solution)/shard_map/ppermute | solution.py:22
  44.9 17.9 %collective-permute-start.6 = (bf16[3,64,512]{2,1,0:T(8,128)(2,1)S(1)}, bf16[3,64,512]{2,1,0:T(8,128)(2,1)S(1)}, u32[]{:S(2)}, u32[]{:S(2)}) collective-permute-start(bf16[3,64,512]{2,1,0:T(8,128)(2,1)S(1)} %get-tuple-element.51), channel_id=1, source_target_pairs={{0,2},{1,3},{2,0},{3,1},{4,6},{5,7},{6,4},{7,5},{8,10},{9,11},{10,... | collective-permute-start | bytes 589832 | tf_op jit(solution)/shard_map/ppermute | solution.py:22
  50.2 12.7 %collective-permute-start.7 = (bf16[3,64,512]{2,1,0:T(8,128)(2,1)S(1)}, bf16[3,64,512]{2,1,0:T(8,128)(2,1)S(1)}, u32[]{:S(2)}, u32[]{:S(2)}) collective-permute-start(bf16[3,64,512]{2,1,0:T(8,128)(2,1)S(1)} %get-tuple-element.52), channel_id=1, source_target_pairs={{0,3},{1,2},{2,1},{3,0},{4,7},{5,6},{6,5},{7,4},{8,11},{9,10},{10,... | collective-permute-start | bytes 589832 | tf_op jit(solution)/shard_map/ppermute | solution.py:22
  50.5 25.5 %copy-start.21 = (bf16[3,64,512]{2,1,0:T(8,128)(2,1)}, bf16[3,64,512]{2,1,0:T(8,128)(2,1)S(1)}, u32[]{:S(2)}) copy-start(bf16[3,64,512]{2,1,0:T(8,128)(2,1)S(1)} %collective-permute-done.5.own1_hbm) | copy-start | bytes 589828
  50.5 25.6 %all-to-all-start = ((bf16[128,8,128]{2,1,0:T(8,128)(2,1)}), bf16[128,8,128]{2,1,0:T(8,128)(2,1)S(1)}, u32[]{:S(2)}, u32[]{:S(2)}) async-start(bf16[128,8,128]{2,1,0:T(8,128)(2,1)} %bitcast.7), calls=%async_computation | async-start | bytes 524288 | tf_op jit(solution)/shard_map/all_to_all | solution.py:793
  62.9 13.2 %collective-permute-start.8 = (bf16[4,64,512]{2,1,0:T(8,128)(2,1)S(1)}, bf16[4,64,512]{2,1,0:T(8,128)(2,1)S(1)}, u32[]{:S(2)}, u32[]{:S(2)}) collective-permute-start(bf16[4,64,512]{2,1,0:T(8,128)(2,1)S(1)} %pad_maximum_fusion.2), channel_id=1, source_target_pairs={{0,4},{4,0},{8,12},{12,8},{16,20},{20,16},{24,28},{28,24},{32,36},... | collective-permute-start | bytes 786440 | tf_op jit(solution)/shard_map/ppermute | solution.py:36
  63.2 12.9 %collective-permute-start.9 = (bf16[4,64,512]{2,1,0:T(8,128)(2,1)S(1)}, bf16[4,64,512]{2,1,0:T(8,128)(2,1)S(1)}, u32[]{:S(2)}, u32[]{:S(2)}) collective-permute-start(bf16[4,64,512]{2,1,0:T(8,128)(2,1)S(1)} %pad_maximum_fusion.3), channel_id=1, source_target_pairs={{4,8},{8,4},{12,16},{16,12},{20,24},{24,20},{28,32},{32,28},{36,40... | collective-permute-start | bytes 786440 | tf_op jit(solution)/shard_map/ppermute | solution.py:36
  (13 other events, 109.3 us)
